TPU v7x, 32 devices: a whole 2x2x4 slice. The times are simulated.
32 devices in a mesh: runs: 2 (over x), sec: 16 (over z, y, core).
Axes of the slice: x: 2, y: 2, z: 4, core: 2. Of those that a mesh axis runs over, the one named last changes fastest.
Arguments:
- edge_rows: bfloat16 [4096, 1024], P(('runs', 'sec')), parts along dimension 0, may hold values from -46 to 46
- corner: bfloat16 [32768, 1024], P(('runs', 'sec')), parts along dimension 0, may hold values from -1 to 2.2
- joining: int32 [32, 16], P('runs'), parts along dimension 0, may hold values from 0 to 15, as said below
- charge_left: int32 [4096], P(('runs', 'sec')), parts along dimension 0, may hold values from 0 to 15
- charge_right: int32 [4096], P(('runs', 'sec')), parts along dimension 0, may hold values from 0 to 15
Outputs:
- isometry: float32 [4096, 1024], P(('runs', 'sec')), parts along dimension 0
There are 2 independent parts, one for each index of `runs`. A program takes and returns all parts, laid end to end along the dimension named above; each array names one. Nothing has to cross between parts.
Inputs may be any that keep to these rules, and one draw needn't show every extreme that they name: joining[charge_left[e], charge_right[e]] names the block that row e needs; each row of joining names every block once; among the 128 rows of one device at most 16 need the same block, and one block, drawn per copy, receives exactly 16 rows from every device.
All inputs are finite; a program needn't handle non-finite values.
Results may differ from a plain program's by a relative error of at most 0.0003.
Values may be sent and summed in bfloat16 or wider, within the bound.
No kernel may reach another device: no remote copies, remote signals or barrier semaphores. Data moves between devices by JAX's collectives and lax.ppermute only.
A program may use at most 128 MiB of HBM per device.

v0:
```python
import math

import jax
import jax.numpy as jnp
from jax import lax
from jax.sharding import PartitionSpec as P


def gram_of(images):
    return lax.dot_general(
        images, images, (((0,), (0,)), ((), ())), precision=lax.Precision.HIGHEST
    )


def reduce_gram(partial_gram):
    return lax.psum(partial_gram, "sec")


def solve_rows(gram_total, images, factor):
    lower = jnp.linalg.cholesky(gram_total)
    solved = lax.linalg.triangular_solve(
        lower, images, left_side=False, lower=True, transpose_a=True
    )
    return solved * factor


def per_device(edge_rows, corner, joining, charge_left, charge_right):
    row_count, feature_len = edge_rows.shape
    owners = lax.axis_size("sec")
    capacity = 2 * row_count // owners
    factor = math.sqrt(row_count * owners)
    target = joining[charge_left, charge_right]
    labels = jnp.arange(owners, dtype=jnp.int32)
    onehot = (target[:, None] == labels[None, :]).astype(jnp.int32)
    before = jnp.cumsum(onehot, axis=0) - onehot
    order_in = jnp.sum(before * onehot, axis=1)
    slot_index = target * capacity + order_in
    packed = (
        jnp.zeros((owners * capacity, feature_len), edge_rows.dtype).at[slot_index].set(edge_rows)
    )
    arrived = lax.all_to_all(
        packed.reshape(owners, capacity, feature_len),
        "sec",
        split_axis=0,
        concat_axis=0,
        tiled=True,
    )
    product = jnp.dot(
        arrived.reshape(owners * capacity, feature_len), corner, preferred_element_type=jnp.float32
    )
    returned = lax.all_to_all(
        product.reshape(owners, capacity, feature_len),
        "sec",
        split_axis=0,
        concat_axis=0,
        tiled=True,
    )
    home_rows = returned.reshape(owners * capacity, feature_len)[slot_index]
    gram_total = reduce_gram(gram_of(home_rows))
    result = solve_rows(gram_total, home_rows, factor)
    return result


def solution(mesh):
    placed = (
        P(("runs", "sec"), None),
        P(("runs", "sec"), None),
        P("runs", None),
        P(("runs", "sec")),
        P(("runs", "sec")),
    )
    return jax.shard_map(
        per_device, mesh=mesh, in_specs=placed, out_specs=P(("runs", "sec"), None), check_vma=False
    )
```

profile of v0, /device:TPU:0, one launch (start us, length us, event | category | flops | bytes accessed | tf_op | source)
XLA Modules:
  0.0 532.5 jit_solution(10985662273501543571)
XLA Ops:
  7.4 1.8 gather_fusion
  9.6 1.7 scatter_custom_fusion
  11.4 21.7 %all_to_all.10 = bf16[16,16,1024]{2,1,0:T(8,128)(2,1)S(1)} all-to-all(bf16[16,16,1024]{2,1,0:T(8,128)(2,1)S(1)} %bitcast.114), channel_id=1, replica_groups=mesh['runs'=2,'sec'=16] {'sec'}, dimensions={0} | all-to-all | bytes 1048576 | tf_op jit(solution)/shard_map/all_to_all | solution.py:41
  33.0 1.7 fusion.1
  34.7 4.1 all-to-all-start.1
  38.9 22.9 %all-to-all-done.1 = f32[16,16,1024]{2,1,0:T(8,128)S(1)} async-done(((f32[16,16,1024]{2,1,0:T(8,128)}), f32[16,16,1024]{2,1,0:T(8,128)S(1)}, u32[]{:S(2)}, u32[]{:S(2)}) %all-to-all-start.1) | async-done | bytes 1048608 | tf_op jit(solution)/shard_map/all_to_all | solution.py:51
  63.3 6.6 %fusion.73 = f32[1024,1024]{0,1:T(8,128)} fusion(f32[128,1024]{1,0:T(8,128)} %gather_fusion.1), kind=kOutput, calls=%fused_computation.176 | convolution fusion | flops 1610612736 | bytes 4718592 | tf_op jit(solution)/shard_map/dot_general | solution.py:10
  70.0 113.8 %all-reduce.3.cloned.1.call-done = f32[1024,1024]{0,1:T(8,128)} async-done(((f32[1024,1024]{0,1:T(8,128)}), f32[1024,1024]{0,1:T(8,128)}) %all-reduce.3.cloned.1.call-update) | async-done | bytes 4194320 | tf_op jit(solution)/shard_map/psum | solution.py:16
  183.8 5.8 %copy.10 = f32[1024,1024]{1,0:T(8,128)} copy(f32[1024,1024]{0,1:T(8,128)} %all-reduce.3.cloned.1.call-done) | data formatting | bytes 8388608 | tf_op jit(solution)/shard_map/psum | solution.py:16
  189.6 4.4 fusion
  194.1 1.9 copy-done.1
  196.0 11.7 %cholesky.223 = f32[128,128]{1,0:T(8,128)S(1)} custom-call(f32[128,128]{1,0:T(8,128)S(1)} %cholesky.580), custom_call_target="Cholesky" | custom-call | tf_op jit(solution)/shard_map/jit(cholesky)/cholesky | solution.py:20
  207.8 9.8 %custom-call.62 = f32[1,128,128]{1,2,0:T(8,128)S(1)} custom-call(f32[1,128,128]{2,1,0:T(8,128)S(1)} %get-tuple-element.69), custom_call_target="InvertDiagBlocksLowerTriangular" | custom-call | tf_op jit(solution)/shard_map/jit(cholesky)/cholesky | solution.py:20
  217.6 2.5 cholesky.255
  220.1 2.4 constant_dynamic-update-slice_fusion.31
  224.0 11.9 %cholesky.244 = f32[128,128]{1,0:T(8,128)S(1)} custom-call(f32[128,128]{1,0:T(8,128)S(1)} %cholesky.584), custom_call_target="Cholesky" | custom-call | tf_op jit(solution)/shard_map/jit(cholesky)/cholesky | solution.py:20
  236.5 9.8 %custom-call.63 = f32[1,128,128]{1,2,0:T(8,128)S(1)} custom-call(f32[1,128,128]{2,1,0:T(8,128)S(1)} %get-tuple-element.66), custom_call_target="InvertDiagBlocksLowerTriangular" | custom-call | tf_op jit(solution)/shard_map/jit(cholesky)/cholesky | solution.py:20
  247.6 2.1 convolution_subtract_fusion.1
  249.7 11.7 %cholesky.468 = f32[128,128]{1,0:T(8,128)S(1)} custom-call(f32[128,128]{1,0:T(8,128)S(1)} %cholesky.589), custom_call_target="Cholesky" | custom-call | tf_op jit(solution)/shard_map/jit(cholesky)/cholesky | solution.py:20
  262.7 9.8 %custom-call.64 = f32[1,128,128]{1,2,0:T(8,128)S(1)} custom-call(f32[1,128,128]{2,1,0:T(8,128)S(1)} %get-tuple-element.63), custom_call_target="InvertDiagBlocksLowerTriangular" | custom-call | tf_op jit(solution)/shard_map/jit(cholesky)/cholesky | solution.py:20
  273.7 2.3 convolution_subtract_fusion.2
  276.1 11.9 %cholesky.487 = f32[128,128]{1,0:T(8,128)S(1)} custom-call(f32[128,128]{1,0:T(8,128)S(1)} %cholesky.594), custom_call_target="Cholesky" | custom-call | tf_op jit(solution)/shard_map/jit(cholesky)/cholesky | solution.py:20
  289.2 9.8 %custom-call.65 = f32[1,128,128]{1,2,0:T(8,128)S(1)} custom-call(f32[1,128,128]{2,1,0:T(8,128)S(1)} %get-tuple-element.60), custom_call_target="InvertDiagBlocksLowerTriangular" | custom-call | tf_op jit(solution)/shard_map/jit(cholesky)/cholesky | solution.py:20
  300.2 2.3 convolution_subtract_fusion.3
  302.5 11.7 %cholesky.506 = f32[128,128]{1,0:T(8,128)S(1)} custom-call(f32[128,128]{1,0:T(8,128)S(1)} %cholesky.599), custom_call_target="Cholesky" | custom-call | tf_op jit(solution)/shard_map/jit(cholesky)/cholesky | solution.py:20
  315.5 10.2 %custom-call.66 = f32[1,128,128]{1,2,0:T(8,128)S(1)} custom-call(f32[1,128,128]{2,1,0:T(8,128)S(1)} %get-tuple-element.57), custom_call_target="InvertDiagBlocksLowerTriangular" | custom-call | tf_op jit(solution)/shard_map/jit(cholesky)/cholesky | solution.py:20
  326.7 2.3 convolution_subtract_fusion.4
  329.0 11.7 %cholesky.526 = f32[128,128]{1,0:T(8,128)S(1)} custom-call(f32[128,128]{1,0:T(8,128)S(1)} %cholesky.604), custom_call_target="Cholesky" | custom-call | tf_op jit(solution)/shard_map/jit(cholesky)/cholesky | solution.py:20
  342.0 9.8 %custom-call.67 = f32[1,128,128]{1,2,0:T(8,128)S(1)} custom-call(f32[1,128,128]{2,1,0:T(8,128)S(1)} %get-tuple-element.54), custom_call_target="InvertDiagBlocksLowerTriangular" | custom-call | tf_op jit(solution)/shard_map/jit(cholesky)/cholesky | solution.py:20
  352.8 2.0 convolution_subtract_fusion.5
  354.8 11.9 %cholesky.546 = f32[128,128]{1,0:T(8,128)S(1)} custom-call(f32[128,128]{1,0:T(8,128)S(1)} %cholesky.609), custom_call_target="Cholesky" | custom-call | tf_op jit(solution)/shard_map/jit(cholesky)/cholesky | solution.py:20
  367.9 9.8 %custom-call.68 = f32[1,128,128]{1,2,0:T(8,128)S(1)} custom-call(f32[1,128,128]{2,1,0:T(8,128)S(1)} %get-tuple-element.51), custom_call_target="InvertDiagBlocksLowerTriangular" | custom-call | tf_op jit(solution)/shard_map/jit(cholesky)/cholesky | solution.py:20
  378.6 1.8 convolution_subtract_fusion.11
  380.4 11.7 %cholesky.564 = f32[128,128]{1,0:T(8,128)S(1)} custom-call(f32[128,128]{1,0:T(8,128)S(1)} %convolution_subtract_fusion.11), custom_call_target="Cholesky" | custom-call | tf_op jit(solution)/shard_map/jit(cholesky)/cholesky | solution.py:20
  399.0 4.8 select_select_fusion
  403.9 27.6 %while.1 = (s32[]{:T(128)}, f32[1024,1024]{1,0:T(8,128)}, s32[8,2]{0,1:T(2,128)S(1)}, f32[8,128,128]{2,1,0:T(8,128)}, s32[]{:T(128)}) while((s32[]{:T(128)}, f32[1024,1024]{1,0:T(8,128)}, s32[8,2]{0,1:T(2,128)S(1)}, f32[8,128,128]{2,1,0:T(8,128)}, s32[]{:T(128)}) %tuple.57), condition=%wide.while_cond, body=%wide.while_body.sunk | while | flops 2 | bytes 132705 | solution.py:21
  404.5 2.9 bitcast_dynamic-update-slice_fusion.2
  408.0 2.8 bitcast_dynamic-update-slice_fusion.2
  411.4 2.8 bitcast_dynamic-update-slice_fusion.2
  414.9 2.8 bitcast_dynamic-update-slice_fusion.2
  418.4 2.8 bitcast_dynamic-update-slice_fusion.2
  421.8 2.8 bitcast_dynamic-update-slice_fusion.2
  425.3 2.8 bitcast_dynamic-update-slice_fusion.2
  428.7 2.8 bitcast_dynamic-update-slice_fusion.2
  431.5 79.6 %custom-call.69 = f32[8,128,128]{1,2,0:T(8,128)S(1)} custom-call(f32[8,128,128]{2,1,0:T(8,128)} %get-tuple-element.12), custom_call_target="InvertDiagBlocksLowerTriangular" | custom-call | tf_op jit(solution)/shard_map/triangular_solve | solution.py:21
  518.0 1.7 convolution_subtract_fusion.8
  520.0 1.8 convolution_subtract_fusion.7
  522.1 1.9 convolution_subtract_fusion.6
  (76 shorter events, 33.7 us)
Async XLA Ops:
  6.5 26.5 %copy-start = (bf16[1024,1024]{1,0:T(8,128)(2,1)S(1)}, bf16[1024,1024]{1,0:T(8,128)(2,1)}, u32[]{:S(2)}) copy-start(bf16[1024,1024]{1,0:T(8,128)(2,1)} %param.6) | copy-start | bytes 6291460
  34.7 27.0 %all-to-all-start.1 = ((f32[16,16,1024]{2,1,0:T(8,128)}), f32[16,16,1024]{2,1,0:T(8,128)S(1)}, u32[]{:S(2)}, u32[]{:S(2)}) async-start(f32[16,16,1024]{2,1,0:T(8,128)} %fusion.1), calls=%async_computation.1 | async-start | bytes 2097152 | tf_op jit(solution)/shard_map/all_to_all | solution.py:51
  38.8 145.0 %all-reduce.3.cloned.1.call-start = ((), (), s32[]{:S(2)}) async-start(), calls=%async_computation.2 | async-start | bytes 8388608 | tf_op jit(solution)/shard_map/psum | solution.py:16
  194.1 1.9 copy-start.1
  399.0 112.1 %copy-start.2 = (f32[128,1024]{1,0:T(8,128)S(1)}, f32[128,1024]{1,0:T(8,128)}, u32[]{:S(2)}) copy-start(f32[128,1024]{1,0:T(8,128)} %gather_fusion.1) | copy-start | bytes 1572868
Sparse Core Ops, SparseCore 0:
  70.1 113.6 all-reduce.2
where the time goes:
time: 539 us; the launch traced here: 533 us
  other arithmetic  263 us (49%)
  waiting for transfers between devices  137 us (25%)
  matrix products  44.5 us (8%)
  local copies, waits for them, and re-layouts  44.1 us (8%)
  blocking collectives  21.7 us (4%)
  between operations  18.9 us (4%)
    another operation x30, other arithmetic, solve_rows(): lower = jnp.linalg.cholesky(gram_total)  172 us
    psum x1, waiting for transfers between devices, reduce_gram(): return lax.psum(partial_gram, 'sec')  114 us
    another operation x3, other arithmetic, solve_rows(): lax.linalg.triangular_solve(lower, images, left_side=False, lower=True, t...  84.5 us
    another operation x24, local copies, waits for them, and re-layouts  27.6 us
    another operation x14, matrix products, solve_rows(): lower = jnp.linalg.cholesky(gram_total)  23.1 us
    all_to_all x1, waiting for transfers between devices, per_device(): lax.all_to_all(product.reshape(owners, capacity, feature_len), 'sec', spl...  22.9 us
    all_to_all x1, blocking collectives, per_device(): lax.all_to_all(packed.reshape(owners, capacity, feature_len), 'sec', spli...  21.7 us
    another operation x15, matrix products, solve_rows(): lax.linalg.triangular_solve(lower, images, left_side=False, lower=True, t...  13.1 us
  transfers between devices with their start and end apart: 2, of which 2 were waited for; matrix products, arithmetic and copies ran while one was open for 0% of the time, Pallas kernels for 0%

commit v1 on v0

v1 whole, which is shorter than its diff:
```python
import functools
import math

import jax
import jax.numpy as jnp
from jax import lax
from jax.experimental import pallas as pl
from jax.experimental.pallas import tpu as pltpu
from jax.sharding import PartitionSpec as P

SIDE = 128
HIGHEST = lax.Precision.HIGHEST


def column_offsets(count):
    offsets = [0]
    for j in range(count):
        offsets.append(offsets[-1] + (count - j) * SIDE)
    return offsets


def dot_nt(a, b):
    return lax.dot_general(
        a, b, (((1,), (1,)), ((), ())), precision=HIGHEST, preferred_element_type=jnp.float32
    )


def dot_tn(a, b):
    return lax.dot_general(
        a, b, (((0,), (0,)), ((), ())), precision=HIGHEST, preferred_element_type=jnp.float32
    )


def images_kernel(arrived_ref, corner_ref, images_ref, gram_ref):
    width = corner_ref.shape[1]
    count = width // SIDE
    offsets = column_offsets(count)
    images = jnp.dot(arrived_ref[...], corner_ref[...], preferred_element_type=jnp.float32)
    images_ref[...] = images
    for j in range(0, count, 2):
        part = dot_tn(images[:, j * SIDE :], images[:, j * SIDE : (j + 2) * SIDE])
        gram_ref[offsets[j] : offsets[j + 1], :] = part[:, :SIDE]
        gram_ref[offsets[j + 1] : offsets[j + 2], :] = part[SIDE:, SIDE:]


def invert_factor(block):
    size = block.shape[0]
    lane = lax.broadcasted_iota(jnp.int32, (8, size), 1)
    sub = lax.broadcasted_iota(jnp.int32, (8, size), 0)

    def spread(x):
        return jnp.broadcast_to(x, (8, size))

    groups = size // 8
    for m in range(groups):
        g = 8 * m
        inside = (lane >= g) & (lane < g + 8)
        pivots = block[g : g + 8, :]
        columns = [spread(pivots[:, g + j : g + j + 1]) for j in range(8)]
        pivots = jnp.where(inside, (lane - g == sub).astype(jnp.float32), pivots)
        rows, below = {}, {}
        for r in range(m + 1, groups):
            x = block[8 * r : 8 * r + 8, :]
            below[r] = [spread(x[:, g + j : g + j + 1]) for j in range(8)]
            rows[r] = jnp.where(inside, 0.0, x)
        diagonal = columns[0]
        for j in range(8):
            inverse = 1.0 / spread(columns[j][j : j + 1, :])
            pivot_row = spread(pivots[j : j + 1, :])
            if j:
                diagonal = jnp.where(sub == j, columns[j], diagonal)
            weight = jnp.where(sub > j, columns[j], 0.0) * inverse
            pivots = pivots - weight * pivot_row
            heads = {k: spread(columns[k][j : j + 1, :]) for k in range(j + 1, 8)}
            for k in range(j + 1, 8):
                columns[k] = columns[k] - weight * heads[k]
            for r in range(m + 1, groups):
                weight_r = below[r][j] * inverse
                rows[r] = rows[r] - weight_r * pivot_row
                for k in range(j + 1, 8):
                    below[r][k] = below[r][k] - weight_r * heads[k]
        block[g : g + 8, :] = pivots * lax.rsqrt(diagonal)
        for r in range(m + 1, groups):
            block[8 * r : 8 * r + 8, :] = rows[r]


def cholesky_kernel(count, gram_ref, lower_ref, block):
    offsets = column_offsets(count)
    row = lax.broadcasted_iota(jnp.int32, (SIDE, SIDE), 0)
    col = lax.broadcasted_iota(jnp.int32, (SIDE, SIDE), 1)
    lower_ref[...] = gram_ref[...]

    def update(k):
        if k == count - 1:
            return
        top, bottom = offsets[k] + SIDE, offsets[k + 1]
        panel = dot_nt(lower_ref[top:bottom, :], lower_ref[offsets[k] : top, :])
        lower_ref[top:bottom, :] = panel
        for j in range(k + 1, count):
            first = (j - k - 1) * SIDE
            lower_ref[offsets[j] : offsets[j + 1], :] -= dot_nt(
                panel[first:], panel[first : first + SIDE]
            )

    def step(k, carry):
        start = pl.multiple_of((k * count - (k * (k - 1)) // 2) * SIDE, SIDE)
        block[...] = lower_ref[pl.ds(start, SIDE), :]
        invert_factor(block)
        lower_ref[pl.ds(start, SIDE), :] = jnp.where(col <= row, block[...], 0.0)
        for kk in range(count):
            pl.when(k == kk)(functools.partial(update, kk))
        return carry

    lax.fori_loop(0, count, step, 0)


def solve_kernel(count, factor, home_ref, lower_ref, out_ref, rest):
    offsets = column_offsets(count)
    rest[...] = home_ref[...]
    for k in range(count):
        here = slice(k * SIDE, (k + 1) * SIDE)
        top = offsets[k] + SIDE
        solved = dot_nt(rest[:, here], lower_ref[offsets[k] : top, :])
        out_ref[:, here] = solved * factor
        if k < count - 1:
            rest[:, (k + 1) * SIDE :] -= dot_nt(solved, lower_ref[top : offsets[k + 1], :])


def kernel_call(kernel, out_shape, scratch=()):
    return pl.pallas_call(
        kernel,
        out_shape=out_shape,
        scratch_shapes=list(scratch),
        compiler_params=pltpu.CompilerParams(vmem_limit_bytes=40 << 20),
    )


def swap(x, bit):
    return lax.ppermute(x, "sec", [(i, i ^ bit) for i in range(lax.axis_size("sec"))])


def halve(x, bit):
    upper = (lax.axis_index("sec") // bit) % 2
    half = x.shape[0] // 2
    sent = lax.dynamic_slice_in_dim(x, (1 - upper) * half, half, 0)
    kept = lax.dynamic_slice_in_dim(x, upper * half, half, 0)
    return kept + swap(sent, bit)


def double(x, bit):
    upper = (lax.axis_index("sec") // bit) % 2 == 1
    other = swap(x, bit)
    return jnp.where(
        upper, jnp.concatenate([other, x], axis=0), jnp.concatenate([x, other], axis=0)
    )


def reduce_gram(packed):
    bits = [1 << b for b in range(1, lax.axis_size("sec").bit_length() - 1)]
    cut = len(bits) // 2
    orders = [bits, bits[cut:] + bits[:cut]]
    mine = halve(packed, 1)
    streams = []
    for order, part in zip(orders, jnp.split(mine, 2, axis=0)):
        for bit in order:
            part = halve(part, bit)
        streams.append(part)
    whole = []
    for order, part in zip(orders, streams):
        for bit in reversed(order):
            part = double(part, bit)
        whole.append(part)
    return double(jnp.concatenate(whole, axis=0), 1)


def per_device(edge_rows, corner, joining, charge_left, charge_right):
    row_count, feature_len = edge_rows.shape
    owners = lax.axis_size("sec")
    capacity = 2 * row_count // owners
    slots = owners * capacity
    factor = math.sqrt(row_count * owners)
    count = feature_len // SIDE
    packed_rows = column_offsets(count)[-1]
    f32 = jnp.float32
    target = joining[charge_left, charge_right]
    labels = jnp.arange(owners, dtype=jnp.int32)
    onehot = (target[:, None] == labels[None, :]).astype(jnp.int32)
    before = jnp.cumsum(onehot, axis=0) - onehot
    order_in = jnp.sum(before * onehot, axis=1)
    slot_index = target * capacity + order_in
    packed = jnp.zeros((slots, feature_len), edge_rows.dtype).at[slot_index].set(edge_rows)
    arrived = lax.all_to_all(
        packed.reshape(owners, capacity, feature_len), "sec", split_axis=0, concat_axis=0, tiled=True
    )
    product, gram = kernel_call(
        images_kernel,
        (
            jax.ShapeDtypeStruct((slots, feature_len), f32),
            jax.ShapeDtypeStruct((packed_rows, SIDE), f32),
        ),
    )(arrived.reshape(slots, feature_len), corner)
    returned = lax.all_to_all(
        product.reshape(owners, capacity, feature_len), "sec", split_axis=0, concat_axis=0, tiled=True
    )
    total = reduce_gram(gram)
    lower = kernel_call(
        functools.partial(cholesky_kernel, count),
        jax.ShapeDtypeStruct((packed_rows, SIDE), f32),
        [pltpu.VMEM((SIDE, SIDE), f32)],
    )(total)
    home_rows = returned.reshape(slots, feature_len)[slot_index]
    return kernel_call(
        functools.partial(solve_kernel, count, factor),
        jax.ShapeDtypeStruct((row_count, feature_len), f32),
        [pltpu.VMEM((row_count, feature_len), f32)],
    )(home_rows, lower)


def solution(mesh):
    placed = (
        P(("runs", "sec"), None),
        P(("runs", "sec"), None),
        P("runs", None),
        P(("runs", "sec")),
        P(("runs", "sec")),
    )
    return jax.shard_map(
        per_device, mesh=mesh, in_specs=placed, out_specs=P(("runs", "sec"), None), check_vma=False
    )
```

time: 539 us -> 157 us (0.29)
  other arithmetic: 263 us -> 5.93 us
  waiting for transfers between devices: 137 us -> 69 us
  Pallas kernels: 0 us -> 50.3 us
  matrix products: 44.5 us -> 0 us
  local copies, waits for them, and re-layouts: 44.1 us -> 6.32 us
  blocking collectives: 21.7 us -> 0 us
  starting transfers between devices: 4.14 us -> 23.3 us
  between operations: 18.9 us -> 0.27 us
    another operation x33 -> x0, other arithmetic: 257 us -> none  [the longest x30 172 us: solve_rows(): lower = jnp.linalg.cholesky(gram_total)]
    psum x1 -> x0, waiting for transfers between devices: 114 us -> none  [reduce_gram(): return lax.psum(partial_gram, 'sec')]
    pallas_call x0 -> x3, Pallas kernels: none -> 50.3 us  [the longest x1 41.9 us: per_device(): kernel_call(functools.partial(cholesky_kernel, count), jax.ShapeDtypeStru...]
    another operation x29 -> x0, matrix products: 36.2 us -> none  [the longest x14 23.1 us: solve_rows(): lower = jnp.linalg.cholesky(gram_total)]
    ppermute x0 -> x14, waiting for transfers between devices: none -> 33.4 us  [swap(): lax.ppermute(x, 'sec', [(i, i ^ bit) for i in range(lax.axis_size('sec'))])]
    another operation x33 -> x0, local copies, waits for them, and re-layouts: 30.2 us -> none
    all_to_all x1 -> x0, blocking collectives: 21.7 us -> none  [per_device(): lax.all_to_all(packed.reshape(owners, capacity, feature_len), 'sec', spli...]
    all_to_all x0 -> x1, waiting for transfers between devices: none -> 14.4 us  [per_device(): lax.all_to_all(packed.reshape(owners, capacity, feature_len), 'sec', spli...]
  transfers between devices with their start and end apart: 2 -> 16, of which waited for: 2 -> 12; matrix products, arithmetic and copies ran while one was open for 0% -> 1% of each run, Pallas kernels for 0% -> 0%
where the time goes in v1:
time: 157 us; the launch traced here: 155 us
  waiting for transfers between devices  69 us (44%)
  Pallas kernels  50.3 us (32%)
  starting transfers between devices  23.3 us (15%)
  local copies, waits for them, and re-layouts  6.32 us (4%)
  other arithmetic  5.93 us (4%)
    pallas_call x1, Pallas kernels, per_device(): kernel_call(functools.partial(cholesky_kernel, count), jax.ShapeDtypeStru...  41.9 us
    ppermute x14, waiting for transfers between devices, swap(): lax.ppermute(x, 'sec', [(i, i ^ bit) for i in range(lax.axis_size('sec'))])  33.4 us
    all_to_all x1, waiting for transfers between devices, per_device(): lax.all_to_all(product.reshape(owners, capacity, feature_len), 'sec', spl...  21.2 us
    all_to_all x1, waiting for transfers between devices, per_device(): lax.all_to_all(packed.reshape(owners, capacity, feature_len), 'sec', spli...  14.4 us
    ppermute x14, starting transfers between devices, swap(): lax.ppermute(x, 'sec', [(i, i ^ bit) for i in range(lax.axis_size('sec'))])  11.2 us
    all_to_all x1, starting transfers between devices, per_device(): lax.all_to_all(packed.reshape(owners, capacity, feature_len), 'sec', spli...  7.39 us
    pallas_call x1, Pallas kernels, per_device(): kernel_call(functools.partial(solve_kernel, count, factor), jax.ShapeDtyp...  5.5 us
    all_to_all x1, starting transfers between devices, per_device(): lax.all_to_all(product.reshape(owners, capacity, feature_len), 'sec', spl...  4.77 us
  transfers between devices with their start and end apart: 16, of which 12 were waited for; matrix products, arithmetic and copies ran while one was open for 1% of the time, Pallas kernels for 0%

profile of v1, /device:TPU:0, one launch (start us, length us, event | category | flops | bytes accessed | tf_op | source)
XLA Modules:
  0.0 155.2 jit_solution(5623467993573300805)
XLA Ops:
  0.0 0.7 fusion.5
  0.7 0.0 copy-done
  0.7 1.3 gather_fusion
  2.0 0.1 fusion.2
  2.1 0.2 reduce_window_sum.11
  2.2 0.2 select_reduce_fusion
  2.4 2.4 %scatter_custom_fusion = bf16[256,1024]{1,0:T(8,128)(2,1)} fusion(s32[128]{0:T(128)S(1)} %fusion.8, bf16[128,1024]{1,0:T(8,128)(2,1)} %param.5, bf16[]{:T(256)} %constant.117.clone.1), kind=kCustom, calls=%fused_computation.12 | custom fusion | bytes 524800 | tf_op jit(solution)/shard_map/scatter | solution.py:191
  4.8 7.4 %all-to-all-start = ((bf16[16,16,1024]{2,1,0:T(8,128)(2,1)}), bf16[16,16,1024]{2,1,0:T(8,128)(2,1)S(1)}, u32[]{:S(2)}, u32[]{:S(2)}) async-start(bf16[16,16,1024]{2,1,0:T(8,128)(2,1)} %bitcast.2), calls=%async_computation | async-start | bytes 1048576 | tf_op jit(solution)/shard_map/all_to_all | solution.py:192
  12.2 14.4 %all-to-all-done = bf16[16,16,1024]{2,1,0:T(8,128)(2,1)S(1)} async-done(((bf16[16,16,1024]{2,1,0:T(8,128)(2,1)}), bf16[16,16,1024]{2,1,0:T(8,128)(2,1)S(1)}, u32[]{:S(2)}, u32[]{:S(2)}) %all-to-all-start) | async-done | bytes 524320 | tf_op jit(solution)/shard_map/all_to_all | solution.py:192
  26.7 1.6 %copy-done.1 = bf16[1024,1024]{1,0:T(8,128)(2,1)S(1)} copy-done((bf16[1024,1024]{1,0:T(8,128)(2,1)S(1)}, bf16[1024,1024]{1,0:T(8,128)(2,1)}, u32[]{:S(2)}) %copy-start.1) | copy-done | bytes 2097176
  28.3 2.9 %shard_map.55 = (f32[256,1024]{1,0:T(8,128)}, f32[4608,128]{1,0:T(8,128)S(1)}) custom-call(bf16[256,1024]{1,0:T(8,128)(2,1)S(1)} %bitcast.8, bf16[1024,1024]{1,0:T(8,128)(2,1)S(1)} %copy-done.1), custom_call_target="tpu_custom_call" | custom-call | tf_op jit(solution)/shard_map/pallas_call | solution.py:195
  31.2 0.1 constant_dynamic-slice_fusion.5
  31.3 0.1 collective-permute-start
  31.4 2.9 %collective-permute-done = f32[2304,128]{1,0:T(8,128)} collective-permute-done((f32[2304,128]{1,0:T(8,128)S(1)}, f32[2304,128]{1,0:T(8,128)}, u32[]{:S(2)}, u32[]{:S(2)}) %collective-permute-start) | collective-permute-done | bytes 1179680 | tf_op jit(solution)/shard_map/ppermute | solution.py:139
  34.3 1.4 dynamic-slice_add_fusion
  35.7 0.1 fusion.9
  35.9 1.5 collective-permute-start.7
  37.3 1.0 collective-permute-start.1
  38.4 6.6 %collective-permute-done.7 = f32[576,128]{1,0:T(8,128)S(1)} collective-permute-done((f32[576,128]{1,0:T(8,128)S(1)}, f32[576,128]{1,0:T(8,128)S(1)}, u32[]{:S(2)}, u32[]{:S(2)}) %collective-permute-start.7) | collective-permute-done | bytes 294944 | tf_op jit(solution)/shard_map/ppermute | solution.py:139
  45.0 2.3 %collective-permute-start.8 = (f32[288,128]{1,0:T(8,128)S(1)}, f32[288,128]{1,0:T(8,128)S(1)}, u32[]{:S(2)}, u32[]{:S(2)}) collective-permute-start(f32[288,128]{1,0:T(8,128)S(1)} %constant_dynamic-slice_fusion), channel_id=1, source_target_pairs={{0,8},{1,9},{2,10},{3,11},{4,12},{5,13},{6,14},{7,15},{8,0},{9,1},... | collective-permute-start | bytes 442376 | tf_op jit(solution)/shard_map/ppermute | solution.py:139
  47.4 0.0 collective-permute-done.1
  47.4 0.4 collective-permute-start.2
  47.8 6.6 %collective-permute-done.8 = f32[288,128]{1,0:T(8,128)S(1)} collective-permute-done((f32[288,128]{1,0:T(8,128)S(1)}, f32[288,128]{1,0:T(8,128)S(1)}, u32[]{:S(2)}, u32[]{:S(2)}) %collective-permute-start.8) | collective-permute-done | bytes 147488 | tf_op jit(solution)/shard_map/ppermute | solution.py:139
  54.4 1.2 collective-permute-start.9
  55.6 0.0 collective-permute-done.2
  55.7 0.6 collective-permute-start.3
  56.3 2.9 %collective-permute-done.9 = f32[144,128]{1,0:T(8,128)S(1)} collective-permute-done((f32[144,128]{1,0:T(8,128)S(1)}, f32[144,128]{1,0:T(8,128)S(1)}, u32[]{:S(2)}, u32[]{:S(2)}) %collective-permute-start.9) | collective-permute-done | bytes 73760 | tf_op jit(solution)/shard_map/ppermute | solution.py:139
  59.1 0.9 collective-permute-start.10
  60.1 1.2 collective-permute-done.3
  61.2 0.4 collective-permute-start.4
  61.7 1.9 %collective-permute-done.10 = f32[144,128]{1,0:T(8,128)S(1)} collective-permute-done((f32[144,128]{1,0:T(8,128)S(1)}, f32[144,128]{1,0:T(8,128)S(1)}, u32[]{:S(2)}, u32[]{:S(2)}) %collective-permute-start.10) | collective-permute-done | bytes 73760 | tf_op jit(solution)/shard_map/ppermute | solution.py:139
  63.6 0.8 collective-permute-start.11
  64.3 4.6 %collective-permute-done.4 = f32[144,128]{1,0:T(8,128)S(1)} collective-permute-done((f32[144,128]{1,0:T(8,128)S(1)}, f32[144,128]{1,0:T(8,128)S(1)}, u32[]{:S(2)}, u32[]{:S(2)}) %collective-permute-start.4) | collective-permute-done | bytes 73760 | tf_op jit(solution)/shard_map/ppermute | solution.py:139
  69.0 0.1 collective-permute-start.5
  69.1 3.0 %collective-permute-done.11 = f32[288,128]{1,0:T(8,128)S(1)} collective-permute-done((f32[288,128]{1,0:T(8,128)S(1)}, f32[288,128]{1,0:T(8,128)S(1)}, u32[]{:S(2)}, u32[]{:S(2)}) %collective-permute-start.11) | collective-permute-done | bytes 147488 | tf_op jit(solution)/shard_map/ppermute | solution.py:139
  72.1 0.4 collective-permute-start.12
  72.5 3.2 %collective-permute-done.5 = f32[288,128]{1,0:T(8,128)S(1)} collective-permute-done((f32[288,128]{1,0:T(8,128)S(1)}, f32[288,128]{1,0:T(8,128)S(1)}, u32[]{:S(2)}, u32[]{:S(2)}) %collective-permute-start.5) | collective-permute-done | bytes 147488 | tf_op jit(solution)/shard_map/ppermute | solution.py:139
  75.8 1.4 collective-permute-start.6
  77.2 4.8 %all-to-all-start.1 = ((f32[16,16,1024]{2,1,0:T(8,128)}), f32[16,16,1024]{2,1,0:T(8,128)S(1)}, u32[]{:S(2)}, u32[]{:S(2)}) async-start(f32[16,16,1024]{2,1,0:T(8,128)} %bitcast.4), calls=%async_computation.1 | async-start | bytes 2097152 | tf_op jit(solution)/shard_map/all_to_all | solution.py:202
  82.1 0.5 collective-permute-done.6
  82.6 1.1 pad_maximum_fusion
  83.8 0.0 collective-permute-start.13
  83.8 21.2 %all-to-all-done.1 = f32[16,16,1024]{2,1,0:T(8,128)S(1)} async-done(((f32[16,16,1024]{2,1,0:T(8,128)}), f32[16,16,1024]{2,1,0:T(8,128)S(1)}, u32[]{:S(2)}, u32[]{:S(2)}) %all-to-all-start.1) | async-done | bytes 1048608 | tf_op jit(solution)/shard_map/all_to_all | solution.py:202
  104.9 0.8 gather_fusion.1
  105.7 0.0 collective-permute-done.13
  105.8 2.0 %maximum_select_fusion.gram_ref = f32[4608,128]{1,0:T(8,128)S(1)} fusion(f32[1152,128]{1,0:T(8,128)S(1)} %maximum_select_fusion.2, f32[1152,128]{1,0:T(8,128)S(1)} %maximum_select_fusion.1, f32[2304,128]{1,0:T(8,128)} %collective-permute-done.13, pred[]{:T(512)S(6)} %eq.46), kind=kLoop, calls=%fused_computation.3 | loop fusion | flops 2949120 | bytes 4718593 | tf_op jit(solution)/shard_map/jit(_where)/select_n | solution.py:153
  107.7 41.9 %shard_map.56.lower_ref = f32[4608,128]{1,0:T(8,128)S(1)} custom-call(f32[4608,128]{1,0:T(8,128)S(1)} %maximum_select_fusion.gram_ref), custom_call_target="tpu_custom_call" | custom-call | tf_op jit(solution)/shard_map/pallas_call | solution.py:206
  149.7 5.5 %shard_map.57 = f32[128,1024]{1,0:T(8,128)} custom-call(f32[128,1024]{1,0:T(8,128)S(1)} %gather_fusion.1, f32[4608,128]{1,0:T(8,128)S(1)} %shard_map.56.lower_ref), custom_call_target="tpu_custom_call" | custom-call | tf_op jit(solution)/shard_map/pallas_call | solution.py:212
  (23 shorter events, 0.4 us)
Async XLA Ops:
  0.0 0.7 copy-start
  4.8 21.9 %all-to-all-start = ((bf16[16,16,1024]{2,1,0:T(8,128)(2,1)}), bf16[16,16,1024]{2,1,0:T(8,128)(2,1)S(1)}, u32[]{:S(2)}, u32[]{:S(2)}) async-start(bf16[16,16,1024]{2,1,0:T(8,128)(2,1)} %bitcast.2), calls=%async_computation | async-start | bytes 1048576 | tf_op jit(solution)/shard_map/all_to_all | solution.py:192
  26.7 1.6 %copy-start.1 = (bf16[1024,1024]{1,0:T(8,128)(2,1)S(1)}, bf16[1024,1024]{1,0:T(8,128)(2,1)}, u32[]{:S(2)}) copy-start(bf16[1024,1024]{1,0:T(8,128)(2,1)} %corner_ref.1) | copy-start | bytes 6291460
  31.3 3.0 %collective-permute-start = (f32[2304,128]{1,0:T(8,128)S(1)}, f32[2304,128]{1,0:T(8,128)}, u32[]{:S(2)}, u32[]{:S(2)}) collective-permute-start(f32[2304,128]{1,0:T(8,128)S(1)} %constant_dynamic-slice_fusion.5), channel_id=1, source_target_pairs={{0,1},{1,0},{2,3},{3,2},{4,5},{5,4},{6,7},{7,6},{8,9},{9,8},{10,11... | collective-permute-start | bytes 3538952 | tf_op jit(solution)/shard_map/ppermute | solution.py:139
  35.9 9.1 %collective-permute-start.7 = (f32[576,128]{1,0:T(8,128)S(1)}, f32[576,128]{1,0:T(8,128)S(1)}, u32[]{:S(2)}, u32[]{:S(2)}) collective-permute-start(f32[576,128]{1,0:T(8,128)S(1)} %constant_dynamic-slice_fusion.1), channel_id=1, source_target_pairs={{0,4},{1,5},{2,6},{3,7},{4,0},{5,1},{6,2},{7,3},{8,12},{9,13},{10,... | collective-permute-start | bytes 884744 | tf_op jit(solution)/shard_map/ppermute | solution.py:139
  37.3 10.0 %collective-permute-start.1 = (f32[576,128]{1,0:T(8,128)S(1)}, f32[576,128]{1,0:T(8,128)S(1)}, u32[]{:S(2)}, u32[]{:S(2)}) collective-permute-start(f32[576,128]{1,0:T(8,128)S(1)} %constant_dynamic-slice_fusion.4), channel_id=1, source_target_pairs={{0,2},{1,3},{2,0},{3,1},{4,6},{5,7},{6,4},{7,5},{8,10},{9,11},{10,... | collective-permute-start | bytes 884744 | tf_op jit(solution)/shard_map/ppermute | solution.py:139
  45.0 9.3 %collective-permute-start.8 = (f32[288,128]{1,0:T(8,128)S(1)}, f32[288,128]{1,0:T(8,128)S(1)}, u32[]{:S(2)}, u32[]{:S(2)}) collective-permute-start(f32[288,128]{1,0:T(8,128)S(1)} %constant_dynamic-slice_fusion), channel_id=1, source_target_pairs={{0,8},{1,9},{2,10},{3,11},{4,12},{5,13},{6,14},{7,15},{8,0},{9,1},... | collective-permute-start | bytes 442376 | tf_op jit(solution)/shard_map/ppermute | solution.py:139
  47.4 8.2 %collective-permute-start.2 = (f32[288,128]{1,0:T(8,128)S(1)}, f32[288,128]{1,0:T(8,128)S(1)}, u32[]{:S(2)}, u32[]{:S(2)}) collective-permute-start(f32[288,128]{1,0:T(8,128)S(1)} %constant_dynamic-slice_fusion.3), channel_id=1, source_target_pairs={{0,4},{1,5},{2,6},{3,7},{4,0},{5,1},{6,2},{7,3},{8,12},{9,13},{10,... | collective-permute-start | bytes 442376 | tf_op jit(solution)/shard_map/ppermute | solution.py:139
  54.4 4.7 %collective-permute-start.9 = (f32[144,128]{1,0:T(8,128)S(1)}, f32[144,128]{1,0:T(8,128)S(1)}, u32[]{:S(2)}, u32[]{:S(2)}) collective-permute-start(f32[144,128]{1,0:T(8,128)S(1)} %constant_dynamic-slice_fusion.6), channel_id=1, source_target_pairs={{0,2},{1,3},{2,0},{3,1},{4,6},{5,7},{6,4},{7,5},{8,10},{9,11},{10,... | collective-permute-start | bytes 221192 | tf_op jit(solution)/shard_map/ppermute | solution.py:139
  55.7 5.6 %collective-permute-start.3 = (f32[144,128]{1,0:T(8,128)S(1)}, f32[144,128]{1,0:T(8,128)S(1)}, u32[]{:S(2)}, u32[]{:S(2)}) collective-permute-start(f32[144,128]{1,0:T(8,128)S(1)} %constant_dynamic-slice_fusion.2), channel_id=1, source_target_pairs={{0,8},{1,9},{2,10},{3,11},{4,12},{5,13},{6,14},{7,15},{8,0},{9,1},... | collective-permute-start | bytes 221192 | tf_op jit(solution)/shard_map/ppermute | solution.py:139
  59.1 4.4 %collective-permute-start.10 = (f32[144,128]{1,0:T(8,128)S(1)}, f32[144,128]{1,0:T(8,128)S(1)}, u32[]{:S(2)}, u32[]{:S(2)}) collective-permute-start(f32[144,128]{1,0:T(8,128)S(1)} %dynamic-slice_add_fusion.5), channel_id=1, source_target_pairs={{0,2},{1,3},{2,0},{3,1},{4,6},{5,7},{6,4},{7,5},{8,10},{9,11},{10,... | collective-permute-start | bytes 221192 | tf_op jit(solution)/shard_map/ppermute | solution.py:139
  61.2 7.7 %collective-permute-start.4 = (f32[144,128]{1,0:T(8,128)S(1)}, f32[144,128]{1,0:T(8,128)S(1)}, u32[]{:S(2)}, u32[]{:S(2)}) collective-permute-start(f32[144,128]{1,0:T(8,128)S(1)} %dynamic-slice_add_fusion.6), channel_id=1, source_target_pairs={{0,8},{1,9},{2,10},{3,11},{4,12},{5,13},{6,14},{7,15},{8,0},{9,1},... | collective-permute-start | bytes 221192 | tf_op jit(solution)/shard_map/ppermute | solution.py:139
  63.6 8.5 %collective-permute-start.11 = (f32[288,128]{1,0:T(8,128)S(1)}, f32[288,128]{1,0:T(8,128)S(1)}, u32[]{:S(2)}, u32[]{:S(2)}) collective-permute-start(f32[288,128]{1,0:T(8,128)S(1)} %maximum_select_fusion.6), channel_id=1, source_target_pairs={{0,8},{1,9},{2,10},{3,11},{4,12},{5,13},{6,14},{7,15},{8,0},{9,1},... | collective-permute-start | bytes 442376 | tf_op jit(solution)/shard_map/ppermute | solution.py:139
  69.0 6.8 %collective-permute-start.5 = (f32[288,128]{1,0:T(8,128)S(1)}, f32[288,128]{1,0:T(8,128)S(1)}, u32[]{:S(2)}, u32[]{:S(2)}) collective-permute-start(f32[288,128]{1,0:T(8,128)S(1)} %maximum_select_fusion.5), channel_id=1, source_target_pairs={{0,4},{1,5},{2,6},{3,7},{4,0},{5,1},{6,2},{7,3},{8,12},{9,13},{10,... | collective-permute-start | bytes 442376 | tf_op jit(solution)/shard_map/ppermute | solution.py:139
  72.1 9.9 %collective-permute-start.12 = (f32[576,128]{1,0:T(8,128)S(1)}, f32[576,128]{1,0:T(8,128)S(1)}, u32[]{:S(2)}, u32[]{:S(2)}) collective-permute-start(f32[576,128]{1,0:T(8,128)S(1)} %maximum_select_fusion.4), channel_id=1, source_target_pairs={{0,4},{1,5},{2,6},{3,7},{4,0},{5,1},{6,2},{7,3},{8,12},{9,13},{10,... | collective-permute-start | bytes 884744 | tf_op jit(solution)/shard_map/ppermute | solution.py:139
  75.8 6.8 %collective-permute-start.6 = (f32[576,128]{1,0:T(8,128)S(1)}, f32[576,128]{1,0:T(8,128)S(1)}, u32[]{:S(2)}, u32[]{:S(2)}) collective-permute-start(f32[576,128]{1,0:T(8,128)S(1)} %maximum_select_fusion.3), channel_id=1, source_target_pairs={{0,2},{1,3},{2,0},{3,1},{4,6},{5,7},{6,4},{7,5},{8,10},{9,11},{10,... | collective-permute-start | bytes 884744 | tf_op jit(solution)/shard_map/ppermute | solution.py:139
  77.2 27.7 %all-to-all-start.1 = ((f32[16,16,1024]{2,1,0:T(8,128)}), f32[16,16,1024]{2,1,0:T(8,128)S(1)}, u32[]{:S(2)}, u32[]{:S(2)}) async-start(f32[16,16,1024]{2,1,0:T(8,128)} %bitcast.4), calls=%async_computation.1 | async-start | bytes 2097152 | tf_op jit(solution)/shard_map/all_to_all | solution.py:202
  83.8 22.0 %collective-permute-start.13 = (f32[2304,128]{1,0:T(8,128)}, f32[2304,128]{1,0:T(8,128)}, u32[]{:S(2)}, u32[]{:S(2)}) collective-permute-start(f32[2304,128]{1,0:T(8,128)} %pad_maximum_fusion), channel_id=1, source_target_pairs={{0,1},{1,0},{2,3},{3,2},{4,5},{5,4},{6,7},{7,6},{8,9},{9,8},{10,11... | collective-permute-start | bytes 3538952 | tf_op jit(solution)/shard_map/ppermute | solution.py:139

commit v2 on v1

v2 whole, which is shorter than its diff:
```python
import functools
import math

import jax
import jax.numpy as jnp
from jax import lax
from jax.experimental import pallas as pl
from jax.experimental.pallas import tpu as pltpu
from jax.sharding import PartitionSpec as P

SIDE = 128


def column_offsets(count):
    offsets = [0]
    for j in range(count):
        offsets.append(offsets[-1] + (count - j) * SIDE)
    return offsets


def split(x):
    high = x.astype(jnp.bfloat16)
    return high, (x - high.astype(jnp.float32)).astype(jnp.bfloat16)


def left(x, axis):
    high, low = split(x)
    return jnp.concatenate([high, high, low], axis=axis)


def right(x, axis):
    high, low = split(x)
    return jnp.concatenate([high, low, high], axis=axis)


def dot_nt(a, b):
    return lax.dot_general(a, b, (((1,), (1,)), ((), ())), preferred_element_type=jnp.float32)


def dot_tn(a, b):
    return lax.dot_general(a, b, (((0,), (0,)), ((), ())), preferred_element_type=jnp.float32)


def iota(shape, axis):
    return lax.broadcasted_iota(jnp.int32, shape, axis)


def route_kernel(capacity, edge_ref, joining_ref, left_ref, right_ref, slot_ref, packed_ref):
    bf16 = jnp.bfloat16
    rows = edge_ref.shape[0]
    owners = joining_ref.shape[0]
    slots = packed_ref.shape[0]
    one = lambda hit: hit.astype(jnp.float32)
    label = iota((owners, rows), 0)
    is_left = one(label == left_ref[...]).astype(bf16)
    options = dot_tn(joining_ref[...].astype(jnp.float32).astype(bf16), is_left)
    target = jnp.sum(jnp.where(label == right_ref[...], options, 0.0), axis=0, keepdims=True)
    is_target = label.astype(jnp.float32) == target
    earlier = one(iota((rows, rows), 0) < iota((rows, rows), 1)).astype(bf16)
    before = jnp.dot(one(is_target).astype(bf16), earlier, preferred_element_type=jnp.float32)
    order = jnp.sum(jnp.where(is_target, before, 0.0), axis=0, keepdims=True)
    slot = (target * capacity + order).astype(jnp.int32)
    slot_ref[...] = slot
    placed = one(iota((slots, rows), 0) == slot).astype(bf16)
    packed_ref[...] = jnp.dot(
        placed, edge_ref[...], preferred_element_type=jnp.float32
    ).astype(bf16)


def images_kernel(arrived_ref, corner_ref, images_ref, gram_ref):
    width = corner_ref.shape[1]
    count = width // SIDE
    offsets = column_offsets(count)
    images = jnp.dot(arrived_ref[...], corner_ref[...], preferred_element_type=jnp.float32)
    images_ref[...] = images
    first, second = left(images, 0), right(images, 0)
    for j in range(0, count, 2):
        part = dot_tn(first[:, j * SIDE :], second[:, j * SIDE : (j + 2) * SIDE])
        gram_ref[offsets[j] : offsets[j + 1], :] = part[:, :SIDE]
        gram_ref[offsets[j + 1] : offsets[j + 2], :] = part[SIDE:, SIDE:]


def eliminate(rows, start):
    shape = rows[0].shape
    lane, sub = iota(shape, 1), iota(shape, 0)
    rows = list(rows)
    groups = len(rows)

    def spread(x):
        return jnp.broadcast_to(x, shape)

    def columns_of(x, first):
        return [spread(x[:, first + j : first + j + 1]) for j in range(8)]

    pivots = columns_of(rows[0], start)
    for m in range(groups):
        g = start + 8 * m
        later = range(m + 1, groups)
        inside = (lane >= g) & (lane < g + 8)
        current = rows[m]
        ahead, ahead_below = [], []
        if later:
            ahead = columns_of(current, g + 8)
            ahead_below = columns_of(rows[m + 1], g + 8)
        below = {r: columns_of(rows[r], g) for r in later}
        current = jnp.where(inside, (lane - g == sub).astype(jnp.float32), current)
        for r in later:
            rows[r] = jnp.where(inside, 0.0, rows[r])
        diagonal = pivots[0]
        for j in range(8):
            inverse = 1.0 / spread(pivots[j][j : j + 1, :])
            pivot_row = spread(current[j : j + 1, :])
            heads = [spread(x[j : j + 1, :]) for x in pivots[j + 1 :]]
            ahead_heads = [spread(x[j : j + 1, :]) for x in ahead]
            if j:
                diagonal = jnp.where(sub == j, pivots[j], diagonal)
            if j < 7:
                weight = jnp.where(sub > j, pivots[j], 0.0) * inverse
                current = current - weight * pivot_row
                for k, head in enumerate(heads, j + 1):
                    pivots[k] = pivots[k] - weight * head
                ahead = [x - weight * head for x, head in zip(ahead, ahead_heads)]
            for r in later:
                weight = below[r][j] * inverse
                rows[r] = rows[r] - weight * pivot_row
                for k, head in enumerate(heads, j + 1):
                    below[r][k] = below[r][k] - weight * head
                if r == m + 1:
                    ahead_below = [x - weight * head for x, head in zip(ahead_below, ahead_heads)]
        rows[m] = current * lax.rsqrt(diagonal)
        pivots = ahead_below
    return rows


def invert_factor(block):
    size = block.shape[0]
    half = size // 2
    groups = range(0, half, 8)
    lane, row = iota((half, size), 1), iota((half, size), 0)
    upper = jnp.concatenate(eliminate([block[g : g + 8, :] for g in groups], 0), axis=0)
    inverse = jnp.where((lane < half) & (lane > row), 0.0, upper)
    lower = jnp.where(lane < half, 0.0, block[half:, :])
    lower = lower - dot_tn(left(upper[:, half:], 0), right(inverse, 0))
    lower = jnp.concatenate(eliminate([lower[g : g + 8, :] for g in groups], half), axis=0)
    return jnp.concatenate(
        [jnp.where(lane < half, inverse, 0.0), jnp.where(lane <= row + half, lower, 0.0)], axis=0
    )


def cholesky_kernel(count, gram_ref, lower_ref):
    offsets = column_offsets(count)
    lower_ref[...] = gram_ref[...]

    def update(k, first, second, columns):
        for j in columns[::2]:
            top = (j - k - 1) * SIDE
            part = dot_nt(first[top:], second[top : top + 2 * SIDE])
            lower_ref[offsets[j] : offsets[j + 1], :] -= part[:, :SIDE]
            if j + 1 in columns:
                lower_ref[offsets[j + 1] : offsets[j + 2], :] -= part[SIDE:, SIDE:]

    previous = None
    for k in range(count):
        top, bottom = offsets[k] + SIDE, offsets[k + 1]
        inverse = invert_factor(lower_ref[offsets[k] : top, :])
        if previous is not None:
            update(k - 1, *previous, range(k + 1, count))
        lower_ref[offsets[k] : top, :] = inverse
        if k + 1 < count:
            panel = dot_nt(left(lower_ref[top:bottom, :], 1), right(inverse, 1))
            lower_ref[top:bottom, :] = panel
            previous = left(panel, 1), right(panel, 1)
            update(k, *previous, range(k + 1, k + 2))


def solve_kernel(count, factor, returned_ref, slot_ref, lower_ref, out_ref, rest):
    offsets = column_offsets(count)
    slots, rows = returned_ref.shape[0], slot_ref.shape[1]
    placed = (iota((slots, rows), 0) == slot_ref[...]).astype(jnp.float32).astype(jnp.bfloat16)
    high, low = split(returned_ref[...])
    rest[...] = dot_tn(placed, high) + dot_tn(placed, low)
    for k in range(count):
        here = slice(k * SIDE, (k + 1) * SIDE)
        top = offsets[k] + SIDE
        solved = dot_nt(left(rest[:, here], 1), right(lower_ref[offsets[k] : top, :], 1))
        out_ref[:, here] = solved * factor
        if k < count - 1:
            rest[:, (k + 1) * SIDE :] -= dot_nt(
                left(solved, 1), right(lower_ref[top : offsets[k + 1], :], 1)
            )


def kernel_call(kernel, out_shape, scratch=(), work=0):
    return pl.pallas_call(
        kernel,
        out_shape=out_shape,
        scratch_shapes=list(scratch),
        cost_estimate=pl.CostEstimate(flops=2 * work, bytes_accessed=0, transcendentals=0),
        compiler_params=pltpu.CompilerParams(vmem_limit_bytes=16 << 20),
    )


def swap(x, bit):
    return lax.ppermute(x, "sec", [(i, i ^ bit) for i in range(lax.axis_size("sec"))])


def halve(x, bit):
    upper = (lax.axis_index("sec") // bit) % 2
    half = x.shape[0] // 2
    sent = lax.dynamic_slice_in_dim(x, (1 - upper) * half, half, 0)
    kept = lax.dynamic_slice_in_dim(x, upper * half, half, 0)
    return kept + swap(sent, bit)


def double(x, bit):
    upper = (lax.axis_index("sec") // bit) % 2 == 1
    other = swap(x, bit)
    return jnp.where(
        upper, jnp.concatenate([other, x], axis=0), jnp.concatenate([x, other], axis=0)
    )


def reduce_gram(packed):
    bits = [1 << b for b in range(1, lax.axis_size("sec").bit_length() - 1)]
    cut = len(bits) // 2
    orders = [bits, bits[cut:] + bits[:cut]]
    mine = halve(packed, 1)
    streams = []
    for order, part in zip(orders, jnp.split(mine, 2, axis=0)):
        for bit in order:
            part = halve(part, bit)
        streams.append(part)
    whole = []
    for order, part in zip(orders, streams):
        for bit in reversed(order):
            part = double(part, bit)
        whole.append(part)
    return double(jnp.concatenate(whole, axis=0), 1)


def per_device(edge_rows, corner, joining, charge_left, charge_right):
    row_count, feature_len = edge_rows.shape
    owners = lax.axis_size("sec")
    capacity = 2 * row_count // owners
    slots = owners * capacity
    factor = math.sqrt(row_count * owners)
    count = feature_len // SIDE
    packed_rows = column_offsets(count)[-1]
    f32 = jnp.float32
    slot, packed = kernel_call(
        functools.partial(route_kernel, capacity),
        (
            jax.ShapeDtypeStruct((1, row_count), jnp.int32),
            jax.ShapeDtypeStruct((slots, feature_len), edge_rows.dtype),
        ),
    )(edge_rows, joining, charge_left[None, :], charge_right[None, :])
    arrived = lax.all_to_all(
        packed.reshape(owners, capacity, feature_len), "sec", split_axis=0, concat_axis=0, tiled=True
    )
    product, gram = kernel_call(
        images_kernel,
        (
            jax.ShapeDtypeStruct((slots, feature_len), f32),
            jax.ShapeDtypeStruct((packed_rows, SIDE), f32),
        ),
    )(arrived.reshape(slots, feature_len), corner)
    total = reduce_gram(gram)
    product, total = lax.optimization_barrier((product, total))
    returned = lax.all_to_all(
        product.reshape(owners, capacity, feature_len), "sec", split_axis=0, concat_axis=0, tiled=True
    )
    lower = kernel_call(
        functools.partial(cholesky_kernel, count),
        jax.ShapeDtypeStruct((packed_rows, SIDE), f32),
        work=20 * packed_rows * feature_len * feature_len,
    )(total)
    returned, lower = lax.optimization_barrier((returned, lower))
    return kernel_call(
        functools.partial(solve_kernel, count, factor),
        jax.ShapeDtypeStruct((row_count, feature_len), f32),
        [pltpu.VMEM((row_count, feature_len), f32)],
    )(returned.reshape(slots, feature_len), slot, lower)


def solution(mesh):
    placed = (
        P(("runs", "sec"), None),
        P(("runs", "sec"), None),
        P("runs", None),
        P(("runs", "sec")),
        P(("runs", "sec")),
    )
    return jax.shard_map(
        per_device, mesh=mesh, in_specs=placed, out_specs=P(("runs", "sec"), None), check_vma=False
    )
```

time: 157 us -> 125 us (0.80)
  Pallas kernels: 50.3 us -> 33.4 us
  waiting for transfers between devices: 69 us -> 55.6 us
  other arithmetic: 5.93 us -> 3.78 us
  local copies, waits for them, and re-layouts: 6.32 us -> 7.93 us
    all_to_all x1, waiting for transfers between devices: 21.2 us -> 0.01 us  [per_device(): lax.all_to_all(product.reshape(owners, capacity, feature_len), 'sec', spl...]
    pallas_call x1, Pallas kernels: 41.9 us -> 25.6 us  [per_device(): kernel_call(functools.partial(cholesky_kernel, count), jax.ShapeDtypeStru...]
    ppermute x14, waiting for transfers between devices: 33.4 us -> 41.1 us  [swap(): lax.ppermute(x, 'sec', [(i, i ^ bit) for i in range(lax.axis_size('sec'))])]
    unnamed x4 -> x14, local copies, waits for them, and re-layouts: 1.6 us -> 7.65 us
    scatter x1 -> x0, local copies, waits for them, and re-layouts: 2.38 us -> none  [per_device(): jnp.zeros((slots, feature_len), edge_rows.dtype).at[slot_index]]
    gather x2 -> x0, local copies, waits for them, and re-layouts: 2.07 us -> none  [the longest x1 1.27 us: per_device(): target = joining[charge_left, charge_right]]
  transfers between devices with their start and end apart: 16 -> 16, of which waited for: 12 -> 13; matrix products, arithmetic and copies ran while one was open for 1% -> 0% of each run, Pallas kernels for 0% -> 21%
where the time goes in v2:
time: 125 us; the launch traced here: 124 us
  waiting for transfers between devices  55.6 us (44%)
  Pallas kernels  33.4 us (27%)
  starting transfers between devices  23.5 us (19%)
  local copies, waits for them, and re-layouts  7.93 us (6%)
  other arithmetic  3.78 us (3%)
    ppermute x14, waiting for transfers between devices, swap(): lax.ppermute(x, 'sec', [(i, i ^ bit) for i in range(lax.axis_size('sec'))])  41.1 us
    pallas_call x1, Pallas kernels, per_device(): kernel_call(functools.partial(cholesky_kernel, count), jax.ShapeDtypeStru...  25.6 us
    all_to_all x1, waiting for transfers between devices, per_device(): lax.all_to_all(packed.reshape(owners, capacity, feature_len), 'sec', spli...  14.4 us
    ppermute x14, starting transfers between devices, swap(): lax.ppermute(x, 'sec', [(i, i ^ bit) for i in range(lax.axis_size('sec'))])  11.2 us
    unnamed x14, local copies, waits for them, and re-layouts  7.65 us
    all_to_all x1, starting transfers between devices, per_device(): lax.all_to_all(packed.reshape(owners, capacity, feature_len), 'sec', spli...  7.38 us
    all_to_all x1, starting transfers between devices, per_device(): lax.all_to_all(product.reshape(owners, capacity, feature_len), 'sec', spl...  4.87 us
    pallas_call x1, Pallas kernels, per_device(): kernel_call(functools.partial(solve_kernel, count, factor), jax.ShapeDtyp...  4.6 us
  transfers between devices with their start and end apart: 16, of which 13 were waited for; matrix products, arithmetic and copies ran while one was open for 0% of the time, Pallas kernels for 21%

profile of v2, /device:TPU:0, one launch (start us, length us, event | category | flops | bytes accessed | tf_op | source)
XLA Modules:
  0.0 124.4 jit_solution(2959477895590575248)
XLA Ops:
  0.0 0.9 copy-done.3
  1.0 0.7 copy-done.4
  1.7 0.7 copy-done.5
  2.3 0.7 copy-done.6
  3.0 1.4 %shard_map.55 = (s32[1,128]{1,0:T(1,128)S(1)}, bf16[256,1024]{1,0:T(8,128)(2,1)}) custom-call(bf16[128,1024]{1,0:T(8,128)(2,1)S(1)} %copy-done.3, s32[16,16]{1,0:T(8,128)S(1)} %copy-done.4, s32[1,128]{1,0:T(1,128)S(1)} %bitcast.7, s32[1,128]{1,0:T(1,128)S(1)} %bitcast.8), custom_call_target="tpu_custom_call" | custom-call | tf_op jit(solution)/shard_map/pallas_call | solution.py:250
  4.3 7.4 %all-to-all-start = ((bf16[16,16,1024]{2,1,0:T(8,128)(2,1)}), bf16[16,16,1024]{2,1,0:T(8,128)(2,1)S(1)}, u32[]{:S(2)}, u32[]{:S(2)}) async-start(bf16[16,16,1024]{2,1,0:T(8,128)(2,1)} %bitcast.2), calls=%async_computation | async-start | bytes 1048576 | tf_op jit(solution)/shard_map/all_to_all | solution.py:257
  11.7 14.4 %all-to-all-done = bf16[16,16,1024]{2,1,0:T(8,128)(2,1)S(1)} async-done(((bf16[16,16,1024]{2,1,0:T(8,128)(2,1)}), bf16[16,16,1024]{2,1,0:T(8,128)(2,1)S(1)}, u32[]{:S(2)}, u32[]{:S(2)}) %all-to-all-start) | async-done | bytes 524320 | tf_op jit(solution)/shard_map/all_to_all | solution.py:257
  26.2 1.6 %copy-done.2 = bf16[1024,1024]{1,0:T(8,128)(2,1)S(1)} copy-done((bf16[1024,1024]{1,0:T(8,128)(2,1)S(1)}, bf16[1024,1024]{1,0:T(8,128)(2,1)}, u32[]{:S(2)}) %copy-start.2) | copy-done | bytes 2097176
  27.8 1.8 %shard_map.56 = (f32[256,1024]{1,0:T(8,128)}, f32[4608,128]{1,0:T(8,128)S(1)}) custom-call(bf16[256,1024]{1,0:T(8,128)(2,1)S(1)} %bitcast.6, bf16[1024,1024]{1,0:T(8,128)(2,1)S(1)} %copy-done.2), custom_call_target="tpu_custom_call" | custom-call | tf_op jit(solution)/shard_map/pallas_call | solution.py:260
  29.6 0.1 constant_dynamic-slice_fusion.6
  29.7 0.1 collective-permute-start
  29.8 2.9 %collective-permute-done = f32[2304,128]{1,0:T(8,128)} collective-permute-done((f32[2304,128]{1,0:T(8,128)S(1)}, f32[2304,128]{1,0:T(8,128)}, u32[]{:S(2)}, u32[]{:S(2)}) %collective-permute-start) | collective-permute-done | bytes 1179680 | tf_op jit(solution)/shard_map/ppermute | solution.py:204
  32.8 1.4 %dynamic-slice_add_fusion = f32[2304,128]{1,0:T(8,128)S(1)} fusion(f32[2304,128]{1,0:T(8,128)} %collective-permute-done, f32[4608,128]{1,0:T(8,128)S(1)} %get-tuple-element.15, s32[]{:T(128)S(6)} %select_n.163), kind=kLoop, calls=%fused_computation.2 | loop fusion | flops 294912 | bytes 3538948 | tf_op jit(solution)/shard_map/add | solution.py:212
  34.2 0.1 fusion
  34.3 1.5 %collective-permute-start.7 = (f32[576,128]{1,0:T(8,128)S(1)}, f32[576,128]{1,0:T(8,128)S(1)}, u32[]{:S(2)}, u32[]{:S(2)}) collective-permute-start(f32[576,128]{1,0:T(8,128)S(1)} %constant_dynamic-slice_fusion.2), channel_id=1, source_target_pairs={{0,4},{1,5},{2,6},{3,7},{4,0},{5,1},{6,2},{7,3},{8,12},{9,13},{10,... | collective-permute-start | bytes 884744 | tf_op jit(solution)/shard_map/ppermute | solution.py:204
  35.8 1.0 collective-permute-start.1
  36.8 6.6 %collective-permute-done.7 = f32[576,128]{1,0:T(8,128)S(1)} collective-permute-done((f32[576,128]{1,0:T(8,128)S(1)}, f32[576,128]{1,0:T(8,128)S(1)}, u32[]{:S(2)}, u32[]{:S(2)}) %collective-permute-start.7) | collective-permute-done | bytes 294944 | tf_op jit(solution)/shard_map/ppermute | solution.py:204
  43.5 2.3 %collective-permute-start.8 = (f32[288,128]{1,0:T(8,128)S(1)}, f32[288,128]{1,0:T(8,128)S(1)}, u32[]{:S(2)}, u32[]{:S(2)}) collective-permute-start(f32[288,128]{1,0:T(8,128)S(1)} %constant_dynamic-slice_fusion.1), channel_id=1, source_target_pairs={{0,8},{1,9},{2,10},{3,11},{4,12},{5,13},{6,14},{7,15},{8,0},{9,1},... | collective-permute-start | bytes 442376 | tf_op jit(solution)/shard_map/ppermute | solution.py:204
  45.8 0.0 collective-permute-done.1
  45.9 0.4 collective-permute-start.2
  46.2 6.5 %collective-permute-done.8 = f32[288,128]{1,0:T(8,128)S(1)} collective-permute-done((f32[288,128]{1,0:T(8,128)S(1)}, f32[288,128]{1,0:T(8,128)S(1)}, u32[]{:S(2)}, u32[]{:S(2)}) %collective-permute-start.8) | collective-permute-done | bytes 147488 | tf_op jit(solution)/shard_map/ppermute | solution.py:204
  52.8 1.2 collective-permute-start.9
  54.1 0.0 collective-permute-done.2
  54.1 0.6 collective-permute-start.3
  54.7 2.9 %collective-permute-done.9 = f32[144,128]{1,0:T(8,128)S(1)} collective-permute-done((f32[144,128]{1,0:T(8,128)S(1)}, f32[144,128]{1,0:T(8,128)S(1)}, u32[]{:S(2)}, u32[]{:S(2)}) %collective-permute-start.9) | collective-permute-done | bytes 73760 | tf_op jit(solution)/shard_map/ppermute | solution.py:204
  57.6 0.9 collective-permute-start.10
  58.5 1.2 collective-permute-done.3
  59.7 0.4 collective-permute-start.4
  60.1 1.9 %collective-permute-done.10 = f32[144,128]{1,0:T(8,128)S(1)} collective-permute-done((f32[144,128]{1,0:T(8,128)S(1)}, f32[144,128]{1,0:T(8,128)S(1)}, u32[]{:S(2)}, u32[]{:S(2)}) %collective-permute-start.10) | collective-permute-done | bytes 73760 | tf_op jit(solution)/shard_map/ppermute | solution.py:204
  62.0 0.8 collective-permute-start.11
  62.8 4.6 %collective-permute-done.4 = f32[144,128]{1,0:T(8,128)S(1)} collective-permute-done((f32[144,128]{1,0:T(8,128)S(1)}, f32[144,128]{1,0:T(8,128)S(1)}, u32[]{:S(2)}, u32[]{:S(2)}) %collective-permute-start.4) | collective-permute-done | bytes 73760 | tf_op jit(solution)/shard_map/ppermute | solution.py:204
  67.4 0.1 collective-permute-start.5
  67.5 3.0 %collective-permute-done.11 = f32[288,128]{1,0:T(8,128)S(1)} collective-permute-done((f32[288,128]{1,0:T(8,128)S(1)}, f32[288,128]{1,0:T(8,128)S(1)}, u32[]{:S(2)}, u32[]{:S(2)}) %collective-permute-start.11) | collective-permute-done | bytes 147488 | tf_op jit(solution)/shard_map/ppermute | solution.py:204
  70.6 0.4 collective-permute-start.12
  71.0 3.3 %collective-permute-done.5 = f32[288,128]{1,0:T(8,128)S(1)} collective-permute-done((f32[288,128]{1,0:T(8,128)S(1)}, f32[288,128]{1,0:T(8,128)S(1)}, u32[]{:S(2)}, u32[]{:S(2)}) %collective-permute-start.5) | collective-permute-done | bytes 147488 | tf_op jit(solution)/shard_map/ppermute | solution.py:204
  74.3 1.4 %collective-permute-start.6 = (f32[576,128]{1,0:T(8,128)S(1)}, f32[576,128]{1,0:T(8,128)S(1)}, u32[]{:S(2)}, u32[]{:S(2)}) collective-permute-start(f32[576,128]{1,0:T(8,128)S(1)} %maximum_select_fusion.3), channel_id=1, source_target_pairs={{0,2},{1,3},{2,0},{3,1},{4,6},{5,7},{6,4},{7,5},{8,10},{9,11},{10,... | collective-permute-start | bytes 884744 | tf_op jit(solution)/shard_map/ppermute | solution.py:204
  75.7 2.5 %collective-permute-done.12 = f32[576,128]{1,0:T(8,128)S(1)} collective-permute-done((f32[576,128]{1,0:T(8,128)S(1)}, f32[576,128]{1,0:T(8,128)S(1)}, u32[]{:S(2)}, u32[]{:S(2)}) %collective-permute-start.12) | collective-permute-done | bytes 294944 | tf_op jit(solution)/shard_map/ppermute | solution.py:204
  78.2 2.8 %collective-permute-done.6 = f32[576,128]{1,0:T(8,128)S(1)} collective-permute-done((f32[576,128]{1,0:T(8,128)S(1)}, f32[576,128]{1,0:T(8,128)S(1)}, u32[]{:S(2)}, u32[]{:S(2)}) %collective-permute-start.6) | collective-permute-done | bytes 294944 | tf_op jit(solution)/shard_map/ppermute | solution.py:204
  81.1 0.1 pad_maximum_fusion
  81.2 0.1 collective-permute-start.13
  81.3 3.0 %collective-permute-done.13 = f32[2304,128]{1,0:T(8,128)} collective-permute-done((f32[2304,128]{1,0:T(8,128)S(1)}, f32[2304,128]{1,0:T(8,128)}, u32[]{:S(2)}, u32[]{:S(2)}) %collective-permute-start.13) | collective-permute-done | bytes 1179680 | tf_op jit(solution)/shard_map/ppermute | solution.py:204
  84.2 2.0 %maximum_select_fusion.gram_ref = f32[4608,128]{1,0:T(8,128)S(1)} fusion(f32[1152,128]{1,0:T(8,128)S(1)} %maximum_select_fusion.2, f32[1152,128]{1,0:T(8,128)S(1)} %maximum_select_fusion.1, f32[2304,128]{1,0:T(8,128)} %collective-permute-done.13, pred[]{:T(512)S(6)} %eq.30), kind=kLoop, calls=%fused_computation | loop fusion | flops 2949120 | bytes 4718593 | tf_op jit(solution)/shard_map/jit(_where)/select_n | solution.py:218
  86.2 4.9 %all-to-all-start.1 = ((f32[16,16,1024]{2,1,0:T(8,128)}), f32[16,16,1024]{2,1,0:T(8,128)}, u32[]{:S(2)}, u32[]{:S(2)}) async-start(f32[16,16,1024]{2,1,0:T(8,128)} %bitcast.4), calls=%async_computation.1 | async-start | bytes 2097152 | tf_op jit(solution)/shard_map/all_to_all | solution.py:269
  91.1 25.6 %shard_map.57.lower_ref = f32[4608,128]{1,0:T(8,128)S(1)} custom-call(f32[4608,128]{1,0:T(8,128)S(1)} %maximum_select_fusion.gram_ref), custom_call_target="tpu_custom_call" | custom-call | flops 193273528320 | tf_op jit(solution)/shard_map/pallas_call | solution.py:272
  116.7 1.4 %copy-done = f32[4608,128]{1,0:T(8,128)} copy-done((f32[4608,128]{1,0:T(8,128)}, f32[4608,128]{1,0:T(8,128)S(1)}, u32[]{:S(2)}) %copy-start) | copy-done | bytes 2359320
  118.2 0.0 all-to-all-done.1
  118.2 1.7 %copy-done.1 = f32[4608,128]{1,0:T(8,128)S(1)} copy-done((f32[4608,128]{1,0:T(8,128)S(1)}, f32[4608,128]{1,0:T(8,128)}, u32[]{:S(2)}) %copy-start.1) | copy-done | bytes 2359320
  119.8 4.6 %shard_map.58 = f32[128,1024]{1,0:T(8,128)} custom-call(f32[256,1024]{1,0:T(8,128)} %bitcast.5.returned_ref, s32[1,128]{1,0:T(1,128)S(1)} %get-tuple-element.19.slot_ref, f32[4608,128]{1,0:T(8,128)S(1)} %copy-done.1), custom_call_target="tpu_custom_call" | custom-call | tf_op jit(solution)/shard_map/pallas_call | solution.py:278
  (25 shorter events, 0.4 us)
Async XLA Ops:
  0.0 0.9 copy-start.3
  1.0 0.7 copy-start.4
  1.6 0.7 copy-start.5
  2.3 0.7 copy-start.6
  4.3 21.9 %all-to-all-start = ((bf16[16,16,1024]{2,1,0:T(8,128)(2,1)}), bf16[16,16,1024]{2,1,0:T(8,128)(2,1)S(1)}, u32[]{:S(2)}, u32[]{:S(2)}) async-start(bf16[16,16,1024]{2,1,0:T(8,128)(2,1)} %bitcast.2), calls=%async_computation | async-start | bytes 1048576 | tf_op jit(solution)/shard_map/all_to_all | solution.py:257
  26.2 1.6 %copy-start.2 = (bf16[1024,1024]{1,0:T(8,128)(2,1)S(1)}, bf16[1024,1024]{1,0:T(8,128)(2,1)}, u32[]{:S(2)}) copy-start(bf16[1024,1024]{1,0:T(8,128)(2,1)} %corner_ref.1) | copy-start | bytes 6291460
  29.7 3.0 %collective-permute-start = (f32[2304,128]{1,0:T(8,128)S(1)}, f32[2304,128]{1,0:T(8,128)}, u32[]{:S(2)}, u32[]{:S(2)}) collective-permute-start(f32[2304,128]{1,0:T(8,128)S(1)} %constant_dynamic-slice_fusion.6), channel_id=1, source_target_pairs={{0,1},{1,0},{2,3},{3,2},{4,5},{5,4},{6,7},{7,6},{8,9},{9,8},{10,11... | collective-permute-start | bytes 3538952 | tf_op jit(solution)/shard_map/ppermute | solution.py:204
  34.3 9.1 %collective-permute-start.7 = (f32[576,128]{1,0:T(8,128)S(1)}, f32[576,128]{1,0:T(8,128)S(1)}, u32[]{:S(2)}, u32[]{:S(2)}) collective-permute-start(f32[576,128]{1,0:T(8,128)S(1)} %constant_dynamic-slice_fusion.2), channel_id=1, source_target_pairs={{0,4},{1,5},{2,6},{3,7},{4,0},{5,1},{6,2},{7,3},{8,12},{9,13},{10,... | collective-permute-start | bytes 884744 | tf_op jit(solution)/shard_map/ppermute | solution.py:204
  35.8 10.0 %collective-permute-start.1 = (f32[576,128]{1,0:T(8,128)S(1)}, f32[576,128]{1,0:T(8,128)S(1)}, u32[]{:S(2)}, u32[]{:S(2)}) collective-permute-start(f32[576,128]{1,0:T(8,128)S(1)} %constant_dynamic-slice_fusion.5), channel_id=1, source_target_pairs={{0,2},{1,3},{2,0},{3,1},{4,6},{5,7},{6,4},{7,5},{8,10},{9,11},{10,... | collective-permute-start | bytes 884744 | tf_op jit(solution)/shard_map/ppermute | solution.py:204
  43.5 9.3 %collective-permute-start.8 = (f32[288,128]{1,0:T(8,128)S(1)}, f32[288,128]{1,0:T(8,128)S(1)}, u32[]{:S(2)}, u32[]{:S(2)}) collective-permute-start(f32[288,128]{1,0:T(8,128)S(1)} %constant_dynamic-slice_fusion.1), channel_id=1, source_target_pairs={{0,8},{1,9},{2,10},{3,11},{4,12},{5,13},{6,14},{7,15},{8,0},{9,1},... | collective-permute-start | bytes 442376 | tf_op jit(solution)/shard_map/ppermute | solution.py:204
  45.9 8.2 %collective-permute-start.2 = (f32[288,128]{1,0:T(8,128)S(1)}, f32[288,128]{1,0:T(8,128)S(1)}, u32[]{:S(2)}, u32[]{:S(2)}) collective-permute-start(f32[288,128]{1,0:T(8,128)S(1)} %constant_dynamic-slice_fusion.4), channel_id=1, source_target_pairs={{0,4},{1,5},{2,6},{3,7},{4,0},{5,1},{6,2},{7,3},{8,12},{9,13},{10,... | collective-permute-start | bytes 442376 | tf_op jit(solution)/shard_map/ppermute | solution.py:204
  52.8 4.7 %collective-permute-start.9 = (f32[144,128]{1,0:T(8,128)S(1)}, f32[144,128]{1,0:T(8,128)S(1)}, u32[]{:S(2)}, u32[]{:S(2)}) collective-permute-start(f32[144,128]{1,0:T(8,128)S(1)} %constant_dynamic-slice_fusion), channel_id=1, source_target_pairs={{0,2},{1,3},{2,0},{3,1},{4,6},{5,7},{6,4},{7,5},{8,10},{9,11},{10,... | collective-permute-start | bytes 221192 | tf_op jit(solution)/shard_map/ppermute | solution.py:204
  54.1 5.6 %collective-permute-start.3 = (f32[144,128]{1,0:T(8,128)S(1)}, f32[144,128]{1,0:T(8,128)S(1)}, u32[]{:S(2)}, u32[]{:S(2)}) collective-permute-start(f32[144,128]{1,0:T(8,128)S(1)} %constant_dynamic-slice_fusion.3), channel_id=1, source_target_pairs={{0,8},{1,9},{2,10},{3,11},{4,12},{5,13},{6,14},{7,15},{8,0},{9,1},... | collective-permute-start | bytes 221192 | tf_op jit(solution)/shard_map/ppermute | solution.py:204
  57.6 4.4 %collective-permute-start.10 = (f32[144,128]{1,0:T(8,128)S(1)}, f32[144,128]{1,0:T(8,128)S(1)}, u32[]{:S(2)}, u32[]{:S(2)}) collective-permute-start(f32[144,128]{1,0:T(8,128)S(1)} %dynamic-slice_add_fusion.5), channel_id=1, source_target_pairs={{0,2},{1,3},{2,0},{3,1},{4,6},{5,7},{6,4},{7,5},{8,10},{9,11},{10,... | collective-permute-start | bytes 221192 | tf_op jit(solution)/shard_map/ppermute | solution.py:204
  59.7 7.7 %collective-permute-start.4 = (f32[144,128]{1,0:T(8,128)S(1)}, f32[144,128]{1,0:T(8,128)S(1)}, u32[]{:S(2)}, u32[]{:S(2)}) collective-permute-start(f32[144,128]{1,0:T(8,128)S(1)} %dynamic-slice_add_fusion.6), channel_id=1, source_target_pairs={{0,8},{1,9},{2,10},{3,11},{4,12},{5,13},{6,14},{7,15},{8,0},{9,1},... | collective-permute-start | bytes 221192 | tf_op jit(solution)/shard_map/ppermute | solution.py:204
  62.0 8.6 %collective-permute-start.11 = (f32[288,128]{1,0:T(8,128)S(1)}, f32[288,128]{1,0:T(8,128)S(1)}, u32[]{:S(2)}, u32[]{:S(2)}) collective-permute-start(f32[288,128]{1,0:T(8,128)S(1)} %maximum_select_fusion.6), channel_id=1, source_target_pairs={{0,8},{1,9},{2,10},{3,11},{4,12},{5,13},{6,14},{7,15},{8,0},{9,1},... | collective-permute-start | bytes 442376 | tf_op jit(solution)/shard_map/ppermute | solution.py:204
  67.4 6.8 %collective-permute-start.5 = (f32[288,128]{1,0:T(8,128)S(1)}, f32[288,128]{1,0:T(8,128)S(1)}, u32[]{:S(2)}, u32[]{:S(2)}) collective-permute-start(f32[288,128]{1,0:T(8,128)S(1)} %maximum_select_fusion.5), channel_id=1, source_target_pairs={{0,4},{1,5},{2,6},{3,7},{4,0},{5,1},{6,2},{7,3},{8,12},{9,13},{10,... | collective-permute-start | bytes 442376 | tf_op jit(solution)/shard_map/ppermute | solution.py:204
  70.6 7.6 %collective-permute-start.12 = (f32[576,128]{1,0:T(8,128)S(1)}, f32[576,128]{1,0:T(8,128)S(1)}, u32[]{:S(2)}, u32[]{:S(2)}) collective-permute-start(f32[576,128]{1,0:T(8,128)S(1)} %maximum_select_fusion.4), channel_id=1, source_target_pairs={{0,4},{1,5},{2,6},{3,7},{4,0},{5,1},{6,2},{7,3},{8,12},{9,13},{10,... | collective-permute-start | bytes 884744 | tf_op jit(solution)/shard_map/ppermute | solution.py:204
  74.3 6.8 %collective-permute-start.6 = (f32[576,128]{1,0:T(8,128)S(1)}, f32[576,128]{1,0:T(8,128)S(1)}, u32[]{:S(2)}, u32[]{:S(2)}) collective-permute-start(f32[576,128]{1,0:T(8,128)S(1)} %maximum_select_fusion.3), channel_id=1, source_target_pairs={{0,2},{1,3},{2,0},{3,1},{4,6},{5,7},{6,4},{7,5},{8,10},{9,11},{10,... | collective-permute-start | bytes 884744 | tf_op jit(solution)/shard_map/ppermute | solution.py:204
  81.2 3.0 %collective-permute-start.13 = (f32[2304,128]{1,0:T(8,128)S(1)}, f32[2304,128]{1,0:T(8,128)}, u32[]{:S(2)}, u32[]{:S(2)}) collective-permute-start(f32[2304,128]{1,0:T(8,128)S(1)} %pad_maximum_fusion), channel_id=1, source_target_pairs={{0,1},{1,0},{2,3},{3,2},{4,5},{5,4},{6,7},{7,6},{8,9},{9,8},{10,11... | collective-permute-start | bytes 3538952 | tf_op jit(solution)/shard_map/ppermute | solution.py:204
  86.2 31.9 %all-to-all-start.1 = ((f32[16,16,1024]{2,1,0:T(8,128)}), f32[16,16,1024]{2,1,0:T(8,128)}, u32[]{:S(2)}, u32[]{:S(2)}) async-start(f32[16,16,1024]{2,1,0:T(8,128)} %bitcast.4), calls=%async_computation.1 | async-start | bytes 2097152 | tf_op jit(solution)/shard_map/all_to_all | solution.py:269
  116.7 1.4 %copy-start = (f32[4608,128]{1,0:T(8,128)}, f32[4608,128]{1,0:T(8,128)S(1)}, u32[]{:S(2)}) copy-start(f32[4608,128]{1,0:T(8,128)S(1)} %shard_map.57.lower_ref) | copy-start | bytes 7077892
  118.2 1.7 %copy-start.1 = (f32[4608,128]{1,0:T(8,128)S(1)}, f32[4608,128]{1,0:T(8,128)}, u32[]{:S(2)}) copy-start(f32[4608,128]{1,0:T(8,128)} %copy-done) | copy-start | bytes 7077892

commit v3 on v2

v3 whole, which is shorter than its diff:
```python
import functools
import math

import jax
import jax.numpy as jnp
from jax import lax
from jax.experimental import pallas as pl
from jax.experimental.pallas import tpu as pltpu
from jax.sharding import PartitionSpec as P

SIDE = 128


def column_offsets(count):
    offsets = [0]
    for j in range(count):
        offsets.append(offsets[-1] + (count - j) * SIDE)
    return offsets


def split(x):
    high = x.astype(jnp.bfloat16)
    return high, (x - high.astype(jnp.float32)).astype(jnp.bfloat16)


def left(x, axis):
    high, low = split(x)
    return jnp.concatenate([high, high, low], axis=axis)


def right(x, axis):
    high, low = split(x)
    return jnp.concatenate([high, low, high], axis=axis)


def dot_nt(a, b):
    return lax.dot_general(a, b, (((1,), (1,)), ((), ())), preferred_element_type=jnp.float32)


def dot_tn(a, b):
    return lax.dot_general(a, b, (((0,), (0,)), ((), ())), preferred_element_type=jnp.float32)


def dot_nn(a, b):
    return jnp.dot(a, b, preferred_element_type=jnp.float32)


def iota(shape, axis):
    return lax.broadcasted_iota(jnp.int32, shape, axis)


def route_kernel(
    capacity, edge_hbm, joining_hbm, left_hbm, right_hbm, slot_ref, packed_ref,
    edge_ref, joining_ref, left_ref, right_ref, done,
):
    bf16 = jnp.bfloat16
    pairs = [
        (joining_hbm, joining_ref),
        (left_hbm, left_ref),
        (right_hbm, right_ref),
        (edge_hbm, edge_ref),
    ]
    copies = [pltpu.make_async_copy(a, b, done.at[i]) for i, (a, b) in enumerate(pairs)]
    for copy in copies:
        copy.start()
    rows = edge_ref.shape[0]
    owners = joining_ref.shape[0]
    slots = packed_ref.shape[0]
    one = lambda hit: hit.astype(jnp.float32)
    label = iota((owners, rows), 0)
    for copy in copies[:3]:
        copy.wait()
    is_left = one(label == left_ref[...]).astype(bf16)
    options = dot_tn(joining_ref[...].astype(jnp.float32).astype(bf16), is_left)
    target = jnp.sum(jnp.where(label == right_ref[...], options, 0.0), axis=0, keepdims=True)
    is_target = label.astype(jnp.float32) == target
    earlier = one(iota((rows, rows), 0) < iota((rows, rows), 1)).astype(bf16)
    before = jnp.dot(one(is_target).astype(bf16), earlier, preferred_element_type=jnp.float32)
    order = jnp.sum(jnp.where(is_target, before, 0.0), axis=0, keepdims=True)
    slot = (target * capacity + order).astype(jnp.int32)
    slot_ref[...] = slot
    placed = one(iota((slots, rows), 0) == slot).astype(bf16)
    copies[3].wait()
    packed_ref[...] = jnp.dot(
        placed, edge_ref[...], preferred_element_type=jnp.float32
    ).astype(bf16)


def fetch_kernel(mine_hbm, other_hbm, mine_ref, other_ref, done):
    copies = [
        pltpu.make_async_copy(mine_hbm, mine_ref, done.at[0]),
        pltpu.make_async_copy(other_hbm, other_ref, done.at[1]),
    ]
    for copy in copies:
        copy.start()
    for copy in copies:
        copy.wait()


def shares(count):
    pairs = list(range(count // 2))
    outer = [p for p in pairs if p % 4 in (0, 3)]
    return outer, [p for p in pairs if p not in outer]


def share_rows(count):
    offsets = column_offsets(count)
    full = (offsets[-1] - count // 2 * SIDE) // 2
    return (full + 128) // 2, full // 2


def images_kernel(
    core_ref, arrived_ref, other_arrived_ref, corner_ref, other_corner_ref, images_ref, gram_ref
):
    width = corner_ref.shape[1]
    count = width // SIDE
    others = dot_nn(other_arrived_ref[...], other_corner_ref[...])
    images = dot_nn(arrived_ref[...], corner_ref[...])
    images_ref[...] = images
    images = jnp.concatenate([images, others], axis=0)
    first, second = left(images, 0), right(images, 0)
    row, col = iota((SIDE, SIDE), 0), iota((SIDE, SIDE), 1)

    def store(at, x):
        gram_ref[at : at + x.shape[0], :] = x

    def share(pairs):
        at = 0
        diagonals = []
        for p in pairs:
            start = 2 * p * SIDE
            part = dot_tn(first[:, start:], second[:, start : start + 2 * SIDE])
            upper, lower = part[:SIDE, :SIDE], part[SIDE : 2 * SIDE, SIDE:]
            store(at, jnp.where(row >= col, upper, lower))
            store(at + SIDE, part[SIDE : 2 * SIDE, :SIDE])
            diagonals.append(jnp.sum(jnp.where(row == col, lower, 0.0), axis=0, keepdims=True))
            at += 2 * SIDE
            rest = width - start - 2 * SIDE
            if rest:
                store(at, part[2 * SIDE :, :SIDE])
                store(at + rest, part[2 * SIDE :, SIDE:])
                at += 2 * rest
        store(at, jnp.zeros((gram_ref.shape[0] - at, SIDE), jnp.float32))
        for i, diagonal in enumerate(diagonals):
            store(at + i, diagonal)

    for core, pairs in enumerate(shares(count)):
        pl.when(core_ref[0] == core)(functools.partial(share, pairs))


def unpack_share(count, core, parts, lower_ref, diagonal_ref, done):
    offsets = column_offsets(count)
    cut = parts[0].shape[0]
    copies = []

    def copy(target, source, rows):
        for ref, low in ((parts[0], 0), (parts[1], cut)):
            begin, end = max(source, low), min(source + rows, low + ref.shape[0])
            if begin < end:
                copies.append(
                    pltpu.make_async_copy(
                        ref.at[begin - low : end - low],
                        lower_ref.at[target + begin - source : target + end - source],
                        done.at[core, len(copies)],
                    )
                )

    at = 0
    for p in shares(count)[core]:
        first, second = offsets[2 * p], offsets[2 * p + 1]
        rest = (count - 2 * p - 2) * SIDE
        copy(first, at, 2 * SIDE)
        if rest:
            copy(first + 2 * SIDE, at + 2 * SIDE, rest)
            copy(second + SIDE, at + 2 * SIDE + rest, rest)
        at += 2 * SIDE + 2 * rest
    copies.append(
        pltpu.make_async_copy(
            parts[1].at[at - cut : at - cut + 8], diagonal_ref.at[core], done.at[core, len(copies)]
        )
    )
    return copies


def part_diagonals(count, core, lower_ref, diagonal_ref, which):
    offsets = column_offsets(count)
    row, col = iota((SIDE, SIDE), 0), iota((SIDE, SIDE), 1)
    for i, p in list(enumerate(shares(count)[core]))[which]:
        first, second = offsets[2 * p], offsets[2 * p + 1]
        both = lower_ref[first : first + SIDE, :]
        turned = both.T
        diagonal = diagonal_ref[core, i : i + 1, :]
        lower_ref[first : first + SIDE, :] = jnp.where(row >= col, both, turned)
        lower_ref[second : second + SIDE, :] = jnp.where(
            row == col, diagonal, jnp.where(row < col, both, turned)
        )


def eliminate(rows, start, tick):
    shape = rows[0].shape
    lane, sub = iota(shape, 1), iota(shape, 0)
    rows = list(rows)
    groups = len(rows)

    def spread(x):
        return jnp.broadcast_to(x, shape)

    def columns_of(x, first):
        return [spread(x[:, first + j : first + j + 1]) for j in range(8)]

    pivots = columns_of(rows[0], start)
    for m in range(groups):
        g = start + 8 * m
        later = range(m + 1, groups)
        inside = (lane >= g) & (lane < g + 8)
        current = rows[m]
        ahead, ahead_below = [], []
        if later:
            ahead = columns_of(current, g + 8)
            ahead_below = columns_of(rows[m + 1], g + 8)
        below = {r: columns_of(rows[r], g) for r in later}
        current = jnp.where(inside, (lane - g == sub).astype(jnp.float32), current)
        for r in later:
            rows[r] = jnp.where(inside, 0.0, rows[r])
        diagonal = pivots[0]
        for j in range(8):
            inverse = 1.0 / spread(pivots[j][j : j + 1, :])
            pivot_row = spread(current[j : j + 1, :])
            heads = [spread(x[j : j + 1, :]) for x in pivots[j + 1 :]]
            ahead_heads = [spread(x[j : j + 1, :]) for x in ahead]
            if j:
                diagonal = jnp.where(sub == j, pivots[j], diagonal)
            if j < 7:
                weight = jnp.where(sub > j, pivots[j], 0.0) * inverse
                current = current - weight * pivot_row
                for k, head in enumerate(heads, j + 1):
                    pivots[k] = pivots[k] - weight * head
                ahead = [x - weight * head for x, head in zip(ahead, ahead_heads)]
            for r in later:
                weight = below[r][j] * inverse
                rows[r] = rows[r] - weight * pivot_row
                for k, head in enumerate(heads, j + 1):
                    below[r][k] = below[r][k] - weight * head
                if r == m + 1:
                    ahead_below = [x - weight * head for x, head in zip(ahead_below, ahead_heads)]
        rows[m] = current * lax.rsqrt(diagonal)
        pivots = ahead_below
        tick()
    return rows


def invert_factor(block, beside=()):
    size = block.shape[0]
    half = size // 2
    groups = range(0, half, 8)
    ticks = 2 * len(groups)
    pending = [list(beside[t * len(beside) // ticks : (t + 1) * len(beside) // ticks]) for t in range(ticks)]
    pending.reverse()

    def tick():
        for piece in pending.pop():
            piece()

    lane, row = iota((half, size), 1), iota((half, size), 0)
    upper = jnp.concatenate(eliminate([block[g : g + 8, :] for g in groups], 0, tick), axis=0)
    inverse = jnp.where((lane < half) & (lane > row), 0.0, upper)
    lower = jnp.where(lane < half, 0.0, block[half:, :])
    lower = lower - dot_tn(left(upper[:, half:], 0), right(inverse, 0))
    lower = jnp.concatenate(
        eliminate([lower[g : g + 8, :] for g in groups], half, tick), axis=0
    )
    return jnp.concatenate(
        [jnp.where(lane < half, inverse, 0.0), jnp.where(lane <= row + half, lower, 0.0)], axis=0
    )


def join_inverses(low, between, high):
    middle = dot_nn(left(high, 1), right(dot_nn(left(between, 1), right(low, 0)), 0))
    return jnp.concatenate(
        [
            jnp.concatenate([low, jnp.zeros((low.shape[0], high.shape[1]), jnp.float32)], axis=1),
            jnp.concatenate([-middle, high], axis=1),
        ],
        axis=0,
    )


def cholesky_kernel(
    count, core_ref, mine0, mine1, other0, other1, inverse_hbm, across_hbm, next_hbm, beyond_hbm, tail_hbm,
    lower_ref, diagonal_ref, inverse_ref, across_ref, next_ref, beyond_ref, done, out_done,
):
    offsets = column_offsets(count)
    half, three = count // 2, 3 * count // 4
    for core in (0, 1):

        @pl.when(core_ref[0] == core)
        def _(core=core):
            copies = unpack_share(count, core, (mine0, mine1), lower_ref, diagonal_ref, done)
            copies += unpack_share(count, 1 - core, (other0, other1), lower_ref, diagonal_ref, done)
            for copy in copies:
                copy.start()

    arrivals = [
        unpack_share(count, core, (mine0, mine1), lower_ref, diagonal_ref, done) for core in (0, 1)
    ]
    arrivals[0][0].wait()
    arrivals[0][-1].wait()
    part_diagonals(count, 0, lower_ref, diagonal_ref, slice(0, 1))

    def arrive():
        for copy in arrivals[0][1:-1] + arrivals[1]:
            copy.wait()
        part_diagonals(count, 0, lower_ref, diagonal_ref, slice(1, None))
        part_diagonals(count, 1, lower_ref, diagonal_ref, slice(None))

    def at(i, j):
        first = offsets[j] + (i - j) * SIDE
        return slice(first, first + SIDE)

    def blocks(rows, columns):
        return jnp.concatenate(
            [lower_ref[at(rows[0], j).start : at(rows[-1], j).stop, :] for j in columns], axis=1
        )

    inverses = {}
    outward = []

    def send(ref, hbm):
        outward.append(pltpu.make_async_copy(ref, hbm, out_done.at[len(outward)]))
        outward[-1].start()

    def pair(p):
        def run():
            inverses[p] = join_inverses(
                lower_ref[at(p, p), :], lower_ref[at(p + 1, p), :], lower_ref[at(p + 1, p + 1), :]
            )

        return run

    def join_half():
        inverse_ref[...] = right(
            join_inverses(inverses[0], blocks(range(2, 4), range(2)), inverses[2]), 1
        )
        send(inverse_ref, inverse_hbm)

    def across():
        across_ref[...] = right(blocks(range(half, count), range(half)), 1)
        send(across_ref, across_hbm)

    def beyond():
        next_ref[...] = right(inverses[half], 1)
        beyond_ref[...] = right(blocks(range(three, count), range(half, three)), 1)
        send(next_ref, next_hbm)
        send(beyond_ref, beyond_hbm)

    extra = {2: [pair(0)], 4: [pair(2), join_half, across], 6: [pair(half), beyond]}

    def rest_of(k, head):
        pieces, forms = [], {}
        if k + 2 >= count:
            return pieces
        rest = slice(at(k + 2, k).start, offsets[k + 1])

        def panel():
            below = dot_nt(left(lower_ref[rest, :], 1), right(lower_ref[at(k, k), :], 1))
            lower_ref[rest, :] = below
            forms["left"], forms["right"] = left(below, 1), right(below, 1)

        def next_column():
            lower_ref[at(k + 2, k + 1).start : offsets[k + 2], :] -= dot_nt(
                forms["left"], right(head, 1)
            )

        def product(j, i):
            def run():
                high = min(i + 2, count)
                rows = slice((i - k - 2) * SIDE, (high - k - 2) * SIDE)
                columns = slice((j - k - 2) * SIDE, (min(j + 2, count) - k - 2) * SIDE)
                part = dot_nt(forms["left"][rows], forms["right"][columns])
                lower_ref[at(i, j).start : at(high - 1, j).stop, :] -= part[:, :SIDE]
                if j + 1 < count:
                    skip = SIDE if i == j else 0
                    lower_ref[at(max(i, j + 1), j + 1).start : at(high - 1, j + 1).stop, :] -= part[
                        skip:, SIDE:
                    ]

            return run

        pieces += [panel, next_column]
        for j in range(k + 2, count, 2):
            for i in range(j, count, 2):
                pieces.append(product(j, i))
        return pieces

    beside = [lambda: None] * 2 + [arrive]
    for k in range(count - 1):
        inverse = invert_factor(lower_ref[at(k, k), :], beside + extra.get(k, []))
        lower_ref[at(k, k), :] = inverse
        head = dot_nt(left(lower_ref[at(k + 1, k), :], 1), right(inverse, 1))
        lower_ref[at(k + 1, k), :] = head
        lower_ref[at(k + 1, k + 1), :] -= dot_nt(left(head, 1), right(head, 1))
        beside = rest_of(k, head)
    send(lower_ref.at[offsets[count - 2] :], tail_hbm)
    for copy in outward:
        copy.wait()


def solve_kernel(
    count, factor, slot_ref, tail_hbm, returned_hbm, inverse_hbm, across_hbm, next_hbm, beyond_hbm, out_ref,
    tail_ref, returned_ref, inverse_ref, across_ref, next_ref, beyond_ref, done,
):
    half, three = count // 2 * SIDE, 3 * count // 4 * SIDE
    pairs = [
        (tail_hbm, tail_ref),
        (returned_hbm, returned_ref),
        (inverse_hbm, inverse_ref),
        (across_hbm, across_ref),
        (next_hbm, next_ref),
        (beyond_hbm, beyond_ref),
    ]
    copies = [pltpu.make_async_copy(a, b, done.at[i]) for i, (a, b) in enumerate(pairs)]
    for copy in copies:
        copy.start()
    slots, rows = returned_ref.shape[0], slot_ref.shape[1]
    width = returned_ref.shape[1]
    placed = (iota((slots, rows), 0) == slot_ref[...]).astype(jnp.float32).astype(jnp.bfloat16)
    rest = {}

    def home():
        copies[1].wait()
        high, low = split(returned_ref[...])
        rest[0] = dot_tn(placed, high) + dot_tn(placed, low)

    def solved(first, last, inverse):
        x = dot_nt(left(rest[first][:, : last - first], 1), inverse)
        out_ref[:, first:last] = x * factor
        rest[last] = left(x, 1)

    def update(first, last, below):
        rest[last] = rest[first][:, last - first :] - dot_nt(rest[last], below)

    def ready(i, ref):
        copies[i].wait()
        return ref[...]

    steps = [
        home,
        lambda: solved(0, half, ready(2, inverse_ref)),
        lambda: update(0, half, ready(3, across_ref)),
        lambda: solved(half, three, ready(4, next_ref)),
        lambda: update(half, three, ready(5, beyond_ref)),
        lambda: solved(three, three + SIDE, right(tail_ref[:SIDE, :], 1)),
        lambda: update(three, three + SIDE, right(tail_ref[SIDE : 2 * SIDE, :], 1)),
    ]
    copies[0].wait()
    last = invert_factor(tail_ref[2 * SIDE :, :], [lambda: None] * 2 + steps)
    solved(width - SIDE, width, right(last, 1))


SMEM = pl.BlockSpec(memory_space=pltpu.SMEM)
VMEM = pl.BlockSpec(memory_space=pltpu.VMEM)
ANY = pl.BlockSpec(memory_space=pl.ANY)


def kernel_call(kernel, in_specs, out_shape, scratch=(), out_specs=None, mib=16, work=0):
    return pl.pallas_call(
        kernel,
        in_specs=in_specs,
        out_specs=out_specs or jax.tree.map(lambda _: VMEM, out_shape),
        out_shape=out_shape,
        scratch_shapes=list(scratch),
        cost_estimate=pl.CostEstimate(flops=2 * work, bytes_accessed=0, transcendentals=0),
        compiler_params=pltpu.CompilerParams(vmem_limit_bytes=mib << 20),
    )


def swap(x, bit):
    return lax.ppermute(x, "sec", [(i, i ^ bit) for i in range(lax.axis_size("sec"))])


def halve(x, bit):
    upper = (lax.axis_index("sec") // bit) % 2
    half = x.shape[0] // 2
    sent = lax.dynamic_slice_in_dim(x, (1 - upper) * half, half, 0)
    kept = lax.dynamic_slice_in_dim(x, upper * half, half, 0)
    return kept + swap(sent, bit)


def double(x, bit):
    upper = (lax.axis_index("sec") // bit) % 2 == 1
    other = swap(x, bit)
    return jnp.where(
        upper, jnp.concatenate([other, x], axis=0), jnp.concatenate([x, other], axis=0)
    )


def reduce_shares(share):
    bits = [1 << b for b in range(1, lax.axis_size("sec").bit_length() - 1)]
    orders = [bits, bits[1:2] + bits[:1] + bits[2:]]
    streams = []
    for order, part in zip(orders, share):
        for bit in order:
            part = halve(part, bit)
        streams.append(part)
    whole = []
    for order, part in zip(orders, streams):
        for bit in reversed(order[1:]):
            part = double(part, bit)
        whole.append((part, order[0]))
    return whole


def per_device(edge_rows, corner, joining, charge_left, charge_right):
    row_count, feature_len = edge_rows.shape
    owners = lax.axis_size("sec")
    capacity = 2 * row_count // owners
    slots = owners * capacity
    factor = math.sqrt(row_count * owners)
    count = feature_len // SIDE
    packed_rows = column_offsets(count)[-1]
    f32, i32 = jnp.float32, jnp.int32
    dma = pltpu.SemaphoreType.DMA
    core = (lax.axis_index("sec") % 2).astype(i32)[None]
    slot, packed = kernel_call(
        functools.partial(route_kernel, capacity),
        [ANY] * 4,
        (
            jax.ShapeDtypeStruct((1, row_count), i32),
            jax.ShapeDtypeStruct((slots, feature_len), edge_rows.dtype),
        ),
        [
            pltpu.VMEM((row_count, feature_len), edge_rows.dtype),
            pltpu.VMEM(joining.shape, i32),
            pltpu.VMEM((1, row_count), i32),
            pltpu.VMEM((1, row_count), i32),
            dma((4,)),
        ],
        mib=60,
    )(edge_rows, joining, charge_left[None, :], charge_right[None, :])
    arrived = lax.all_to_all(
        packed.reshape(owners, capacity, feature_len), "sec", split_axis=0, concat_axis=0, tiled=True
    ).reshape(slots, feature_len)
    corners = kernel_call(
        fetch_kernel,
        [ANY] * 2,
        (jax.ShapeDtypeStruct(corner.shape, corner.dtype),) * 2,
        [dma((2,))],
        work=slots * feature_len * feature_len,
        mib=16,
    )(corner, swap(corner, 1))
    product, share = kernel_call(
        images_kernel,
        [SMEM] + [VMEM] * 4,
        (
            jax.ShapeDtypeStruct((slots, feature_len), f32),
            jax.ShapeDtypeStruct((sum(share_rows(count)), SIDE), f32),
        ),
    )(core, arrived, swap(arrived, 1), *corners)
    streams = reduce_shares(jnp.split(share, [share_rows(count)[0]], axis=0))
    (product, first), second = lax.optimization_barrier(((product, streams[0][0]), streams[1][0]))
    streams = [(first, streams[0][1]), (second, streams[1][1])]
    parts = [double(part, bit) for part, bit in streams]
    returned = lax.all_to_all(
        product.reshape(owners, capacity, feature_len), "sec", split_axis=0, concat_axis=0, tiled=True
    )
    half, quarter = feature_len // 2, feature_len // 4
    lower = kernel_call(
        functools.partial(cholesky_kernel, count),
        [SMEM] + [ANY] * 4,
        (
            jax.ShapeDtypeStruct((half, 3 * half), jnp.bfloat16),
            jax.ShapeDtypeStruct((half, 3 * half), jnp.bfloat16),
            jax.ShapeDtypeStruct((quarter, 3 * quarter), jnp.bfloat16),
            jax.ShapeDtypeStruct((quarter, 3 * quarter), jnp.bfloat16),
            jax.ShapeDtypeStruct((3 * SIDE, SIDE), f32),
        ),
        [
            pltpu.VMEM((packed_rows, SIDE), f32),
            pltpu.VMEM((2, 8, SIDE), f32),
            pltpu.VMEM((half, 3 * half), jnp.bfloat16),
            pltpu.VMEM((half, 3 * half), jnp.bfloat16),
            pltpu.VMEM((quarter, 3 * quarter), jnp.bfloat16),
            pltpu.VMEM((quarter, 3 * quarter), jnp.bfloat16),
            dma((2, 8)),
            dma((5,)),
        ],
        (ANY,) * 5,
        mib=60,
        work=20 * packed_rows * feature_len * feature_len,
    )(core, *parts, *[swap(part, 1) for part in parts])
    returned, lower = lax.optimization_barrier((returned, lower))
    return kernel_call(
        functools.partial(solve_kernel, count, factor),
        [VMEM] + [ANY] * 6,
        jax.ShapeDtypeStruct((row_count, feature_len), f32),
        [
            pltpu.VMEM((3 * SIDE, SIDE), f32),
            pltpu.VMEM((slots, feature_len), f32),
            pltpu.VMEM((half, 3 * half), jnp.bfloat16),
            pltpu.VMEM((half, 3 * half), jnp.bfloat16),
            pltpu.VMEM((quarter, 3 * quarter), jnp.bfloat16),
            pltpu.VMEM((quarter, 3 * quarter), jnp.bfloat16),
            dma((6,)),
        ],
        mib=60,
    )(slot, lower[4], returned.reshape(slots, feature_len), *lower[:4])


def solution(mesh):
    placed = (
        P(("runs", "sec"), None),
        P(("runs", "sec"), None),
        P("runs", None),
        P(("runs", "sec")),
        P(("runs", "sec")),
    )
    return jax.shard_map(
        per_device, mesh=mesh, in_specs=placed, out_specs=P(("runs", "sec"), None), check_vma=False
    )
```

time: 125 us -> 111 us (0.89)
  waiting for transfers between devices: 55.6 us -> 31 us
  blocking collectives: 0 us -> 21.5 us
  starting transfers between devices: 23.5 us -> 16.2 us
  local copies, waits for them, and re-layouts: 7.93 us -> 3.4 us
  Pallas kernels: 33.4 us -> 37.9 us
  other arithmetic: 3.78 us -> 0.25 us
    all_to_all x0 -> x1, blocking collectives: none -> 21.5 us  [per_device(): lax.all_to_all(packed.reshape(owners, capacity, feature_len), 'sec', spli...]
    all_to_all x1 -> x0, waiting for transfers between devices: 14.4 us -> none  [per_device(): lax.all_to_all(packed.reshape(owners, capacity, feature_len), 'sec', spli...]
    ppermute x14 -> x16, waiting for transfers between devices: 41.1 us -> 31 us  [swap(): lax.ppermute(x, 'sec', [(i, i ^ bit) for i in range(lax.axis_size('sec'))])]
    all_to_all x1 -> x0, starting transfers between devices: 7.38 us -> none  [per_device(): lax.all_to_all(packed.reshape(owners, capacity, feature_len), 'sec', spli...]
    pallas_call x4 -> x5, Pallas kernels: 33.4 us -> 37.9 us  [the longest x1 25.2 us: per_device(): kernel_call(functools.partial(cholesky_kernel, count), [SMEM] + [ANY] * 4...]
    unnamed x14 -> x10, local copies, waits for them, and re-layouts: 7.65 us -> 3.21 us
    select_n x7 -> x6, other arithmetic: 2.15 us -> 0.14 us  [double(): jnp.where(upper, jnp.concatenate([other, x], axis=0), jnp.concatenate([x,...]
    add x7 -> x6, other arithmetic: 1.55 us -> 0.11 us  [halve(): return kept + swap(sent, bit)]
  transfers between devices with their start and end apart: 16 -> 17, of which waited for: 13 -> 11; matrix products, arithmetic and copies ran while one was open for 0% -> 0% of each run, Pallas kernels for 21% -> 25%
where the time goes in v3:
time: 111 us
  Pallas kernels  37.9 us (34%)
  waiting for transfers between devices  31 us (28%)
  blocking collectives  21.5 us (19%)
  starting transfers between devices  16.2 us (15%)
  local copies, waits for them, and re-layouts  3.4 us (3%)
    ppermute x16, waiting for transfers between devices, swap(): lax.ppermute(x, 'sec', [(i, i ^ bit) for i in range(lax.axis_size('sec'))])  31 us
    pallas_call x1, Pallas kernels, per_device(): kernel_call(functools.partial(cholesky_kernel, count), [SMEM] + [ANY] * 4...  25.2 us
    all_to_all x1, blocking collectives, per_device(): lax.all_to_all(packed.reshape(owners, capacity, feature_len), 'sec', spli...  21.5 us
    ppermute x16, starting transfers between devices, swap(): lax.ppermute(x, 'sec', [(i, i ^ bit) for i in range(lax.axis_size('sec'))])  11.7 us
    pallas_call x1, Pallas kernels, per_device(): kernel_call(functools.partial(solve_kernel, count, factor), [VMEM] + [ANY...  6.74 us
    all_to_all x1, starting transfers between devices, per_device(): lax.all_to_all(product.reshape(owners, capacity, feature_len), 'sec', spl...  4.52 us
    pallas_call x1, Pallas kernels, per_device(): kernel_call(images_kernel, [SMEM] + [VMEM] * 4, (jax.ShapeDtypeStruct((sl...  3.51 us
    unnamed x10, local copies, waits for them, and re-layouts  3.21 us
  transfers between devices with their start and end apart: 17, of which 11 were waited for; matrix products, arithmetic and copies ran while one was open for 0% of the time, Pallas kernels for 25%

profile of v3, /device:TPU:0, one launch (start us, length us, event | category | flops | bytes accessed | tf_op | source)
XLA Modules:
  0.0 110.6 jit_solution(10914518688394179443)
XLA Ops:
  0.0 0.5 collective-permute-start.1
  0.5 2.1 %shard_map.55 = (s32[1,128]{1,0:T(1,128)}, bf16[256,1024]{1,0:T(8,128)(2,1)}) custom-call(bf16[128,1024]{1,0:T(8,128)(2,1)} %edge_hbm.1, s32[16,16]{1,0:T(8,128)} %joining_hbm.1, s32[1,128]{1,0:T(1,128)} %bitcast.10, s32[1,128]{1,0:T(1,128)} %bitcast.11), custom_call_target="tpu_custom_call" | custom-call | tf_op jit(solution)/shard_map/pallas_call | solution.py:524
  2.6 21.5 %all_to_all.10 = bf16[16,16,1024]{2,1,0:T(8,128)(2,1)S(1)} all-to-all(bf16[16,16,1024]{2,1,0:T(8,128)(2,1)} %bitcast.9), channel_id=1, replica_groups=mesh['runs'=2,'sec'=16] {'sec'}, dimensions={0} | all-to-all | bytes 1048576 | tf_op jit(solution)/shard_map/all_to_all | solution.py:540
  24.1 0.0 collective-permute-start
  24.1 0.0 collective-permute-done.1.other_hbm
  24.1 1.6 %copy-done = bf16[1024,1024]{1,0:T(8,128)(2,1)S(1)} copy-done((bf16[1024,1024]{1,0:T(8,128)(2,1)S(1)}, bf16[1024,1024]{1,0:T(8,128)(2,1)}, u32[]{:S(2)}) %copy-start) | copy-done | bytes 2097176
  25.7 0.3 shard_map.56
  26.0 0.0 collective-permute-done.other_arrived_ref
  26.1 3.5 %shard_map.57 = (f32[256,1024]{1,0:T(8,128)}, f32[2112,128]{1,0:T(8,128)S(1)}) custom-call(s32[1]{0:T(128)} %bitcast.2.core_ref, bf16[256,1024]{1,0:T(8,128)(2,1)S(1)} %bitcast.8, bf16[256,1024]{1,0:T(8,128)(2,1)S(1)} %collective-permute-done.other_arrived_ref, bf16[1024,1024]{1,0:T(8,128)(2,1)S(1)} %get-tuple-element.27.corner_ref, ...), custom_call_target="tpu_custom_call" | custom-call | tf_op jit(solution)/shard_map/pallas_call | solution.py:551
  29.6 1.8 %collective-permute-start.7 = (f32[512,128]{1,0:T(8,128)S(1)}, f32[512,128]{1,0:T(8,128)S(1)}, u32[]{:S(2)}, u32[]{:S(2)}) collective-permute-start(f32[512,128]{1,0:T(8,128)S(1)} %constant_dynamic-slice_fusion.2), channel_id=1, source_target_pairs={{0,4},{1,5},{2,6},{3,7},{4,0},{5,1},{6,2},{7,3},{8,12},{9,13},{10,... | collective-permute-start | bytes 786440 | tf_op jit(solution)/shard_map/ppermute | solution.py:478
  31.5 1.0 collective-permute-start.2
  32.5 5.9 %collective-permute-done.7 = f32[512,128]{1,0:T(8,128)S(1)} collective-permute-done((f32[512,128]{1,0:T(8,128)S(1)}, f32[512,128]{1,0:T(8,128)S(1)}, u32[]{:S(2)}, u32[]{:S(2)}) %collective-permute-start.7) | collective-permute-done | bytes 262176 | tf_op jit(solution)/shard_map/ppermute | solution.py:478
  38.5 0.7 collective-permute-start.8
  39.2 0.7 collective-permute-done.2
  39.9 1.1 %collective-permute-start.3 = (f32[272,128]{1,0:T(8,128)S(1)}, f32[272,128]{1,0:T(8,128)S(1)}, u32[]{:S(2)}, u32[]{:S(2)}) collective-permute-start(f32[272,128]{1,0:T(8,128)S(1)} %constant_dynamic-slice_fusion.4), channel_id=1, source_target_pairs={{0,4},{1,5},{2,6},{3,7},{4,0},{5,1},{6,2},{7,3},{8,12},{9,13},{10,... | collective-permute-start | bytes 417800 | tf_op jit(solution)/shard_map/ppermute | solution.py:478
  41.0 2.6 %collective-permute-done.8 = f32[256,128]{1,0:T(8,128)S(1)} collective-permute-done((f32[256,128]{1,0:T(8,128)S(1)}, f32[256,128]{1,0:T(8,128)S(1)}, u32[]{:S(2)}, u32[]{:S(2)}) %collective-permute-start.8) | collective-permute-done | bytes 131104 | tf_op jit(solution)/shard_map/ppermute | solution.py:478
  43.7 2.3 %collective-permute-start.9 = (f32[128,128]{1,0:T(8,128)S(1)}, f32[128,128]{1,0:T(8,128)S(1)}, u32[]{:S(2)}, u32[]{:S(2)}) collective-permute-start(f32[128,128]{1,0:T(8,128)S(1)} %constant_dynamic-slice_fusion), channel_id=1, source_target_pairs={{0,8},{1,9},{2,10},{3,11},{4,12},{5,13},{6,14},{7,15},{8,0},{9,1},... | collective-permute-start | bytes 196616 | tf_op jit(solution)/shard_map/ppermute | solution.py:478
  46.0 0.0 collective-permute-done.3
  46.1 0.8 collective-permute-start.4
  46.8 5.4 %collective-permute-done.9 = f32[128,128]{1,0:T(8,128)S(1)} collective-permute-done((f32[128,128]{1,0:T(8,128)S(1)}, f32[128,128]{1,0:T(8,128)S(1)}, u32[]{:S(2)}, u32[]{:S(2)}) %collective-permute-start.9) | collective-permute-done | bytes 65568 | tf_op jit(solution)/shard_map/ppermute | solution.py:478
  52.3 0.1 collective-permute-start.10
  52.4 1.4 %collective-permute-done.4 = f32[136,128]{1,0:T(8,128)S(1)} collective-permute-done((f32[136,128]{1,0:T(8,128)S(1)}, f32[136,128]{1,0:T(8,128)S(1)}, u32[]{:S(2)}, u32[]{:S(2)}) %collective-permute-start.4) | collective-permute-done | bytes 69664 | tf_op jit(solution)/shard_map/ppermute | solution.py:478
  53.8 1.6 %collective-permute-start.5 = (f32[136,128]{1,0:T(8,128)S(1)}, f32[136,128]{1,0:T(8,128)S(1)}, u32[]{:S(2)}, u32[]{:S(2)}) collective-permute-start(f32[136,128]{1,0:T(8,128)S(1)} %dynamic-slice_add_fusion.4), channel_id=1, source_target_pairs={{0,8},{1,9},{2,10},{3,11},{4,12},{5,13},{6,14},{7,15},{8,0},{9,1},... | collective-permute-start | bytes 208904 | tf_op jit(solution)/shard_map/ppermute | solution.py:478
  55.4 2.8 %collective-permute-done.10 = f32[128,128]{1,0:T(8,128)S(1)} collective-permute-done((f32[128,128]{1,0:T(8,128)S(1)}, f32[128,128]{1,0:T(8,128)S(1)}, u32[]{:S(2)}, u32[]{:S(2)}) %collective-permute-start.10) | collective-permute-done | bytes 65568 | tf_op jit(solution)/shard_map/ppermute | solution.py:478
  58.2 0.1 collective-permute-start.11
  58.3 1.5 %collective-permute-done.5 = f32[136,128]{1,0:T(8,128)S(1)} collective-permute-done((f32[136,128]{1,0:T(8,128)S(1)}, f32[136,128]{1,0:T(8,128)S(1)}, u32[]{:S(2)}, u32[]{:S(2)}) %collective-permute-start.5) | collective-permute-done | bytes 69664 | tf_op jit(solution)/shard_map/ppermute | solution.py:478
  59.8 0.6 collective-permute-start.6
  60.4 2.8 %collective-permute-done.11 = f32[256,128]{1,0:T(8,128)S(1)} collective-permute-done((f32[256,128]{1,0:T(8,128)S(1)}, f32[256,128]{1,0:T(8,128)S(1)}, u32[]{:S(2)}, u32[]{:S(2)}) %collective-permute-start.11) | collective-permute-done | bytes 131104 | tf_op jit(solution)/shard_map/ppermute | solution.py:478
  63.3 1.7 %collective-permute-done.6 = f32[272,128]{1,0:T(8,128)S(1)} collective-permute-done((f32[272,128]{1,0:T(8,128)S(1)}, f32[272,128]{1,0:T(8,128)S(1)}, u32[]{:S(2)}, u32[]{:S(2)}) %collective-permute-start.6) | collective-permute-done | bytes 139296 | tf_op jit(solution)/shard_map/ppermute | solution.py:478
  65.0 0.6 collective-permute-start.12
  65.5 0.1 collective-permute-start.13
  65.7 5.9 %collective-permute-done.12 = f32[544,128]{1,0:T(8,128)S(1)} collective-permute-done((f32[544,128]{1,0:T(8,128)S(1)}, f32[544,128]{1,0:T(8,128)S(1)}, u32[]{:S(2)}, u32[]{:S(2)}) %collective-permute-start.12) | collective-permute-done | bytes 278560 | tf_op jit(solution)/shard_map/ppermute | solution.py:478
  71.6 0.0 copy-start.1
  71.6 0.1 collective-permute-start.14
  71.7 0.2 collective-permute-done.13
  71.9 0.0 copy-start.2
  72.0 0.4 collective-permute-start.15
  72.3 4.5 %all-to-all-start.1 = ((f32[16,16,1024]{2,1,0:T(8,128)}), f32[16,16,1024]{2,1,0:T(8,128)}, u32[]{:S(2)}, u32[]{:S(2)}) async-start(f32[16,16,1024]{2,1,0:T(8,128)} %bitcast.5), calls=%async_computation.1 | async-start | bytes 2097152 | tf_op jit(solution)/shard_map/all_to_all | solution.py:563
  76.8 0.0 collective-permute-done.15.other1
  76.9 0.0 copy-start.4
  76.9 0.0 collective-permute-done.14.other0
  76.9 0.0 copy-done.1
  76.9 0.0 copy-done.2
  76.9 0.8 copy-done.4
  77.7 0.8 copy-done.3
  78.5 25.2 %shard_map.58 = (bf16[512,1536]{1,0:T(8,128)(2,1)}, bf16[512,1536]{1,0:T(8,128)(2,1)}, bf16[256,768]{1,0:T(8,128)(2,1)}, bf16[256,768]{1,0:T(8,128)(2,1)}, f32[384,128]{1,0:T(8,128)}) custom-call(s32[1]{0:T(128)} %bitcast.2.core_ref, f32[1088,128]{1,0:T(8,128)} %copy-done.1, f32[1024,128]{1,0:T(8,128)} %copy-done.2, f32[1088,128]{1,0:T(8,128)} %copy-done.3, ...), custom_call_target="tpu_custom_call" | custom-call | flops 193273528320 | tf_op jit(solution)/shard_map/pallas_call | solution.py:567
  103.7 0.0 all-to-all-done.1
  103.7 6.7 %shard_map.59 = f32[128,1024]{1,0:T(8,128)} custom-call(s32[1,128]{1,0:T(1,128)} %get-tuple-element.25.slot_ref, f32[384,128]{1,0:T(8,128)} %get-tuple-element.39.tail_hbm, f32[256,1024]{1,0:T(8,128)} %bitcast.6.returned_hbm, bf16[512,1536]{1,0:T(8,128)(2,1)} %get-tuple-element.41.inverse_hbm, bf16[512,1536]{1,0:T(8,128)(2,1)} %get-tuple-element.42.across_hbm, ...), custom_call_target="tpu_custom_call" | custom-call | tf_op jit(solution)/shard_map/pallas_call | solution.py:592
  (22 shorter events, 0.4 us)
Async XLA Ops:
  0.0 24.1 %collective-permute-start.1 = (bf16[1024,1024]{1,0:T(8,128)(2,1)}, bf16[1024,1024]{1,0:T(8,128)(2,1)S(1)}, u32[]{:S(2)}, u32[]{:S(2)}) collective-permute-start(bf16[1024,1024]{1,0:T(8,128)(2,1)} %mine_hbm.1), channel_id=1, source_target_pairs={{0,1},{1,0},{2,3},{3,2},{4,5},{5,4},{6,7},{7,6},{8,9},{9,8},{10,11... | collective-permute-start | bytes 6291464 | tf_op jit(solution)/shard_map/ppermute | solution.py:478
  24.1 1.9 %collective-permute-start = (bf16[256,1024]{1,0:T(8,128)(2,1)S(1)}, bf16[256,1024]{1,0:T(8,128)(2,1)S(1)}, u32[]{:S(2)}, u32[]{:S(2)}) collective-permute-start(bf16[256,1024]{1,0:T(8,128)(2,1)S(1)} %bitcast.7), channel_id=1, source_target_pairs={{0,1},{1,0},{2,3},{3,2},{4,5},{5,4},{6,7},{7,6},{8,9},{9,8},{10,11... | collective-permute-start | bytes 1572872 | tf_op jit(solution)/shard_map/ppermute | solution.py:478
  24.1 1.6 %copy-start = (bf16[1024,1024]{1,0:T(8,128)(2,1)S(1)}, bf16[1024,1024]{1,0:T(8,128)(2,1)}, u32[]{:S(2)}) copy-start(bf16[1024,1024]{1,0:T(8,128)(2,1)} %mine_hbm.1) | copy-start | bytes 6291460
  29.6 8.8 %collective-permute-start.7 = (f32[512,128]{1,0:T(8,128)S(1)}, f32[512,128]{1,0:T(8,128)S(1)}, u32[]{:S(2)}, u32[]{:S(2)}) collective-permute-start(f32[512,128]{1,0:T(8,128)S(1)} %constant_dynamic-slice_fusion.2), channel_id=1, source_target_pairs={{0,4},{1,5},{2,6},{3,7},{4,0},{5,1},{6,2},{7,3},{8,12},{9,13},{10,... | collective-permute-start | bytes 786440 | tf_op jit(solution)/shard_map/ppermute | solution.py:478
  31.5 8.3 %collective-permute-start.2 = (f32[544,128]{1,0:T(8,128)S(1)}, f32[544,128]{1,0:T(8,128)S(1)}, u32[]{:S(2)}, u32[]{:S(2)}) collective-permute-start(f32[544,128]{1,0:T(8,128)S(1)} %constant_dynamic-slice_fusion.5), channel_id=1, source_target_pairs={{0,2},{1,3},{2,0},{3,1},{4,6},{5,7},{6,4},{7,5},{8,10},{9,11},{10,... | collective-permute-start | bytes 835592 | tf_op jit(solution)/shard_map/ppermute | solution.py:478
  38.5 5.2 %collective-permute-start.8 = (f32[256,128]{1,0:T(8,128)S(1)}, f32[256,128]{1,0:T(8,128)S(1)}, u32[]{:S(2)}, u32[]{:S(2)}) collective-permute-start(f32[256,128]{1,0:T(8,128)S(1)} %constant_dynamic-slice_fusion.1), channel_id=1, source_target_pairs={{0,2},{1,3},{2,0},{3,1},{4,6},{5,7},{6,4},{7,5},{8,10},{9,11},{10,... | collective-permute-start | bytes 393224 | tf_op jit(solution)/shard_map/ppermute | solution.py:478
  39.9 6.1 %collective-permute-start.3 = (f32[272,128]{1,0:T(8,128)S(1)}, f32[272,128]{1,0:T(8,128)S(1)}, u32[]{:S(2)}, u32[]{:S(2)}) collective-permute-start(f32[272,128]{1,0:T(8,128)S(1)} %constant_dynamic-slice_fusion.4), channel_id=1, source_target_pairs={{0,4},{1,5},{2,6},{3,7},{4,0},{5,1},{6,2},{7,3},{8,12},{9,13},{10,... | collective-permute-start | bytes 417800 | tf_op jit(solution)/shard_map/ppermute | solution.py:478
  43.7 8.6 %collective-permute-start.9 = (f32[128,128]{1,0:T(8,128)S(1)}, f32[128,128]{1,0:T(8,128)S(1)}, u32[]{:S(2)}, u32[]{:S(2)}) collective-permute-start(f32[128,128]{1,0:T(8,128)S(1)} %constant_dynamic-slice_fusion), channel_id=1, source_target_pairs={{0,8},{1,9},{2,10},{3,11},{4,12},{5,13},{6,14},{7,15},{8,0},{9,1},... | collective-permute-start | bytes 196616 | tf_op jit(solution)/shard_map/ppermute | solution.py:478
  46.1 7.7 %collective-permute-start.4 = (f32[136,128]{1,0:T(8,128)S(1)}, f32[136,128]{1,0:T(8,128)S(1)}, u32[]{:S(2)}, u32[]{:S(2)}) collective-permute-start(f32[136,128]{1,0:T(8,128)S(1)} %constant_dynamic-slice_fusion.3), channel_id=1, source_target_pairs={{0,8},{1,9},{2,10},{3,11},{4,12},{5,13},{6,14},{7,15},{8,0},{9,1},... | collective-permute-start | bytes 208904 | tf_op jit(solution)/shard_map/ppermute | solution.py:478
  52.3 5.9 %collective-permute-start.10 = (f32[128,128]{1,0:T(8,128)S(1)}, f32[128,128]{1,0:T(8,128)S(1)}, u32[]{:S(2)}, u32[]{:S(2)}) collective-permute-start(f32[128,128]{1,0:T(8,128)S(1)} %dynamic-slice_add_fusion.5), channel_id=1, source_target_pairs={{0,8},{1,9},{2,10},{3,11},{4,12},{5,13},{6,14},{7,15},{8,0},{9,1},... | collective-permute-start | bytes 196616 | tf_op jit(solution)/shard_map/ppermute | solution.py:478
  53.8 6.0 %collective-permute-start.5 = (f32[136,128]{1,0:T(8,128)S(1)}, f32[136,128]{1,0:T(8,128)S(1)}, u32[]{:S(2)}, u32[]{:S(2)}) collective-permute-start(f32[136,128]{1,0:T(8,128)S(1)} %dynamic-slice_add_fusion.4), channel_id=1, source_target_pairs={{0,8},{1,9},{2,10},{3,11},{4,12},{5,13},{6,14},{7,15},{8,0},{9,1},... | collective-permute-start | bytes 208904 | tf_op jit(solution)/shard_map/ppermute | solution.py:478
  58.2 5.0 %collective-permute-start.11 = (f32[256,128]{1,0:T(8,128)S(1)}, f32[256,128]{1,0:T(8,128)S(1)}, u32[]{:S(2)}, u32[]{:S(2)}) collective-permute-start(f32[256,128]{1,0:T(8,128)S(1)} %maximum_select_fusion.5), channel_id=1, source_target_pairs={{0,2},{1,3},{2,0},{3,1},{4,6},{5,7},{6,4},{7,5},{8,10},{9,11},{10,... | collective-permute-start | bytes 393224 | tf_op jit(solution)/shard_map/ppermute | solution.py:478
  59.8 5.1 %collective-permute-start.6 = (f32[272,128]{1,0:T(8,128)S(1)}, f32[272,128]{1,0:T(8,128)S(1)}, u32[]{:S(2)}, u32[]{:S(2)}) collective-permute-start(f32[272,128]{1,0:T(8,128)S(1)} %maximum_select_fusion.4), channel_id=1, source_target_pairs={{0,4},{1,5},{2,6},{3,7},{4,0},{5,1},{6,2},{7,3},{8,12},{9,13},{10,... | collective-permute-start | bytes 417800 | tf_op jit(solution)/shard_map/ppermute | solution.py:478
  65.0 6.6 %collective-permute-start.12 = (f32[544,128]{1,0:T(8,128)S(1)}, f32[544,128]{1,0:T(8,128)S(1)}, u32[]{:S(2)}, u32[]{:S(2)}) collective-permute-start(f32[544,128]{1,0:T(8,128)S(1)} %maximum_select_fusion.2), channel_id=1, source_target_pairs={{0,2},{1,3},{2,0},{3,1},{4,6},{5,7},{6,4},{7,5},{8,10},{9,11},{10,... | collective-permute-start | bytes 835592 | tf_op jit(solution)/shard_map/ppermute | solution.py:478
  65.5 6.4 %collective-permute-start.13 = (f32[512,128]{1,0:T(8,128)S(1)}, f32[512,128]{1,0:T(8,128)S(1)}, u32[]{:S(2)}, u32[]{:S(2)}) collective-permute-start(f32[512,128]{1,0:T(8,128)S(1)} %maximum_select_fusion.3), channel_id=1, source_target_pairs={{0,4},{1,5},{2,6},{3,7},{4,0},{5,1},{6,2},{7,3},{8,12},{9,13},{10,... | collective-permute-start | bytes 786440 | tf_op jit(solution)/shard_map/ppermute | solution.py:478
  71.6 5.3 %copy-start.1 = (f32[1088,128]{1,0:T(8,128)}, f32[1088,128]{1,0:T(8,128)S(1)}, u32[]{:S(2)}) copy-start(f32[1088,128]{1,0:T(8,128)S(1)} %maximum_select_fusion.mine0) | copy-start | bytes 1671172
  71.6 5.2 %collective-permute-start.14 = (f32[1088,128]{1,0:T(8,128)S(1)}, f32[1088,128]{1,0:T(8,128)S(1)}, u32[]{:S(2)}, u32[]{:S(2)}) collective-permute-start(f32[1088,128]{1,0:T(8,128)S(1)} %maximum_select_fusion.mine0), channel_id=1, source_target_pairs={{0,1},{1,0},{2,3},{3,2},{4,5},{5,4},{6,7},{7,6},{8,9},{9,8},{10,11... | collective-permute-start | bytes 1671176 | tf_op jit(solution)/shard_map/ppermute | solution.py:478
  71.9 4.9 %copy-start.2 = (f32[1024,128]{1,0:T(8,128)}, f32[1024,128]{1,0:T(8,128)S(1)}, u32[]{:S(2)}) copy-start(f32[1024,128]{1,0:T(8,128)S(1)} %maximum_select_fusion.1.mine1) | copy-start | bytes 1572868
  72.0 4.9 %collective-permute-start.15 = (f32[1024,128]{1,0:T(8,128)S(1)}, f32[1024,128]{1,0:T(8,128)S(1)}, u32[]{:S(2)}, u32[]{:S(2)}) collective-permute-start(f32[1024,128]{1,0:T(8,128)S(1)} %maximum_select_fusion.1.mine1), channel_id=1, source_target_pairs={{0,1},{1,0},{2,3},{3,2},{4,5},{5,4},{6,7},{7,6},{8,9},{9,8},{10,11... | collective-permute-start | bytes 1572872 | tf_op jit(solution)/shard_map/ppermute | solution.py:478
  72.3 31.4 %all-to-all-start.1 = ((f32[16,16,1024]{2,1,0:T(8,128)}), f32[16,16,1024]{2,1,0:T(8,128)}, u32[]{:S(2)}, u32[]{:S(2)}) async-start(f32[16,16,1024]{2,1,0:T(8,128)} %bitcast.5), calls=%async_computation.1 | async-start | bytes 2097152 | tf_op jit(solution)/shard_map/all_to_all | solution.py:563
  76.9 0.8 copy-start.4
  77.7 0.8 copy-start.3

commit v4 on v3

--- a/solution.py
+++ b/solution.py
@@ -9,6 +9,7 @@
 from jax.sharding import PartitionSpec as P
 
 SIDE = 128
+LARGE = 32 << 20
 
 
 def column_offsets(count):
@@ -118,7 +119,10 @@
     images = dot_nn(arrived_ref[...], corner_ref[...])
     images_ref[...] = images
     images = jnp.concatenate([images, others], axis=0)
-    first, second = left(images, 0), right(images, 0)
+    high, low = split(images)
+    second = jnp.concatenate([high, low, high], axis=0)
+    high, low = high.T, low.T
+    first = jnp.concatenate([high, high, low], axis=1)
     row, col = iota((SIDE, SIDE), 0), iota((SIDE, SIDE), 1)
 
     def store(at, x):
@@ -129,7 +133,7 @@
         diagonals = []
         for p in pairs:
             start = 2 * p * SIDE
-            part = dot_tn(first[:, start:], second[:, start : start + 2 * SIDE])
+            part = dot_nn(first[start:], second[:, start : start + 2 * SIDE])
             upper, lower = part[:SIDE, :SIDE], part[SIDE : 2 * SIDE, SIDE:]
             store(at, jnp.where(row >= col, upper, lower))
             store(at + SIDE, part[SIDE : 2 * SIDE, :SIDE])
@@ -196,6 +200,9 @@
         )
 
 
+NEAR = 2
+
+
 def eliminate(rows, start, tick):
     shape = rows[0].shape
     lane, sub = iota(shape, 1), iota(shape, 0)
@@ -211,20 +218,23 @@
     pivots = columns_of(rows[0], start)
     for m in range(groups):
         g = start + 8 * m
-        later = range(m + 1, groups)
+        later = range(m + 1, min(groups, m + 1 + NEAR))
+        far = range(m + 1 + NEAR, groups)
         inside = (lane >= g) & (lane < g + 8)
         current = rows[m]
         ahead, ahead_below = [], []
         if later:
             ahead = columns_of(current, g + 8)
             ahead_below = columns_of(rows[m + 1], g + 8)
-        below = {r: columns_of(rows[r], g) for r in later}
+        below = {r: columns_of(rows[r], g) for r in range(m + 1, groups)}
         current = jnp.where(inside, (lane - g == sub).astype(jnp.float32), current)
-        for r in later:
+        for r in range(m + 1, groups):
             rows[r] = jnp.where(inside, 0.0, rows[r])
         diagonal = pivots[0]
+        inverses = []
         for j in range(8):
             inverse = 1.0 / spread(pivots[j][j : j + 1, :])
+            inverses.append(inverse)
             pivot_row = spread(current[j : j + 1, :])
             heads = [spread(x[j : j + 1, :]) for x in pivots[j + 1 :]]
             ahead_heads = [spread(x[j : j + 1, :]) for x in ahead]
@@ -244,6 +254,14 @@
                 if r == m + 1:
                     ahead_below = [x - weight * head for x, head in zip(ahead_below, ahead_heads)]
         rows[m] = current * lax.rsqrt(diagonal)
+        for j in reversed(range(8)):
+            if not far:
+                break
+            solved = spread(current[j : j + 1, :]) * inverses[j]
+            if j:
+                current = current - jnp.where(sub < j, pivots[j], 0.0) * solved
+            for r in far:
+                rows[r] = rows[r] - below[r][j] * solved
         pivots = ahead_below
         tick()
     return rows
@@ -285,8 +303,18 @@
     )
 
 
+def form_slices(count, forms_ref):
+    half, quarter = count // 2 * SIDE, count // 4 * SIDE
+    return [
+        forms_ref.at[:half],
+        forms_ref.at[half : 2 * half],
+        forms_ref.at[2 * half : 2 * half + quarter, : 3 * quarter],
+        forms_ref.at[2 * half : 2 * half + quarter, 3 * quarter :],
+    ]
+
+
 def cholesky_kernel(
-    count, core_ref, mine0, mine1, other0, other1, inverse_hbm, across_hbm, next_hbm, beyond_hbm, tail_hbm,
+    count, core_ref, mine0, mine1, other0, other1, forms_hbm, tail_hbm,
     lower_ref, diagonal_ref, inverse_ref, across_ref, next_ref, beyond_ref, done, out_done,
 ):
     offsets = column_offsets(count)
@@ -324,6 +352,7 @@
 
     inverses = {}
     outward = []
+    form_refs = form_slices(count, forms_hbm)
 
     def send(ref, hbm):
         outward.append(pltpu.make_async_copy(ref, hbm, out_done.at[len(outward)]))
@@ -341,17 +370,17 @@
         inverse_ref[...] = right(
             join_inverses(inverses[0], blocks(range(2, 4), range(2)), inverses[2]), 1
         )
-        send(inverse_ref, inverse_hbm)
+        send(inverse_ref, form_refs[0])
 
     def across():
         across_ref[...] = right(blocks(range(half, count), range(half)), 1)
-        send(across_ref, across_hbm)
+        send(across_ref, form_refs[1])
 
     def beyond():
         next_ref[...] = right(inverses[half], 1)
         beyond_ref[...] = right(blocks(range(three, count), range(half, three)), 1)
-        send(next_ref, next_hbm)
-        send(beyond_ref, beyond_hbm)
+        send(next_ref, form_refs[2])
+        send(beyond_ref, form_refs[3])
 
     extra = {2: [pair(0)], 4: [pair(2), join_half, across], 6: [pair(half), beyond]}
 
@@ -400,24 +429,18 @@
         lower_ref[at(k + 1, k), :] = head
         lower_ref[at(k + 1, k + 1), :] -= dot_nt(left(head, 1), right(head, 1))
         beside = rest_of(k, head)
-    send(lower_ref.at[offsets[count - 2] :], tail_hbm)
+    send(lower_ref.at[offsets[count - 2] :], tail_hbm.at[: 3 * SIDE])
     for copy in outward:
         copy.wait()
 
 
 def solve_kernel(
-    count, factor, slot_ref, tail_hbm, returned_hbm, inverse_hbm, across_hbm, next_hbm, beyond_hbm, out_ref,
+    count, factor, slot_ref, tail_hbm, returned_hbm, forms_hbm, out_ref,
     tail_ref, returned_ref, inverse_ref, across_ref, next_ref, beyond_ref, done,
 ):
     half, three = count // 2 * SIDE, 3 * count // 4 * SIDE
-    pairs = [
-        (tail_hbm, tail_ref),
-        (returned_hbm, returned_ref),
-        (inverse_hbm, inverse_ref),
-        (across_hbm, across_ref),
-        (next_hbm, next_ref),
-        (beyond_hbm, beyond_ref),
-    ]
+    pairs = [(tail_hbm.at[: 3 * SIDE], tail_ref), (returned_hbm, returned_ref)]
+    pairs += zip(form_slices(count, forms_hbm), (inverse_ref, across_ref, next_ref, beyond_ref))
     copies = [pltpu.make_async_copy(a, b, done.at[i]) for i, (a, b) in enumerate(pairs)]
     for copy in copies:
         copy.start()
@@ -432,7 +455,17 @@
         rest[0] = dot_tn(placed, high) + dot_tn(placed, low)
 
     def solved(first, last, inverse):
-        x = dot_nt(left(rest[first][:, : last - first], 1), inverse)
+        source = left(rest[first][:, : last - first], 1)
+        if last - first == half:
+            cut = half // 2
+            short = [slice(i * half, i * half + cut) for i in range(3)]
+            begin = dot_nt(
+                jnp.concatenate([source[:, i] for i in short], axis=1),
+                jnp.concatenate([inverse[:cut, i] for i in short], axis=1),
+            )
+            x = jnp.concatenate([begin, dot_nt(source, inverse[cut:])], axis=1)
+        else:
+            x = dot_nt(source, inverse)
         out_ref[:, first:last] = x * factor
         rest[last] = left(x, 1)
 
@@ -568,11 +601,8 @@
         functools.partial(cholesky_kernel, count),
         [SMEM] + [ANY] * 4,
         (
-            jax.ShapeDtypeStruct((half, 3 * half), jnp.bfloat16),
-            jax.ShapeDtypeStruct((half, 3 * half), jnp.bfloat16),
-            jax.ShapeDtypeStruct((quarter, 3 * quarter), jnp.bfloat16),
-            jax.ShapeDtypeStruct((quarter, 3 * quarter), jnp.bfloat16),
-            jax.ShapeDtypeStruct((3 * SIDE, SIDE), f32),
+            jax.ShapeDtypeStruct((LARGE // 6 // half, 3 * half), jnp.bfloat16),
+            jax.ShapeDtypeStruct((LARGE // 4 // SIDE, SIDE), f32),
         ),
         [
             pltpu.VMEM((packed_rows, SIDE), f32),
@@ -584,14 +614,14 @@
             dma((2, 8)),
             dma((5,)),
         ],
-        (ANY,) * 5,
-        mib=60,
+        (ANY,) * 2,
+        mib=44,
         work=20 * packed_rows * feature_len * feature_len,
     )(core, *parts, *[swap(part, 1) for part in parts])
     returned, lower = lax.optimization_barrier((returned, lower))
     return kernel_call(
         functools.partial(solve_kernel, count, factor),
-        [VMEM] + [ANY] * 6,
+        [VMEM] + [ANY] * 3,
         jax.ShapeDtypeStruct((row_count, feature_len), f32),
         [
             pltpu.VMEM((3 * SIDE, SIDE), f32),
@@ -603,7 +633,7 @@
             dma((6,)),
         ],
         mib=60,
-    )(slot, lower[4], returned.reshape(slots, feature_len), *lower[:4])
+    )(slot, lower[1], returned.reshape(slots, feature_len), lower[0])
 
 
 def solution(mesh):

time: 111 us -> 110 us (level)
  local copies, waits for them, and re-layouts: 3.4 us -> 1.78 us
    unnamed x10 -> x2, local copies, waits for them, and re-layouts: 3.21 us -> 1.59 us
  transfers between devices with their start and end apart: 17 -> 17, of which waited for: 11 -> 11; matrix products, arithmetic and copies ran while one was open for 0% -> 0% of each run, Pallas kernels for 25% -> 26%
where the time goes in v4:
time: 110 us
  Pallas kernels  38.8 us (35%)
  waiting for transfers between devices  30.9 us (28%)
  blocking collectives  21.5 us (20%)
  starting transfers between devices  16 us (15%)
  local copies, waits for them, and re-layouts  1.78 us (2%)
    ppermute x16, waiting for transfers between devices, swap(): lax.ppermute(x, 'sec', [(i, i ^ bit) for i in range(lax.axis_size('sec'))])  30.9 us
    pallas_call x1, Pallas kernels, per_device(): kernel_call(functools.partial(cholesky_kernel, count), [SMEM] + [ANY] * 4...  26.2 us
    all_to_all x1, blocking collectives, per_device(): lax.all_to_all(packed.reshape(owners, capacity, feature_len), 'sec', spli...  21.5 us
    ppermute x16, starting transfers between devices, swap(): lax.ppermute(x, 'sec', [(i, i ^ bit) for i in range(lax.axis_size('sec'))])  11.7 us
    pallas_call x1, Pallas kernels, per_device(): kernel_call(functools.partial(solve_kernel, count, factor), [VMEM] + [ANY...  6.54 us
    all_to_all x1, starting transfers between devices, per_device(): lax.all_to_all(product.reshape(owners, capacity, feature_len), 'sec', spl...  4.34 us
    pallas_call x1, Pallas kernels, per_device(): kernel_call(images_kernel, [SMEM] + [VMEM] * 4, (jax.ShapeDtypeStruct((sl...  3.61 us
  transfers between devices with their start and end apart: 17, of which 11 were waited for; matrix products, arithmetic and copies ran while one was open for 0% of the time, Pallas kernels for 26%

profile of v4, /device:TPU:0, one launch (start us, length us, event | category | flops | bytes accessed | tf_op | source)
XLA Modules:
  0.0 109.7 jit_solution(6424833173552224935)
XLA Ops:
  0.0 0.5 collective-permute-start.1
  0.5 2.1 %shard_map.55 = (s32[1,128]{1,0:T(1,128)}, bf16[256,1024]{1,0:T(8,128)(2,1)}) custom-call(bf16[128,1024]{1,0:T(8,128)(2,1)} %edge_hbm.1, s32[16,16]{1,0:T(8,128)} %joining_hbm.1, s32[1,128]{1,0:T(1,128)} %bitcast.10, s32[1,128]{1,0:T(1,128)} %bitcast.11), custom_call_target="tpu_custom_call" | custom-call | tf_op jit(solution)/shard_map/pallas_call | solution.py:557
  2.6 21.5 %all_to_all.10 = bf16[16,16,1024]{2,1,0:T(8,128)(2,1)S(1)} all-to-all(bf16[16,16,1024]{2,1,0:T(8,128)(2,1)} %bitcast.9), channel_id=1, replica_groups=mesh['runs'=2,'sec'=16] {'sec'}, dimensions={0} | all-to-all | bytes 1048576 | tf_op jit(solution)/shard_map/all_to_all | solution.py:573
  24.1 0.0 collective-permute-start
  24.1 0.0 collective-permute-done.1.other_hbm
  24.1 0.0 copy-start
  24.1 1.6 %copy-done = bf16[1024,1024]{1,0:T(8,128)(2,1)S(1)} copy-done((bf16[1024,1024]{1,0:T(8,128)(2,1)S(1)}, bf16[1024,1024]{1,0:T(8,128)(2,1)}, u32[]{:S(2)}) %copy-start) | copy-done | bytes 2097176
  25.7 0.3 shard_map.56
  26.0 0.0 collective-permute-done.other_arrived_ref
  26.1 3.6 %shard_map.57 = (f32[256,1024]{1,0:T(8,128)}, f32[2112,128]{1,0:T(8,128)S(1)}) custom-call(s32[1]{0:T(128)} %bitcast.2.core_ref, bf16[256,1024]{1,0:T(8,128)(2,1)S(1)} %bitcast.8, bf16[256,1024]{1,0:T(8,128)(2,1)S(1)} %collective-permute-done.other_arrived_ref, bf16[1024,1024]{1,0:T(8,128)(2,1)S(1)} %get-tuple-element.21.corner_ref, ...), custom_call_target="tpu_custom_call" | custom-call | tf_op jit(solution)/shard_map/pallas_call | solution.py:584
  29.7 1.8 %collective-permute-start.7 = (f32[512,128]{1,0:T(8,128)S(1)}, f32[512,128]{1,0:T(8,128)S(1)}, u32[]{:S(2)}, u32[]{:S(2)}) collective-permute-start(f32[512,128]{1,0:T(8,128)S(1)} %constant_dynamic-slice_fusion.2), channel_id=1, source_target_pairs={{0,4},{1,5},{2,6},{3,7},{4,0},{5,1},{6,2},{7,3},{8,12},{9,13},{10,... | collective-permute-start | bytes 786440 | tf_op jit(solution)/shard_map/ppermute | solution.py:511
  31.6 1.0 collective-permute-start.2
  32.6 5.9 %collective-permute-done.7 = f32[512,128]{1,0:T(8,128)S(1)} collective-permute-done((f32[512,128]{1,0:T(8,128)S(1)}, f32[512,128]{1,0:T(8,128)S(1)}, u32[]{:S(2)}, u32[]{:S(2)}) %collective-permute-start.7) | collective-permute-done | bytes 262176 | tf_op jit(solution)/shard_map/ppermute | solution.py:511
  38.6 0.7 collective-permute-start.8
  39.3 0.7 collective-permute-done.2
  40.0 1.1 %collective-permute-start.3 = (f32[272,128]{1,0:T(8,128)S(1)}, f32[272,128]{1,0:T(8,128)S(1)}, u32[]{:S(2)}, u32[]{:S(2)}) collective-permute-start(f32[272,128]{1,0:T(8,128)S(1)} %constant_dynamic-slice_fusion.4), channel_id=1, source_target_pairs={{0,4},{1,5},{2,6},{3,7},{4,0},{5,1},{6,2},{7,3},{8,12},{9,13},{10,... | collective-permute-start | bytes 417800 | tf_op jit(solution)/shard_map/ppermute | solution.py:511
  41.1 2.6 %collective-permute-done.8 = f32[256,128]{1,0:T(8,128)S(1)} collective-permute-done((f32[256,128]{1,0:T(8,128)S(1)}, f32[256,128]{1,0:T(8,128)S(1)}, u32[]{:S(2)}, u32[]{:S(2)}) %collective-permute-start.8) | collective-permute-done | bytes 131104 | tf_op jit(solution)/shard_map/ppermute | solution.py:511
  43.8 2.3 %collective-permute-start.9 = (f32[128,128]{1,0:T(8,128)S(1)}, f32[128,128]{1,0:T(8,128)S(1)}, u32[]{:S(2)}, u32[]{:S(2)}) collective-permute-start(f32[128,128]{1,0:T(8,128)S(1)} %constant_dynamic-slice_fusion), channel_id=1, source_target_pairs={{0,8},{1,9},{2,10},{3,11},{4,12},{5,13},{6,14},{7,15},{8,0},{9,1},... | collective-permute-start | bytes 196616 | tf_op jit(solution)/shard_map/ppermute | solution.py:511
  46.1 0.0 collective-permute-done.3
  46.1 0.8 collective-permute-start.4
  46.9 5.4 %collective-permute-done.9 = f32[128,128]{1,0:T(8,128)S(1)} collective-permute-done((f32[128,128]{1,0:T(8,128)S(1)}, f32[128,128]{1,0:T(8,128)S(1)}, u32[]{:S(2)}, u32[]{:S(2)}) %collective-permute-start.9) | collective-permute-done | bytes 65568 | tf_op jit(solution)/shard_map/ppermute | solution.py:511
  52.4 0.1 collective-permute-start.10
  52.4 1.4 %collective-permute-done.4 = f32[136,128]{1,0:T(8,128)S(1)} collective-permute-done((f32[136,128]{1,0:T(8,128)S(1)}, f32[136,128]{1,0:T(8,128)S(1)}, u32[]{:S(2)}, u32[]{:S(2)}) %collective-permute-start.4) | collective-permute-done | bytes 69664 | tf_op jit(solution)/shard_map/ppermute | solution.py:511
  53.9 1.6 %collective-permute-start.5 = (f32[136,128]{1,0:T(8,128)S(1)}, f32[136,128]{1,0:T(8,128)S(1)}, u32[]{:S(2)}, u32[]{:S(2)}) collective-permute-start(f32[136,128]{1,0:T(8,128)S(1)} %dynamic-slice_add_fusion.4), channel_id=1, source_target_pairs={{0,8},{1,9},{2,10},{3,11},{4,12},{5,13},{6,14},{7,15},{8,0},{9,1},... | collective-permute-start | bytes 208904 | tf_op jit(solution)/shard_map/ppermute | solution.py:511
  55.4 2.8 %collective-permute-done.10 = f32[128,128]{1,0:T(8,128)S(1)} collective-permute-done((f32[128,128]{1,0:T(8,128)S(1)}, f32[128,128]{1,0:T(8,128)S(1)}, u32[]{:S(2)}, u32[]{:S(2)}) %collective-permute-start.10) | collective-permute-done | bytes 65568 | tf_op jit(solution)/shard_map/ppermute | solution.py:511
  58.3 0.1 collective-permute-start.11
  58.4 1.5 %collective-permute-done.5 = f32[136,128]{1,0:T(8,128)S(1)} collective-permute-done((f32[136,128]{1,0:T(8,128)S(1)}, f32[136,128]{1,0:T(8,128)S(1)}, u32[]{:S(2)}, u32[]{:S(2)}) %collective-permute-start.5) | collective-permute-done | bytes 69664 | tf_op jit(solution)/shard_map/ppermute | solution.py:511
  59.9 0.6 collective-permute-start.6
  60.5 2.8 %collective-permute-done.11 = f32[256,128]{1,0:T(8,128)S(1)} collective-permute-done((f32[256,128]{1,0:T(8,128)S(1)}, f32[256,128]{1,0:T(8,128)S(1)}, u32[]{:S(2)}, u32[]{:S(2)}) %collective-permute-start.11) | collective-permute-done | bytes 131104 | tf_op jit(solution)/shard_map/ppermute | solution.py:511
  63.3 1.7 %collective-permute-done.6 = f32[272,128]{1,0:T(8,128)S(1)} collective-permute-done((f32[272,128]{1,0:T(8,128)S(1)}, f32[272,128]{1,0:T(8,128)S(1)}, u32[]{:S(2)}, u32[]{:S(2)}) %collective-permute-start.6) | collective-permute-done | bytes 139296 | tf_op jit(solution)/shard_map/ppermute | solution.py:511
  65.0 0.6 collective-permute-start.12
  65.6 0.1 collective-permute-start.13
  65.7 5.9 %collective-permute-done.12 = f32[544,128]{1,0:T(8,128)S(1)} collective-permute-done((f32[544,128]{1,0:T(8,128)S(1)}, f32[544,128]{1,0:T(8,128)S(1)}, u32[]{:S(2)}, u32[]{:S(2)}) %collective-permute-start.12) | collective-permute-done | bytes 278560 | tf_op jit(solution)/shard_map/ppermute | solution.py:511
  71.7 0.1 collective-permute-start.14
  71.8 0.2 collective-permute-done.13
  72.0 0.4 collective-permute-start.15
  72.4 4.3 %all-to-all-start.1 = ((f32[16,16,1024]{2,1,0:T(8,128)}), f32[16,16,1024]{2,1,0:T(8,128)}, u32[]{:S(2)}, u32[]{:S(2)}) async-start(f32[16,16,1024]{2,1,0:T(8,128)} %bitcast.5), calls=%async_computation.1 | async-start | bytes 2097152 | tf_op jit(solution)/shard_map/all_to_all | solution.py:596
  76.7 0.0 collective-permute-done.15.other1
  76.7 0.0 collective-permute-done.14.other0
  76.7 26.2 %shard_map.58 = (bf16[10922,1536]{1,0:T(8,128)(2,1)}, f32[65536,128]{1,0:T(8,128)}) custom-call(s32[1]{0:T(128)} %bitcast.2.core_ref, f32[1088,128]{1,0:T(8,128)S(1)} %maximum_select_fusion.mine0, f32[1024,128]{1,0:T(8,128)S(1)} %maximum_select_fusion.1.mine1, f32[1088,128]{1,0:T(8,128)S(1)} %collective-permute-done.14.other0, ...), custom_call_target="tpu_custom_call" | custom-call | flops 193273528320 | tf_op jit(solution)/shard_map/pallas_call | solution.py:600
  102.9 0.0 all-to-all-done.1
  102.9 6.5 %shard_map.59 = f32[128,1024]{1,0:T(8,128)} custom-call(s32[1,128]{1,0:T(1,128)} %get-tuple-element.19.slot_ref, f32[65536,128]{1,0:T(8,128)} %get-tuple-element.30.tail_hbm, f32[256,1024]{1,0:T(8,128)} %bitcast.6.returned_hbm, bf16[10922,1536]{1,0:T(8,128)(2,1)} %get-tuple-element.32.forms_hbm), custom_call_target="tpu_custom_call" | custom-call | tf_op jit(solution)/shard_map/pallas_call | solution.py:622
  (20 shorter events, 0.4 us)
Async XLA Ops:
  0.0 24.1 %collective-permute-start.1 = (bf16[1024,1024]{1,0:T(8,128)(2,1)}, bf16[1024,1024]{1,0:T(8,128)(2,1)S(1)}, u32[]{:S(2)}, u32[]{:S(2)}) collective-permute-start(bf16[1024,1024]{1,0:T(8,128)(2,1)} %mine_hbm.1), channel_id=1, source_target_pairs={{0,1},{1,0},{2,3},{3,2},{4,5},{5,4},{6,7},{7,6},{8,9},{9,8},{10,11... | collective-permute-start | bytes 6291464 | tf_op jit(solution)/shard_map/ppermute | solution.py:511
  24.1 1.9 %collective-permute-start = (bf16[256,1024]{1,0:T(8,128)(2,1)S(1)}, bf16[256,1024]{1,0:T(8,128)(2,1)S(1)}, u32[]{:S(2)}, u32[]{:S(2)}) collective-permute-start(bf16[256,1024]{1,0:T(8,128)(2,1)S(1)} %bitcast.7), channel_id=1, source_target_pairs={{0,1},{1,0},{2,3},{3,2},{4,5},{5,4},{6,7},{7,6},{8,9},{9,8},{10,11... | collective-permute-start | bytes 1572872 | tf_op jit(solution)/shard_map/ppermute | solution.py:511
  24.1 1.6 %copy-start = (bf16[1024,1024]{1,0:T(8,128)(2,1)S(1)}, bf16[1024,1024]{1,0:T(8,128)(2,1)}, u32[]{:S(2)}) copy-start(bf16[1024,1024]{1,0:T(8,128)(2,1)} %mine_hbm.1) | copy-start | bytes 6291460
  29.7 8.8 %collective-permute-start.7 = (f32[512,128]{1,0:T(8,128)S(1)}, f32[512,128]{1,0:T(8,128)S(1)}, u32[]{:S(2)}, u32[]{:S(2)}) collective-permute-start(f32[512,128]{1,0:T(8,128)S(1)} %constant_dynamic-slice_fusion.2), channel_id=1, source_target_pairs={{0,4},{1,5},{2,6},{3,7},{4,0},{5,1},{6,2},{7,3},{8,12},{9,13},{10,... | collective-permute-start | bytes 786440 | tf_op jit(solution)/shard_map/ppermute | solution.py:511
  31.6 8.3 %collective-permute-start.2 = (f32[544,128]{1,0:T(8,128)S(1)}, f32[544,128]{1,0:T(8,128)S(1)}, u32[]{:S(2)}, u32[]{:S(2)}) collective-permute-start(f32[544,128]{1,0:T(8,128)S(1)} %constant_dynamic-slice_fusion.5), channel_id=1, source_target_pairs={{0,2},{1,3},{2,0},{3,1},{4,6},{5,7},{6,4},{7,5},{8,10},{9,11},{10,... | collective-permute-start | bytes 835592 | tf_op jit(solution)/shard_map/ppermute | solution.py:511
  38.6 5.2 %collective-permute-start.8 = (f32[256,128]{1,0:T(8,128)S(1)}, f32[256,128]{1,0:T(8,128)S(1)}, u32[]{:S(2)}, u32[]{:S(2)}) collective-permute-start(f32[256,128]{1,0:T(8,128)S(1)} %constant_dynamic-slice_fusion.1), channel_id=1, source_target_pairs={{0,2},{1,3},{2,0},{3,1},{4,6},{5,7},{6,4},{7,5},{8,10},{9,11},{10,... | collective-permute-start | bytes 393224 | tf_op jit(solution)/shard_map/ppermute | solution.py:511
  40.0 6.1 %collective-permute-start.3 = (f32[272,128]{1,0:T(8,128)S(1)}, f32[272,128]{1,0:T(8,128)S(1)}, u32[]{:S(2)}, u32[]{:S(2)}) collective-permute-start(f32[272,128]{1,0:T(8,128)S(1)} %constant_dynamic-slice_fusion.4), channel_id=1, source_target_pairs={{0,4},{1,5},{2,6},{3,7},{4,0},{5,1},{6,2},{7,3},{8,12},{9,13},{10,... | collective-permute-start | bytes 417800 | tf_op jit(solution)/shard_map/ppermute | solution.py:511
  43.8 8.6 %collective-permute-start.9 = (f32[128,128]{1,0:T(8,128)S(1)}, f32[128,128]{1,0:T(8,128)S(1)}, u32[]{:S(2)}, u32[]{:S(2)}) collective-permute-start(f32[128,128]{1,0:T(8,128)S(1)} %constant_dynamic-slice_fusion), channel_id=1, source_target_pairs={{0,8},{1,9},{2,10},{3,11},{4,12},{5,13},{6,14},{7,15},{8,0},{9,1},... | collective-permute-start | bytes 196616 | tf_op jit(solution)/shard_map/ppermute | solution.py:511
  46.1 7.7 %collective-permute-start.4 = (f32[136,128]{1,0:T(8,128)S(1)}, f32[136,128]{1,0:T(8,128)S(1)}, u32[]{:S(2)}, u32[]{:S(2)}) collective-permute-start(f32[136,128]{1,0:T(8,128)S(1)} %constant_dynamic-slice_fusion.3), channel_id=1, source_target_pairs={{0,8},{1,9},{2,10},{3,11},{4,12},{5,13},{6,14},{7,15},{8,0},{9,1},... | collective-permute-start | bytes 208904 | tf_op jit(solution)/shard_map/ppermute | solution.py:511
  52.4 5.9 %collective-permute-start.10 = (f32[128,128]{1,0:T(8,128)S(1)}, f32[128,128]{1,0:T(8,128)S(1)}, u32[]{:S(2)}, u32[]{:S(2)}) collective-permute-start(f32[128,128]{1,0:T(8,128)S(1)} %dynamic-slice_add_fusion.5), channel_id=1, source_target_pairs={{0,8},{1,9},{2,10},{3,11},{4,12},{5,13},{6,14},{7,15},{8,0},{9,1},... | collective-permute-start | bytes 196616 | tf_op jit(solution)/shard_map/ppermute | solution.py:511
  53.9 6.0 %collective-permute-start.5 = (f32[136,128]{1,0:T(8,128)S(1)}, f32[136,128]{1,0:T(8,128)S(1)}, u32[]{:S(2)}, u32[]{:S(2)}) collective-permute-start(f32[136,128]{1,0:T(8,128)S(1)} %dynamic-slice_add_fusion.4), channel_id=1, source_target_pairs={{0,8},{1,9},{2,10},{3,11},{4,12},{5,13},{6,14},{7,15},{8,0},{9,1},... | collective-permute-start | bytes 208904 | tf_op jit(solution)/shard_map/ppermute | solution.py:511
  58.3 5.0 %collective-permute-start.11 = (f32[256,128]{1,0:T(8,128)S(1)}, f32[256,128]{1,0:T(8,128)S(1)}, u32[]{:S(2)}, u32[]{:S(2)}) collective-permute-start(f32[256,128]{1,0:T(8,128)S(1)} %maximum_select_fusion.5), channel_id=1, source_target_pairs={{0,2},{1,3},{2,0},{3,1},{4,6},{5,7},{6,4},{7,5},{8,10},{9,11},{10,... | collective-permute-start | bytes 393224 | tf_op jit(solution)/shard_map/ppermute | solution.py:511
  59.9 5.1 %collective-permute-start.6 = (f32[272,128]{1,0:T(8,128)S(1)}, f32[272,128]{1,0:T(8,128)S(1)}, u32[]{:S(2)}, u32[]{:S(2)}) collective-permute-start(f32[272,128]{1,0:T(8,128)S(1)} %maximum_select_fusion.4), channel_id=1, source_target_pairs={{0,4},{1,5},{2,6},{3,7},{4,0},{5,1},{6,2},{7,3},{8,12},{9,13},{10,... | collective-permute-start | bytes 417800 | tf_op jit(solution)/shard_map/ppermute | solution.py:511
  65.0 6.6 %collective-permute-start.12 = (f32[544,128]{1,0:T(8,128)S(1)}, f32[544,128]{1,0:T(8,128)S(1)}, u32[]{:S(2)}, u32[]{:S(2)}) collective-permute-start(f32[544,128]{1,0:T(8,128)S(1)} %maximum_select_fusion.2), channel_id=1, source_target_pairs={{0,2},{1,3},{2,0},{3,1},{4,6},{5,7},{6,4},{7,5},{8,10},{9,11},{10,... | collective-permute-start | bytes 835592 | tf_op jit(solution)/shard_map/ppermute | solution.py:511
  65.6 6.4 %collective-permute-start.13 = (f32[512,128]{1,0:T(8,128)S(1)}, f32[512,128]{1,0:T(8,128)S(1)}, u32[]{:S(2)}, u32[]{:S(2)}) collective-permute-start(f32[512,128]{1,0:T(8,128)S(1)} %maximum_select_fusion.3), channel_id=1, source_target_pairs={{0,4},{1,5},{2,6},{3,7},{4,0},{5,1},{6,2},{7,3},{8,12},{9,13},{10,... | collective-permute-start | bytes 786440 | tf_op jit(solution)/shard_map/ppermute | solution.py:511
  71.7 5.0 %collective-permute-start.14 = (f32[1088,128]{1,0:T(8,128)S(1)}, f32[1088,128]{1,0:T(8,128)S(1)}, u32[]{:S(2)}, u32[]{:S(2)}) collective-permute-start(f32[1088,128]{1,0:T(8,128)S(1)} %maximum_select_fusion.mine0), channel_id=1, source_target_pairs={{0,1},{1,0},{2,3},{3,2},{4,5},{5,4},{6,7},{7,6},{8,9},{9,8},{10,11... | collective-permute-start | bytes 1671176 | tf_op jit(solution)/shard_map/ppermute | solution.py:511
  72.0 4.7 %collective-permute-start.15 = (f32[1024,128]{1,0:T(8,128)S(1)}, f32[1024,128]{1,0:T(8,128)S(1)}, u32[]{:S(2)}, u32[]{:S(2)}) collective-permute-start(f32[1024,128]{1,0:T(8,128)S(1)} %maximum_select_fusion.1.mine1), channel_id=1, source_target_pairs={{0,1},{1,0},{2,3},{3,2},{4,5},{5,4},{6,7},{7,6},{8,9},{9,8},{10,11... | collective-permute-start | bytes 1572872 | tf_op jit(solution)/shard_map/ppermute | solution.py:511
  72.4 30.5 %all-to-all-start.1 = ((f32[16,16,1024]{2,1,0:T(8,128)}), f32[16,16,1024]{2,1,0:T(8,128)}, u32[]{:S(2)}, u32[]{:S(2)}) async-start(f32[16,16,1024]{2,1,0:T(8,128)} %bitcast.5), calls=%async_computation.1 | async-start | bytes 2097152 | tf_op jit(solution)/shard_map/all_to_all | solution.py:596

commit v5 on v4

--- a/solution.py
+++ b/solution.py
@@ -111,13 +111,16 @@
 
 
 def images_kernel(
-    core_ref, arrived_ref, other_arrived_ref, corner_ref, other_corner_ref, images_ref, gram_ref
+    core_ref, arrived_ref, other_arrived_ref, corner_ref, other_corner_ref, images_hbm, gram_ref,
+    images_ref, done,
 ):
     width = corner_ref.shape[1]
     count = width // SIDE
-    others = dot_nn(other_arrived_ref[...], other_corner_ref[...])
     images = dot_nn(arrived_ref[...], corner_ref[...])
     images_ref[...] = images
+    copy = pltpu.make_async_copy(images_ref, images_hbm, done)
+    copy.start()
+    others = dot_nn(other_arrived_ref[...], other_corner_ref[...])
     images = jnp.concatenate([images, others], axis=0)
     high, low = split(images)
     second = jnp.concatenate([high, low, high], axis=0)
@@ -150,6 +153,7 @@
 
     for core, pairs in enumerate(shares(count)):
         pl.when(core_ref[0] == core)(functools.partial(share, pairs))
+    copy.wait()
 
 
 def unpack_share(count, core, parts, lower_ref, diagonal_ref, done):
@@ -435,8 +439,8 @@
 
 
 def solve_kernel(
-    count, factor, slot_ref, tail_hbm, returned_hbm, forms_hbm, out_ref,
-    tail_ref, returned_ref, inverse_ref, across_ref, next_ref, beyond_ref, done,
+    count, factor, slot_ref, tail_hbm, returned_hbm, forms_hbm, out_hbm,
+    tail_ref, returned_ref, inverse_ref, across_ref, next_ref, beyond_ref, out_ref, done, out_done,
 ):
     half, three = count // 2 * SIDE, 3 * count // 4 * SIDE
     pairs = [(tail_hbm.at[: 3 * SIDE], tail_ref), (returned_hbm, returned_ref)]
@@ -448,6 +452,7 @@
     width = returned_ref.shape[1]
     placed = (iota((slots, rows), 0) == slot_ref[...]).astype(jnp.float32).astype(jnp.bfloat16)
     rest = {}
+    leaving = []
 
     def home():
         copies[1].wait()
@@ -467,6 +472,12 @@
         else:
             x = dot_nt(source, inverse)
         out_ref[:, first:last] = x * factor
+        leaving.append(
+            pltpu.make_async_copy(
+                out_ref.at[:, first:last], out_hbm.at[:, first:last], out_done.at[len(leaving)]
+            )
+        )
+        leaving[-1].start()
         rest[last] = left(x, 1)
 
     def update(first, last, below):
@@ -488,6 +499,8 @@
     copies[0].wait()
     last = invert_factor(tail_ref[2 * SIDE :, :], [lambda: None] * 2 + steps)
     solved(width - SIDE, width, right(last, 1))
+    for copy in leaving:
+        copy.wait()
 
 
 SMEM = pl.BlockSpec(memory_space=pltpu.SMEM)
@@ -588,6 +601,8 @@
             jax.ShapeDtypeStruct((slots, feature_len), f32),
             jax.ShapeDtypeStruct((sum(share_rows(count)), SIDE), f32),
         ),
+        [pltpu.VMEM((slots, feature_len), f32), dma],
+        (ANY, VMEM),
     )(core, arrived, swap(arrived, 1), *corners)
     streams = reduce_shares(jnp.split(share, [share_rows(count)[0]], axis=0))
     (product, first), second = lax.optimization_barrier(((product, streams[0][0]), streams[1][0]))
@@ -630,8 +645,11 @@
             pltpu.VMEM((half, 3 * half), jnp.bfloat16),
             pltpu.VMEM((quarter, 3 * quarter), jnp.bfloat16),
             pltpu.VMEM((quarter, 3 * quarter), jnp.bfloat16),
+            pltpu.VMEM((row_count, feature_len), f32),
             dma((6,)),
+            dma((4,)),
         ],
+        ANY,
         mib=60,
     )(slot, lower[1], returned.reshape(slots, feature_len), lower[0])
 

time: 110 us -> 109 us (level)
  Pallas kernels: 38.8 us -> 37.6 us
where the time goes in v5:
time: 109 us
  Pallas kernels  37.6 us (34%)
  waiting for transfers between devices  30.9 us (28%)
  blocking collectives  21.5 us (20%)
  starting transfers between devices  16 us (15%)
  local copies, waits for them, and re-layouts  1.79 us (2%)
    ppermute x16, waiting for transfers between devices, swap(): lax.ppermute(x, 'sec', [(i, i ^ bit) for i in range(lax.axis_size('sec'))])  30.9 us
    pallas_call x1, Pallas kernels, per_device(): kernel_call(functools.partial(cholesky_kernel, count), [SMEM] + [ANY] * 4...  26.2 us
    all_to_all x1, blocking collectives, per_device(): lax.all_to_all(packed.reshape(owners, capacity, feature_len), 'sec', spli...  21.5 us
    ppermute x16, starting transfers between devices, swap(): lax.ppermute(x, 'sec', [(i, i ^ bit) for i in range(lax.axis_size('sec'))])  11.7 us
    pallas_call x1, Pallas kernels, per_device(): kernel_call(functools.partial(solve_kernel, count, factor), [VMEM] + [ANY...  6.41 us
    all_to_all x1, starting transfers between devices, per_device(): lax.all_to_all(product.reshape(owners, capacity, feature_len), 'sec', spl...  4.34 us
    pallas_call x1, Pallas kernels, per_device(): kernel_call(images_kernel, [SMEM] + [VMEM] * 4, (jax.ShapeDtypeStruct((sl...  2.63 us
  transfers between devices with their start and end apart: 17, of which 11 were waited for; matrix products, arithmetic and copies ran while one was open for 0% of the time, Pallas kernels for 26%

profile of v5, /device:TPU:0, one launch (start us, length us, event | category | flops | bytes accessed | tf_op | source)
XLA Modules:
  0.0 108.6 jit_solution(5363536733592107729)
XLA Ops:
  0.0 0.5 collective-permute-start.1
  0.5 2.1 %shard_map.55 = (s32[1,128]{1,0:T(1,128)}, bf16[256,1024]{1,0:T(8,128)(2,1)}) custom-call(bf16[128,1024]{1,0:T(8,128)(2,1)} %edge_hbm.1, s32[16,16]{1,0:T(8,128)} %joining_hbm.1, s32[1,128]{1,0:T(1,128)} %bitcast.10, s32[1,128]{1,0:T(1,128)} %bitcast.11), custom_call_target="tpu_custom_call" | custom-call | tf_op jit(solution)/shard_map/pallas_call | solution.py:570
  2.6 21.5 %all_to_all.10 = bf16[16,16,1024]{2,1,0:T(8,128)(2,1)S(1)} all-to-all(bf16[16,16,1024]{2,1,0:T(8,128)(2,1)} %bitcast.9), channel_id=1, replica_groups=mesh['runs'=2,'sec'=16] {'sec'}, dimensions={0} | all-to-all | bytes 1048576 | tf_op jit(solution)/shard_map/all_to_all | solution.py:586
  24.1 0.0 collective-permute-start
  24.1 0.0 collective-permute-done.1.other_hbm
  24.1 0.0 copy-start
  24.1 1.6 %copy-done = bf16[1024,1024]{1,0:T(8,128)(2,1)S(1)} copy-done((bf16[1024,1024]{1,0:T(8,128)(2,1)S(1)}, bf16[1024,1024]{1,0:T(8,128)(2,1)}, u32[]{:S(2)}) %copy-start) | copy-done | bytes 2097176
  25.7 0.3 shard_map.56
  26.0 0.0 collective-permute-done.other_arrived_ref
  26.1 2.6 %shard_map.57 = (f32[256,1024]{1,0:T(8,128)}, f32[2112,128]{1,0:T(8,128)S(1)}) custom-call(s32[1]{0:T(128)} %bitcast.2.core_ref, bf16[256,1024]{1,0:T(8,128)(2,1)S(1)} %bitcast.8, bf16[256,1024]{1,0:T(8,128)(2,1)S(1)} %collective-permute-done.other_arrived_ref, bf16[1024,1024]{1,0:T(8,128)(2,1)S(1)} %get-tuple-element.21.corner_ref, ...), custom_call_target="tpu_custom_call" | custom-call | tf_op jit(solution)/shard_map/pallas_call | solution.py:597
  28.8 1.8 %collective-permute-start.7 = (f32[512,128]{1,0:T(8,128)S(1)}, f32[512,128]{1,0:T(8,128)S(1)}, u32[]{:S(2)}, u32[]{:S(2)}) collective-permute-start(f32[512,128]{1,0:T(8,128)S(1)} %constant_dynamic-slice_fusion.2), channel_id=1, source_target_pairs={{0,4},{1,5},{2,6},{3,7},{4,0},{5,1},{6,2},{7,3},{8,12},{9,13},{10,... | collective-permute-start | bytes 786440 | tf_op jit(solution)/shard_map/ppermute | solution.py:524
  30.6 1.0 collective-permute-start.2
  31.6 5.9 %collective-permute-done.7 = f32[512,128]{1,0:T(8,128)S(1)} collective-permute-done((f32[512,128]{1,0:T(8,128)S(1)}, f32[512,128]{1,0:T(8,128)S(1)}, u32[]{:S(2)}, u32[]{:S(2)}) %collective-permute-start.7) | collective-permute-done | bytes 262176 | tf_op jit(solution)/shard_map/ppermute | solution.py:524
  37.6 0.7 collective-permute-start.8
  38.3 0.7 collective-permute-done.2
  39.0 1.1 %collective-permute-start.3 = (f32[272,128]{1,0:T(8,128)S(1)}, f32[272,128]{1,0:T(8,128)S(1)}, u32[]{:S(2)}, u32[]{:S(2)}) collective-permute-start(f32[272,128]{1,0:T(8,128)S(1)} %constant_dynamic-slice_fusion.4), channel_id=1, source_target_pairs={{0,4},{1,5},{2,6},{3,7},{4,0},{5,1},{6,2},{7,3},{8,12},{9,13},{10,... | collective-permute-start | bytes 417800 | tf_op jit(solution)/shard_map/ppermute | solution.py:524
  40.2 2.6 %collective-permute-done.8 = f32[256,128]{1,0:T(8,128)S(1)} collective-permute-done((f32[256,128]{1,0:T(8,128)S(1)}, f32[256,128]{1,0:T(8,128)S(1)}, u32[]{:S(2)}, u32[]{:S(2)}) %collective-permute-start.8) | collective-permute-done | bytes 131104 | tf_op jit(solution)/shard_map/ppermute | solution.py:524
  42.8 2.3 %collective-permute-start.9 = (f32[128,128]{1,0:T(8,128)S(1)}, f32[128,128]{1,0:T(8,128)S(1)}, u32[]{:S(2)}, u32[]{:S(2)}) collective-permute-start(f32[128,128]{1,0:T(8,128)S(1)} %constant_dynamic-slice_fusion), channel_id=1, source_target_pairs={{0,8},{1,9},{2,10},{3,11},{4,12},{5,13},{6,14},{7,15},{8,0},{9,1},... | collective-permute-start | bytes 196616 | tf_op jit(solution)/shard_map/ppermute | solution.py:524
  45.1 0.0 collective-permute-done.3
  45.2 0.8 collective-permute-start.4
  46.0 5.4 %collective-permute-done.9 = f32[128,128]{1,0:T(8,128)S(1)} collective-permute-done((f32[128,128]{1,0:T(8,128)S(1)}, f32[128,128]{1,0:T(8,128)S(1)}, u32[]{:S(2)}, u32[]{:S(2)}) %collective-permute-start.9) | collective-permute-done | bytes 65568 | tf_op jit(solution)/shard_map/ppermute | solution.py:524
  51.4 0.1 collective-permute-start.10
  51.5 1.4 %collective-permute-done.4 = f32[136,128]{1,0:T(8,128)S(1)} collective-permute-done((f32[136,128]{1,0:T(8,128)S(1)}, f32[136,128]{1,0:T(8,128)S(1)}, u32[]{:S(2)}, u32[]{:S(2)}) %collective-permute-start.4) | collective-permute-done | bytes 69664 | tf_op jit(solution)/shard_map/ppermute | solution.py:524
  52.9 1.6 %collective-permute-start.5 = (f32[136,128]{1,0:T(8,128)S(1)}, f32[136,128]{1,0:T(8,128)S(1)}, u32[]{:S(2)}, u32[]{:S(2)}) collective-permute-start(f32[136,128]{1,0:T(8,128)S(1)} %dynamic-slice_add_fusion.4), channel_id=1, source_target_pairs={{0,8},{1,9},{2,10},{3,11},{4,12},{5,13},{6,14},{7,15},{8,0},{9,1},... | collective-permute-start | bytes 208904 | tf_op jit(solution)/shard_map/ppermute | solution.py:524
  54.5 2.8 %collective-permute-done.10 = f32[128,128]{1,0:T(8,128)S(1)} collective-permute-done((f32[128,128]{1,0:T(8,128)S(1)}, f32[128,128]{1,0:T(8,128)S(1)}, u32[]{:S(2)}, u32[]{:S(2)}) %collective-permute-start.10) | collective-permute-done | bytes 65568 | tf_op jit(solution)/shard_map/ppermute | solution.py:524
  57.3 0.1 collective-permute-start.11
  57.4 1.5 %collective-permute-done.5 = f32[136,128]{1,0:T(8,128)S(1)} collective-permute-done((f32[136,128]{1,0:T(8,128)S(1)}, f32[136,128]{1,0:T(8,128)S(1)}, u32[]{:S(2)}, u32[]{:S(2)}) %collective-permute-start.5) | collective-permute-done | bytes 69664 | tf_op jit(solution)/shard_map/ppermute | solution.py:524
  58.9 0.6 collective-permute-start.6
  59.6 2.8 %collective-permute-done.11 = f32[256,128]{1,0:T(8,128)S(1)} collective-permute-done((f32[256,128]{1,0:T(8,128)S(1)}, f32[256,128]{1,0:T(8,128)S(1)}, u32[]{:S(2)}, u32[]{:S(2)}) %collective-permute-start.11) | collective-permute-done | bytes 131104 | tf_op jit(solution)/shard_map/ppermute | solution.py:524
  62.4 1.7 %collective-permute-done.6 = f32[272,128]{1,0:T(8,128)S(1)} collective-permute-done((f32[272,128]{1,0:T(8,128)S(1)}, f32[272,128]{1,0:T(8,128)S(1)}, u32[]{:S(2)}, u32[]{:S(2)}) %collective-permute-start.6) | collective-permute-done | bytes 139296 | tf_op jit(solution)/shard_map/ppermute | solution.py:524
  64.1 0.6 collective-permute-start.12
  64.6 0.1 collective-permute-start.13
  64.8 5.9 %collective-permute-done.12 = f32[544,128]{1,0:T(8,128)S(1)} collective-permute-done((f32[544,128]{1,0:T(8,128)S(1)}, f32[544,128]{1,0:T(8,128)S(1)}, u32[]{:S(2)}, u32[]{:S(2)}) %collective-permute-start.12) | collective-permute-done | bytes 278560 | tf_op jit(solution)/shard_map/ppermute | solution.py:524
  70.7 0.1 collective-permute-start.14
  70.8 0.2 collective-permute-done.13
  71.1 0.4 collective-permute-start.15
  71.4 4.3 %all-to-all-start.1 = ((f32[16,16,1024]{2,1,0:T(8,128)}), f32[16,16,1024]{2,1,0:T(8,128)}, u32[]{:S(2)}, u32[]{:S(2)}) async-start(f32[16,16,1024]{2,1,0:T(8,128)} %bitcast.5), calls=%async_computation.1 | async-start | bytes 2097152 | tf_op jit(solution)/shard_map/all_to_all | solution.py:611
  75.8 0.0 collective-permute-done.15.other1
  75.8 0.0 collective-permute-done.14.other0
  75.8 26.2 %shard_map.58 = (bf16[10922,1536]{1,0:T(8,128)(2,1)}, f32[65536,128]{1,0:T(8,128)}) custom-call(s32[1]{0:T(128)} %bitcast.2.core_ref, f32[1088,128]{1,0:T(8,128)S(1)} %maximum_select_fusion.mine0, f32[1024,128]{1,0:T(8,128)S(1)} %maximum_select_fusion.1.mine1, f32[1088,128]{1,0:T(8,128)S(1)} %collective-permute-done.14.other0, ...), custom_call_target="tpu_custom_call" | custom-call | flops 193273528320 | tf_op jit(solution)/shard_map/pallas_call | solution.py:615
  102.0 0.0 all-to-all-done.1
  102.0 6.4 %shard_map.59 = f32[128,1024]{1,0:T(8,128)} custom-call(s32[1,128]{1,0:T(1,128)} %get-tuple-element.19.slot_ref, f32[65536,128]{1,0:T(8,128)} %get-tuple-element.30.tail_hbm, f32[256,1024]{1,0:T(8,128)} %bitcast.6.returned_hbm, bf16[10922,1536]{1,0:T(8,128)(2,1)} %get-tuple-element.32.forms_hbm), custom_call_target="tpu_custom_call" | custom-call | tf_op jit(solution)/shard_map/pallas_call | solution.py:637
  (20 shorter events, 0.4 us)
Async XLA Ops:
  0.0 24.1 %collective-permute-start.1 = (bf16[1024,1024]{1,0:T(8,128)(2,1)}, bf16[1024,1024]{1,0:T(8,128)(2,1)S(1)}, u32[]{:S(2)}, u32[]{:S(2)}) collective-permute-start(bf16[1024,1024]{1,0:T(8,128)(2,1)} %mine_hbm.1), channel_id=1, source_target_pairs={{0,1},{1,0},{2,3},{3,2},{4,5},{5,4},{6,7},{7,6},{8,9},{9,8},{10,11... | collective-permute-start | bytes 6291464 | tf_op jit(solution)/shard_map/ppermute | solution.py:524
  24.1 1.9 %collective-permute-start = (bf16[256,1024]{1,0:T(8,128)(2,1)S(1)}, bf16[256,1024]{1,0:T(8,128)(2,1)S(1)}, u32[]{:S(2)}, u32[]{:S(2)}) collective-permute-start(bf16[256,1024]{1,0:T(8,128)(2,1)S(1)} %bitcast.7), channel_id=1, source_target_pairs={{0,1},{1,0},{2,3},{3,2},{4,5},{5,4},{6,7},{7,6},{8,9},{9,8},{10,11... | collective-permute-start | bytes 1572872 | tf_op jit(solution)/shard_map/ppermute | solution.py:524
  24.1 1.6 %copy-start = (bf16[1024,1024]{1,0:T(8,128)(2,1)S(1)}, bf16[1024,1024]{1,0:T(8,128)(2,1)}, u32[]{:S(2)}) copy-start(bf16[1024,1024]{1,0:T(8,128)(2,1)} %mine_hbm.1) | copy-start | bytes 6291460
  28.8 8.8 %collective-permute-start.7 = (f32[512,128]{1,0:T(8,128)S(1)}, f32[512,128]{1,0:T(8,128)S(1)}, u32[]{:S(2)}, u32[]{:S(2)}) collective-permute-start(f32[512,128]{1,0:T(8,128)S(1)} %constant_dynamic-slice_fusion.2), channel_id=1, source_target_pairs={{0,4},{1,5},{2,6},{3,7},{4,0},{5,1},{6,2},{7,3},{8,12},{9,13},{10,... | collective-permute-start | bytes 786440 | tf_op jit(solution)/shard_map/ppermute | solution.py:524
  30.6 8.3 %collective-permute-start.2 = (f32[544,128]{1,0:T(8,128)S(1)}, f32[544,128]{1,0:T(8,128)S(1)}, u32[]{:S(2)}, u32[]{:S(2)}) collective-permute-start(f32[544,128]{1,0:T(8,128)S(1)} %constant_dynamic-slice_fusion.5), channel_id=1, source_target_pairs={{0,2},{1,3},{2,0},{3,1},{4,6},{5,7},{6,4},{7,5},{8,10},{9,11},{10,... | collective-permute-start | bytes 835592 | tf_op jit(solution)/shard_map/ppermute | solution.py:524
  37.6 5.2 %collective-permute-start.8 = (f32[256,128]{1,0:T(8,128)S(1)}, f32[256,128]{1,0:T(8,128)S(1)}, u32[]{:S(2)}, u32[]{:S(2)}) collective-permute-start(f32[256,128]{1,0:T(8,128)S(1)} %constant_dynamic-slice_fusion.1), channel_id=1, source_target_pairs={{0,2},{1,3},{2,0},{3,1},{4,6},{5,7},{6,4},{7,5},{8,10},{9,11},{10,... | collective-permute-start | bytes 393224 | tf_op jit(solution)/shard_map/ppermute | solution.py:524
  39.0 6.1 %collective-permute-start.3 = (f32[272,128]{1,0:T(8,128)S(1)}, f32[272,128]{1,0:T(8,128)S(1)}, u32[]{:S(2)}, u32[]{:S(2)}) collective-permute-start(f32[272,128]{1,0:T(8,128)S(1)} %constant_dynamic-slice_fusion.4), channel_id=1, source_target_pairs={{0,4},{1,5},{2,6},{3,7},{4,0},{5,1},{6,2},{7,3},{8,12},{9,13},{10,... | collective-permute-start | bytes 417800 | tf_op jit(solution)/shard_map/ppermute | solution.py:524
  42.8 8.6 %collective-permute-start.9 = (f32[128,128]{1,0:T(8,128)S(1)}, f32[128,128]{1,0:T(8,128)S(1)}, u32[]{:S(2)}, u32[]{:S(2)}) collective-permute-start(f32[128,128]{1,0:T(8,128)S(1)} %constant_dynamic-slice_fusion), channel_id=1, source_target_pairs={{0,8},{1,9},{2,10},{3,11},{4,12},{5,13},{6,14},{7,15},{8,0},{9,1},... | collective-permute-start | bytes 196616 | tf_op jit(solution)/shard_map/ppermute | solution.py:524
  45.2 7.7 %collective-permute-start.4 = (f32[136,128]{1,0:T(8,128)S(1)}, f32[136,128]{1,0:T(8,128)S(1)}, u32[]{:S(2)}, u32[]{:S(2)}) collective-permute-start(f32[136,128]{1,0:T(8,128)S(1)} %constant_dynamic-slice_fusion.3), channel_id=1, source_target_pairs={{0,8},{1,9},{2,10},{3,11},{4,12},{5,13},{6,14},{7,15},{8,0},{9,1},... | collective-permute-start | bytes 208904 | tf_op jit(solution)/shard_map/ppermute | solution.py:524
  51.4 5.9 %collective-permute-start.10 = (f32[128,128]{1,0:T(8,128)S(1)}, f32[128,128]{1,0:T(8,128)S(1)}, u32[]{:S(2)}, u32[]{:S(2)}) collective-permute-start(f32[128,128]{1,0:T(8,128)S(1)} %dynamic-slice_add_fusion.5), channel_id=1, source_target_pairs={{0,8},{1,9},{2,10},{3,11},{4,12},{5,13},{6,14},{7,15},{8,0},{9,1},... | collective-permute-start | bytes 196616 | tf_op jit(solution)/shard_map/ppermute | solution.py:524
  52.9 6.0 %collective-permute-start.5 = (f32[136,128]{1,0:T(8,128)S(1)}, f32[136,128]{1,0:T(8,128)S(1)}, u32[]{:S(2)}, u32[]{:S(2)}) collective-permute-start(f32[136,128]{1,0:T(8,128)S(1)} %dynamic-slice_add_fusion.4), channel_id=1, source_target_pairs={{0,8},{1,9},{2,10},{3,11},{4,12},{5,13},{6,14},{7,15},{8,0},{9,1},... | collective-permute-start | bytes 208904 | tf_op jit(solution)/shard_map/ppermute | solution.py:524
  57.3 5.0 %collective-permute-start.11 = (f32[256,128]{1,0:T(8,128)S(1)}, f32[256,128]{1,0:T(8,128)S(1)}, u32[]{:S(2)}, u32[]{:S(2)}) collective-permute-start(f32[256,128]{1,0:T(8,128)S(1)} %maximum_select_fusion.5), channel_id=1, source_target_pairs={{0,2},{1,3},{2,0},{3,1},{4,6},{5,7},{6,4},{7,5},{8,10},{9,11},{10,... | collective-permute-start | bytes 393224 | tf_op jit(solution)/shard_map/ppermute | solution.py:524
  58.9 5.1 %collective-permute-start.6 = (f32[272,128]{1,0:T(8,128)S(1)}, f32[272,128]{1,0:T(8,128)S(1)}, u32[]{:S(2)}, u32[]{:S(2)}) collective-permute-start(f32[272,128]{1,0:T(8,128)S(1)} %maximum_select_fusion.4), channel_id=1, source_target_pairs={{0,4},{1,5},{2,6},{3,7},{4,0},{5,1},{6,2},{7,3},{8,12},{9,13},{10,... | collective-permute-start | bytes 417800 | tf_op jit(solution)/shard_map/ppermute | solution.py:524
  64.1 6.6 %collective-permute-start.12 = (f32[544,128]{1,0:T(8,128)S(1)}, f32[544,128]{1,0:T(8,128)S(1)}, u32[]{:S(2)}, u32[]{:S(2)}) collective-permute-start(f32[544,128]{1,0:T(8,128)S(1)} %maximum_select_fusion.2), channel_id=1, source_target_pairs={{0,2},{1,3},{2,0},{3,1},{4,6},{5,7},{6,4},{7,5},{8,10},{9,11},{10,... | collective-permute-start | bytes 835592 | tf_op jit(solution)/shard_map/ppermute | solution.py:524
  64.6 6.4 %collective-permute-start.13 = (f32[512,128]{1,0:T(8,128)S(1)}, f32[512,128]{1,0:T(8,128)S(1)}, u32[]{:S(2)}, u32[]{:S(2)}) collective-permute-start(f32[512,128]{1,0:T(8,128)S(1)} %maximum_select_fusion.3), channel_id=1, source_target_pairs={{0,4},{1,5},{2,6},{3,7},{4,0},{5,1},{6,2},{7,3},{8,12},{9,13},{10,... | collective-permute-start | bytes 786440 | tf_op jit(solution)/shard_map/ppermute | solution.py:524
  70.7 5.0 %collective-permute-start.14 = (f32[1088,128]{1,0:T(8,128)S(1)}, f32[1088,128]{1,0:T(8,128)S(1)}, u32[]{:S(2)}, u32[]{:S(2)}) collective-permute-start(f32[1088,128]{1,0:T(8,128)S(1)} %maximum_select_fusion.mine0), channel_id=1, source_target_pairs={{0,1},{1,0},{2,3},{3,2},{4,5},{5,4},{6,7},{7,6},{8,9},{9,8},{10,11... | collective-permute-start | bytes 1671176 | tf_op jit(solution)/shard_map/ppermute | solution.py:524
  71.1 4.7 %collective-permute-start.15 = (f32[1024,128]{1,0:T(8,128)S(1)}, f32[1024,128]{1,0:T(8,128)S(1)}, u32[]{:S(2)}, u32[]{:S(2)}) collective-permute-start(f32[1024,128]{1,0:T(8,128)S(1)} %maximum_select_fusion.1.mine1), channel_id=1, source_target_pairs={{0,1},{1,0},{2,3},{3,2},{4,5},{5,4},{6,7},{7,6},{8,9},{9,8},{10,11... | collective-permute-start | bytes 1572872 | tf_op jit(solution)/shard_map/ppermute | solution.py:524
  71.4 30.5 %all-to-all-start.1 = ((f32[16,16,1024]{2,1,0:T(8,128)}), f32[16,16,1024]{2,1,0:T(8,128)}, u32[]{:S(2)}, u32[]{:S(2)}) async-start(f32[16,16,1024]{2,1,0:T(8,128)} %bitcast.5), calls=%async_computation.1 | async-start | bytes 2097152 | tf_op jit(solution)/shard_map/all_to_all | solution.py:611

commit v6 on v5

--- a/solution.py
+++ b/solution.py
@@ -51,8 +51,8 @@
 
 
 def route_kernel(
-    capacity, edge_hbm, joining_hbm, left_hbm, right_hbm, slot_ref, packed_ref,
-    edge_ref, joining_ref, left_ref, right_ref, done,
+    capacity, edge_hbm, joining_hbm, left_hbm, right_hbm, slot_ref, packed_hbm,
+    packed_ref, edge_ref, joining_ref, left_ref, right_ref, done, out_done,
 ):
     bf16 = jnp.bfloat16
     pairs = [
@@ -82,9 +82,16 @@
     slot_ref[...] = slot
     placed = one(iota((slots, rows), 0) == slot).astype(bf16)
     copies[3].wait()
-    packed_ref[...] = jnp.dot(
-        placed, edge_ref[...], preferred_element_type=jnp.float32
-    ).astype(bf16)
+    half = slots // 2
+    leaving = []
+    for i, part in enumerate((slice(0, half), slice(half, slots))):
+        packed_ref[part, :] = dot_nn(placed[part], edge_ref[...]).astype(bf16)
+        leaving.append(
+            pltpu.make_async_copy(packed_ref.at[part], packed_hbm.at[part], out_done.at[i])
+        )
+        leaving[-1].start()
+    for copy in leaving:
+        copy.wait()
 
 
 def fetch_kernel(mine_hbm, other_hbm, mine_ref, other_ref, done):
@@ -575,12 +582,15 @@
             jax.ShapeDtypeStruct((slots, feature_len), edge_rows.dtype),
         ),
         [
+            pltpu.VMEM((slots, feature_len), edge_rows.dtype),
             pltpu.VMEM((row_count, feature_len), edge_rows.dtype),
             pltpu.VMEM(joining.shape, i32),
             pltpu.VMEM((1, row_count), i32),
             pltpu.VMEM((1, row_count), i32),
             dma((4,)),
+            dma((2,)),
         ],
+        (VMEM, ANY),
         mib=60,
     )(edge_rows, joining, charge_left[None, :], charge_right[None, :])
     arrived = lax.all_to_all(

time: 109 us -> 109 us (level)
  waiting for transfers between devices: 30.9 us -> 29.5 us
  starting transfers between devices: 16 us -> 17.3 us
    ppermute x16, waiting for transfers between devices: 30.9 us -> 29.5 us  [swap(): lax.ppermute(x, 'sec', [(i, i ^ bit) for i in range(lax.axis_size('sec'))])]
    ppermute x16, starting transfers between devices: 11.7 us -> 12.9 us  [swap(): lax.ppermute(x, 'sec', [(i, i ^ bit) for i in range(lax.axis_size('sec'))])]
  transfers between devices with their start and end apart: 17 -> 17, of which waited for: 11 -> 11; matrix products, arithmetic and copies ran while one was open for 0% -> 0% of each run, Pallas kernels for 26% -> 27%
where the time goes in v6:
time: 109 us
  Pallas kernels  38.2 us (35%)
  waiting for transfers between devices  29.5 us (27%)
  blocking collectives  21.5 us (20%)
  starting transfers between devices  17.3 us (16%)
  local copies, waits for them, and re-layouts  1.79 us (2%)
    ppermute x16, waiting for transfers between devices, swap(): lax.ppermute(x, 'sec', [(i, i ^ bit) for i in range(lax.axis_size('sec'))])  29.5 us
    pallas_call x1, Pallas kernels, per_device(): kernel_call(functools.partial(cholesky_kernel, count), [SMEM] + [ANY] * 4...  26.2 us
    all_to_all x1, blocking collectives, per_device(): lax.all_to_all(packed.reshape(owners, capacity, feature_len), 'sec', spli...  21.5 us
    ppermute x16, starting transfers between devices, swap(): lax.ppermute(x, 'sec', [(i, i ^ bit) for i in range(lax.axis_size('sec'))])  12.9 us
    pallas_call x1, Pallas kernels, per_device(): kernel_call(functools.partial(solve_kernel, count, factor), [VMEM] + [ANY...  6.41 us
    all_to_all x1, starting transfers between devices, per_device(): lax.all_to_all(product.reshape(owners, capacity, feature_len), 'sec', spl...  4.46 us
    pallas_call x1, Pallas kernels, per_device(): kernel_call(functools.partial(route_kernel, capacity), [ANY] * 4, (jax.Sh...  2.65 us
    pallas_call x1, Pallas kernels, per_device(): kernel_call(images_kernel, [SMEM] + [VMEM] * 4, (jax.ShapeDtypeStruct((sl...  2.63 us
  transfers between devices with their start and end apart: 17, of which 11 were waited for; matrix products, arithmetic and copies ran while one was open for 0% of the time, Pallas kernels for 27%

profile of v6, /device:TPU:0, one launch (start us, length us, event | category | flops | bytes accessed | tf_op | source)
XLA Modules:
  0.0 108.9 jit_solution(14305682654639336625)
XLA Ops:
  0.0 0.5 collective-permute-start.1
  0.5 2.6 %shard_map.55 = (s32[1,128]{1,0:T(1,128)}, bf16[256,1024]{1,0:T(8,128)(2,1)}) custom-call(bf16[128,1024]{1,0:T(8,128)(2,1)} %edge_hbm.1, s32[16,16]{1,0:T(8,128)} %joining_hbm.1, s32[1,128]{1,0:T(1,128)} %bitcast.10, s32[1,128]{1,0:T(1,128)} %bitcast.11), custom_call_target="tpu_custom_call" | custom-call | tf_op jit(solution)/shard_map/pallas_call | solution.py:577
  3.1 21.5 %all_to_all.10 = bf16[16,16,1024]{2,1,0:T(8,128)(2,1)S(1)} all-to-all(bf16[16,16,1024]{2,1,0:T(8,128)(2,1)} %bitcast.9), channel_id=1, replica_groups=mesh['runs'=2,'sec'=16] {'sec'}, dimensions={0} | all-to-all | bytes 1048576 | tf_op jit(solution)/shard_map/all_to_all | solution.py:596
  24.6 0.0 collective-permute-start
  24.7 0.0 collective-permute-done.1.other_hbm
  24.7 0.0 copy-start
  24.7 1.6 %copy-done = bf16[1024,1024]{1,0:T(8,128)(2,1)S(1)} copy-done((bf16[1024,1024]{1,0:T(8,128)(2,1)S(1)}, bf16[1024,1024]{1,0:T(8,128)(2,1)}, u32[]{:S(2)}) %copy-start) | copy-done | bytes 2097176
  26.2 0.3 shard_map.56
  26.6 0.0 collective-permute-done.other_arrived_ref
  26.6 2.6 %shard_map.57 = (f32[256,1024]{1,0:T(8,128)}, f32[2112,128]{1,0:T(8,128)S(1)}) custom-call(s32[1]{0:T(128)} %bitcast.2.core_ref, bf16[256,1024]{1,0:T(8,128)(2,1)S(1)} %bitcast.8, bf16[256,1024]{1,0:T(8,128)(2,1)S(1)} %collective-permute-done.other_arrived_ref, bf16[1024,1024]{1,0:T(8,128)(2,1)S(1)} %get-tuple-element.21.corner_ref, ...), custom_call_target="tpu_custom_call" | custom-call | tf_op jit(solution)/shard_map/pallas_call | solution.py:607
  29.3 1.8 %collective-permute-start.7 = (f32[512,128]{1,0:T(8,128)S(1)}, f32[512,128]{1,0:T(8,128)S(1)}, u32[]{:S(2)}, u32[]{:S(2)}) collective-permute-start(f32[512,128]{1,0:T(8,128)S(1)} %constant_dynamic-slice_fusion.2), channel_id=1, source_target_pairs={{0,4},{1,5},{2,6},{3,7},{4,0},{5,1},{6,2},{7,3},{8,12},{9,13},{10,... | collective-permute-start | bytes 786440 | tf_op jit(solution)/shard_map/ppermute | solution.py:531
  31.2 1.0 collective-permute-start.2
  32.1 5.9 %collective-permute-done.7 = f32[512,128]{1,0:T(8,128)S(1)} collective-permute-done((f32[512,128]{1,0:T(8,128)S(1)}, f32[512,128]{1,0:T(8,128)S(1)}, u32[]{:S(2)}, u32[]{:S(2)}) %collective-permute-start.7) | collective-permute-done | bytes 262176 | tf_op jit(solution)/shard_map/ppermute | solution.py:531
  38.1 0.7 collective-permute-start.8
  38.8 0.7 collective-permute-done.2
  39.6 1.1 %collective-permute-start.3 = (f32[272,128]{1,0:T(8,128)S(1)}, f32[272,128]{1,0:T(8,128)S(1)}, u32[]{:S(2)}, u32[]{:S(2)}) collective-permute-start(f32[272,128]{1,0:T(8,128)S(1)} %constant_dynamic-slice_fusion.4), channel_id=1, source_target_pairs={{0,4},{1,5},{2,6},{3,7},{4,0},{5,1},{6,2},{7,3},{8,12},{9,13},{10,... | collective-permute-start | bytes 417800 | tf_op jit(solution)/shard_map/ppermute | solution.py:531
  40.7 2.6 %collective-permute-done.8 = f32[256,128]{1,0:T(8,128)S(1)} collective-permute-done((f32[256,128]{1,0:T(8,128)S(1)}, f32[256,128]{1,0:T(8,128)S(1)}, u32[]{:S(2)}, u32[]{:S(2)}) %collective-permute-start.8) | collective-permute-done | bytes 131104 | tf_op jit(solution)/shard_map/ppermute | solution.py:531
  43.3 2.3 %collective-permute-start.9 = (f32[128,128]{1,0:T(8,128)S(1)}, f32[128,128]{1,0:T(8,128)S(1)}, u32[]{:S(2)}, u32[]{:S(2)}) collective-permute-start(f32[128,128]{1,0:T(8,128)S(1)} %constant_dynamic-slice_fusion), channel_id=1, source_target_pairs={{0,8},{1,9},{2,10},{3,11},{4,12},{5,13},{6,14},{7,15},{8,0},{9,1},... | collective-permute-start | bytes 196616 | tf_op jit(solution)/shard_map/ppermute | solution.py:531
  45.7 0.0 collective-permute-done.3
  45.7 0.8 collective-permute-start.4
  46.5 5.4 %collective-permute-done.9 = f32[128,128]{1,0:T(8,128)S(1)} collective-permute-done((f32[128,128]{1,0:T(8,128)S(1)}, f32[128,128]{1,0:T(8,128)S(1)}, u32[]{:S(2)}, u32[]{:S(2)}) %collective-permute-start.9) | collective-permute-done | bytes 65568 | tf_op jit(solution)/shard_map/ppermute | solution.py:531
  51.9 0.1 collective-permute-start.10
  52.0 1.4 %collective-permute-done.4 = f32[136,128]{1,0:T(8,128)S(1)} collective-permute-done((f32[136,128]{1,0:T(8,128)S(1)}, f32[136,128]{1,0:T(8,128)S(1)}, u32[]{:S(2)}, u32[]{:S(2)}) %collective-permute-start.4) | collective-permute-done | bytes 69664 | tf_op jit(solution)/shard_map/ppermute | solution.py:531
  53.4 1.6 %collective-permute-start.5 = (f32[136,128]{1,0:T(8,128)S(1)}, f32[136,128]{1,0:T(8,128)S(1)}, u32[]{:S(2)}, u32[]{:S(2)}) collective-permute-start(f32[136,128]{1,0:T(8,128)S(1)} %dynamic-slice_add_fusion.4), channel_id=1, source_target_pairs={{0,8},{1,9},{2,10},{3,11},{4,12},{5,13},{6,14},{7,15},{8,0},{9,1},... | collective-permute-start | bytes 208904 | tf_op jit(solution)/shard_map/ppermute | solution.py:531
  55.0 2.8 %collective-permute-done.10 = f32[128,128]{1,0:T(8,128)S(1)} collective-permute-done((f32[128,128]{1,0:T(8,128)S(1)}, f32[128,128]{1,0:T(8,128)S(1)}, u32[]{:S(2)}, u32[]{:S(2)}) %collective-permute-start.10) | collective-permute-done | bytes 65568 | tf_op jit(solution)/shard_map/ppermute | solution.py:531
  57.9 0.1 collective-permute-start.11
  57.9 0.8 collective-permute-done.5
  58.7 1.4 %collective-permute-start.6 = (f32[272,128]{1,0:T(8,128)S(1)}, f32[272,128]{1,0:T(8,128)S(1)}, u32[]{:S(2)}, u32[]{:S(2)}) collective-permute-start(f32[272,128]{1,0:T(8,128)S(1)} %maximum_select_fusion.4), channel_id=1, source_target_pairs={{0,4},{1,5},{2,6},{3,7},{4,0},{5,1},{6,2},{7,3},{8,12},{9,13},{10,... | collective-permute-start | bytes 417800 | tf_op jit(solution)/shard_map/ppermute | solution.py:531
  60.1 2.8 %collective-permute-done.11 = f32[256,128]{1,0:T(8,128)S(1)} collective-permute-done((f32[256,128]{1,0:T(8,128)S(1)}, f32[256,128]{1,0:T(8,128)S(1)}, u32[]{:S(2)}, u32[]{:S(2)}) %collective-permute-start.11) | collective-permute-done | bytes 131104 | tf_op jit(solution)/shard_map/ppermute | solution.py:531
  62.9 0.9 collective-permute-done.6
  63.9 1.3 %collective-permute-start.12 = (f32[544,128]{1,0:T(8,128)S(1)}, f32[544,128]{1,0:T(8,128)S(1)}, u32[]{:S(2)}, u32[]{:S(2)}) collective-permute-start(f32[544,128]{1,0:T(8,128)S(1)} %maximum_select_fusion.2), channel_id=1, source_target_pairs={{0,2},{1,3},{2,0},{3,1},{4,6},{5,7},{6,4},{7,5},{8,10},{9,11},{10,... | collective-permute-start | bytes 835592 | tf_op jit(solution)/shard_map/ppermute | solution.py:531
  65.2 0.1 collective-permute-start.13
  65.3 5.6 %collective-permute-done.12 = f32[544,128]{1,0:T(8,128)S(1)} collective-permute-done((f32[544,128]{1,0:T(8,128)S(1)}, f32[544,128]{1,0:T(8,128)S(1)}, u32[]{:S(2)}, u32[]{:S(2)}) %collective-permute-start.12) | collective-permute-done | bytes 278560 | tf_op jit(solution)/shard_map/ppermute | solution.py:531
  70.9 0.1 collective-permute-start.14
  71.0 0.6 collective-permute-done.13
  71.6 0.1 collective-permute-start.15
  71.7 4.5 %all-to-all-start.1 = ((f32[16,16,1024]{2,1,0:T(8,128)}), f32[16,16,1024]{2,1,0:T(8,128)}, u32[]{:S(2)}, u32[]{:S(2)}) async-start(f32[16,16,1024]{2,1,0:T(8,128)} %bitcast.5), calls=%async_computation.1 | async-start | bytes 2097152 | tf_op jit(solution)/shard_map/all_to_all | solution.py:621
  76.1 0.0 collective-permute-done.15.other1
  76.1 0.0 collective-permute-done.14.other0
  76.2 26.2 %shard_map.58 = (bf16[10922,1536]{1,0:T(8,128)(2,1)}, f32[65536,128]{1,0:T(8,128)}) custom-call(s32[1]{0:T(128)} %bitcast.2.core_ref, f32[1088,128]{1,0:T(8,128)S(1)} %maximum_select_fusion.mine0, f32[1024,128]{1,0:T(8,128)S(1)} %maximum_select_fusion.1.mine1, f32[1088,128]{1,0:T(8,128)S(1)} %collective-permute-done.14.other0, ...), custom_call_target="tpu_custom_call" | custom-call | flops 193273528320 | tf_op jit(solution)/shard_map/pallas_call | solution.py:625
  102.3 0.0 all-to-all-done.1
  102.3 6.4 %shard_map.59 = f32[128,1024]{1,0:T(8,128)} custom-call(s32[1,128]{1,0:T(1,128)} %get-tuple-element.19.slot_ref, f32[65536,128]{1,0:T(8,128)} %get-tuple-element.30.tail_hbm, f32[256,1024]{1,0:T(8,128)} %bitcast.6.returned_hbm, bf16[10922,1536]{1,0:T(8,128)(2,1)} %get-tuple-element.32.forms_hbm), custom_call_target="tpu_custom_call" | custom-call | tf_op jit(solution)/shard_map/pallas_call | solution.py:647
  (20 shorter events, 0.4 us)
Async XLA Ops:
  0.0 24.7 %collective-permute-start.1 = (bf16[1024,1024]{1,0:T(8,128)(2,1)}, bf16[1024,1024]{1,0:T(8,128)(2,1)S(1)}, u32[]{:S(2)}, u32[]{:S(2)}) collective-permute-start(bf16[1024,1024]{1,0:T(8,128)(2,1)} %mine_hbm.1), channel_id=1, source_target_pairs={{0,1},{1,0},{2,3},{3,2},{4,5},{5,4},{6,7},{7,6},{8,9},{9,8},{10,11... | collective-permute-start | bytes 6291464 | tf_op jit(solution)/shard_map/ppermute | solution.py:531
  24.6 1.9 %collective-permute-start = (bf16[256,1024]{1,0:T(8,128)(2,1)S(1)}, bf16[256,1024]{1,0:T(8,128)(2,1)S(1)}, u32[]{:S(2)}, u32[]{:S(2)}) collective-permute-start(bf16[256,1024]{1,0:T(8,128)(2,1)S(1)} %bitcast.7), channel_id=1, source_target_pairs={{0,1},{1,0},{2,3},{3,2},{4,5},{5,4},{6,7},{7,6},{8,9},{9,8},{10,11... | collective-permute-start | bytes 1572872 | tf_op jit(solution)/shard_map/ppermute | solution.py:531
  24.7 1.6 %copy-start = (bf16[1024,1024]{1,0:T(8,128)(2,1)S(1)}, bf16[1024,1024]{1,0:T(8,128)(2,1)}, u32[]{:S(2)}) copy-start(bf16[1024,1024]{1,0:T(8,128)(2,1)} %mine_hbm.1) | copy-start | bytes 6291460
  29.3 8.8 %collective-permute-start.7 = (f32[512,128]{1,0:T(8,128)S(1)}, f32[512,128]{1,0:T(8,128)S(1)}, u32[]{:S(2)}, u32[]{:S(2)}) collective-permute-start(f32[512,128]{1,0:T(8,128)S(1)} %constant_dynamic-slice_fusion.2), channel_id=1, source_target_pairs={{0,4},{1,5},{2,6},{3,7},{4,0},{5,1},{6,2},{7,3},{8,12},{9,13},{10,... | collective-permute-start | bytes 786440 | tf_op jit(solution)/shard_map/ppermute | solution.py:531
  31.2 8.3 %collective-permute-start.2 = (f32[544,128]{1,0:T(8,128)S(1)}, f32[544,128]{1,0:T(8,128)S(1)}, u32[]{:S(2)}, u32[]{:S(2)}) collective-permute-start(f32[544,128]{1,0:T(8,128)S(1)} %constant_dynamic-slice_fusion.5), channel_id=1, source_target_pairs={{0,2},{1,3},{2,0},{3,1},{4,6},{5,7},{6,4},{7,5},{8,10},{9,11},{10,... | collective-permute-start | bytes 835592 | tf_op jit(solution)/shard_map/ppermute | solution.py:531
  38.1 5.2 %collective-permute-start.8 = (f32[256,128]{1,0:T(8,128)S(1)}, f32[256,128]{1,0:T(8,128)S(1)}, u32[]{:S(2)}, u32[]{:S(2)}) collective-permute-start(f32[256,128]{1,0:T(8,128)S(1)} %constant_dynamic-slice_fusion.1), channel_id=1, source_target_pairs={{0,2},{1,3},{2,0},{3,1},{4,6},{5,7},{6,4},{7,5},{8,10},{9,11},{10,... | collective-permute-start | bytes 393224 | tf_op jit(solution)/shard_map/ppermute | solution.py:531
  39.6 6.1 %collective-permute-start.3 = (f32[272,128]{1,0:T(8,128)S(1)}, f32[272,128]{1,0:T(8,128)S(1)}, u32[]{:S(2)}, u32[]{:S(2)}) collective-permute-start(f32[272,128]{1,0:T(8,128)S(1)} %constant_dynamic-slice_fusion.4), channel_id=1, source_target_pairs={{0,4},{1,5},{2,6},{3,7},{4,0},{5,1},{6,2},{7,3},{8,12},{9,13},{10,... | collective-permute-start | bytes 417800 | tf_op jit(solution)/shard_map/ppermute | solution.py:531
  43.3 8.6 %collective-permute-start.9 = (f32[128,128]{1,0:T(8,128)S(1)}, f32[128,128]{1,0:T(8,128)S(1)}, u32[]{:S(2)}, u32[]{:S(2)}) collective-permute-start(f32[128,128]{1,0:T(8,128)S(1)} %constant_dynamic-slice_fusion), channel_id=1, source_target_pairs={{0,8},{1,9},{2,10},{3,11},{4,12},{5,13},{6,14},{7,15},{8,0},{9,1},... | collective-permute-start | bytes 196616 | tf_op jit(solution)/shard_map/ppermute | solution.py:531
  45.7 7.7 %collective-permute-start.4 = (f32[136,128]{1,0:T(8,128)S(1)}, f32[136,128]{1,0:T(8,128)S(1)}, u32[]{:S(2)}, u32[]{:S(2)}) collective-permute-start(f32[136,128]{1,0:T(8,128)S(1)} %constant_dynamic-slice_fusion.3), channel_id=1, source_target_pairs={{0,8},{1,9},{2,10},{3,11},{4,12},{5,13},{6,14},{7,15},{8,0},{9,1},... | collective-permute-start | bytes 208904 | tf_op jit(solution)/shard_map/ppermute | solution.py:531
  51.9 5.9 %collective-permute-start.10 = (f32[128,128]{1,0:T(8,128)S(1)}, f32[128,128]{1,0:T(8,128)S(1)}, u32[]{:S(2)}, u32[]{:S(2)}) collective-permute-start(f32[128,128]{1,0:T(8,128)S(1)} %dynamic-slice_add_fusion.5), channel_id=1, source_target_pairs={{0,8},{1,9},{2,10},{3,11},{4,12},{5,13},{6,14},{7,15},{8,0},{9,1},... | collective-permute-start | bytes 196616 | tf_op jit(solution)/shard_map/ppermute | solution.py:531
  53.4 5.3 %collective-permute-start.5 = (f32[136,128]{1,0:T(8,128)S(1)}, f32[136,128]{1,0:T(8,128)S(1)}, u32[]{:S(2)}, u32[]{:S(2)}) collective-permute-start(f32[136,128]{1,0:T(8,128)S(1)} %dynamic-slice_add_fusion.4), channel_id=1, source_target_pairs={{0,8},{1,9},{2,10},{3,11},{4,12},{5,13},{6,14},{7,15},{8,0},{9,1},... | collective-permute-start | bytes 208904 | tf_op jit(solution)/shard_map/ppermute | solution.py:531
  57.9 5.0 %collective-permute-start.11 = (f32[256,128]{1,0:T(8,128)S(1)}, f32[256,128]{1,0:T(8,128)S(1)}, u32[]{:S(2)}, u32[]{:S(2)}) collective-permute-start(f32[256,128]{1,0:T(8,128)S(1)} %maximum_select_fusion.5), channel_id=1, source_target_pairs={{0,2},{1,3},{2,0},{3,1},{4,6},{5,7},{6,4},{7,5},{8,10},{9,11},{10,... | collective-permute-start | bytes 393224 | tf_op jit(solution)/shard_map/ppermute | solution.py:531
  58.7 5.1 %collective-permute-start.6 = (f32[272,128]{1,0:T(8,128)S(1)}, f32[272,128]{1,0:T(8,128)S(1)}, u32[]{:S(2)}, u32[]{:S(2)}) collective-permute-start(f32[272,128]{1,0:T(8,128)S(1)} %maximum_select_fusion.4), channel_id=1, source_target_pairs={{0,4},{1,5},{2,6},{3,7},{4,0},{5,1},{6,2},{7,3},{8,12},{9,13},{10,... | collective-permute-start | bytes 417800 | tf_op jit(solution)/shard_map/ppermute | solution.py:531
  63.9 7.0 %collective-permute-start.12 = (f32[544,128]{1,0:T(8,128)S(1)}, f32[544,128]{1,0:T(8,128)S(1)}, u32[]{:S(2)}, u32[]{:S(2)}) collective-permute-start(f32[544,128]{1,0:T(8,128)S(1)} %maximum_select_fusion.2), channel_id=1, source_target_pairs={{0,2},{1,3},{2,0},{3,1},{4,6},{5,7},{6,4},{7,5},{8,10},{9,11},{10,... | collective-permute-start | bytes 835592 | tf_op jit(solution)/shard_map/ppermute | solution.py:531
  65.2 6.4 %collective-permute-start.13 = (f32[512,128]{1,0:T(8,128)S(1)}, f32[512,128]{1,0:T(8,128)S(1)}, u32[]{:S(2)}, u32[]{:S(2)}) collective-permute-start(f32[512,128]{1,0:T(8,128)S(1)} %maximum_select_fusion.3), channel_id=1, source_target_pairs={{0,4},{1,5},{2,6},{3,7},{4,0},{5,1},{6,2},{7,3},{8,12},{9,13},{10,... | collective-permute-start | bytes 786440 | tf_op jit(solution)/shard_map/ppermute | solution.py:531
  70.9 5.2 %collective-permute-start.14 = (f32[1088,128]{1,0:T(8,128)S(1)}, f32[1088,128]{1,0:T(8,128)S(1)}, u32[]{:S(2)}, u32[]{:S(2)}) collective-permute-start(f32[1088,128]{1,0:T(8,128)S(1)} %maximum_select_fusion.mine0), channel_id=1, source_target_pairs={{0,1},{1,0},{2,3},{3,2},{4,5},{5,4},{6,7},{7,6},{8,9},{9,8},{10,11... | collective-permute-start | bytes 1671176 | tf_op jit(solution)/shard_map/ppermute | solution.py:531
  71.6 4.6 %collective-permute-start.15 = (f32[1024,128]{1,0:T(8,128)S(1)}, f32[1024,128]{1,0:T(8,128)S(1)}, u32[]{:S(2)}, u32[]{:S(2)}) collective-permute-start(f32[1024,128]{1,0:T(8,128)S(1)} %maximum_select_fusion.1.mine1), channel_id=1, source_target_pairs={{0,1},{1,0},{2,3},{3,2},{4,5},{5,4},{6,7},{7,6},{8,9},{9,8},{10,11... | collective-permute-start | bytes 1572872 | tf_op jit(solution)/shard_map/ppermute | solution.py:531
  71.7 30.7 %all-to-all-start.1 = ((f32[16,16,1024]{2,1,0:T(8,128)}), f32[16,16,1024]{2,1,0:T(8,128)}, u32[]{:S(2)}, u32[]{:S(2)}) async-start(f32[16,16,1024]{2,1,0:T(8,128)} %bitcast.5), calls=%async_computation.1 | async-start | bytes 2097152 | tf_op jit(solution)/shard_map/all_to_all | solution.py:621
